TPU v7x, 32 devices: a whole 2x2x4 slice. The times are simulated.
32 devices in a mesh: groups: 2 (over y), slab: 16 (over z, x, core).
Axes of the slice: x: 2, y: 2, z: 4, core: 2. Of those that a mesh axis runs over, the one named last changes fastest.
Arguments:
- estimate: float32 [128, 2048, 128], P('slab', 'groups'), parts along dimension 1, may hold values from 0.2 to 5
- recorded: float32 [4, 128, 2048, 128], P(None, 'slab', 'groups'), parts along dimension 2, may hold values from 0.2 to 5
- lateral: float32 [4, 2, 31], replicated, may hold values from 0.05 to 1
- axial_taps: float32 [4, 101], replicated, may hold values from 0.05 to 1
Outputs:
- restored: float32 [128, 2048, 128], P('slab', 'groups'), parts along dimension 1
There are 2 independent parts, one for each index of `groups`. A program takes and returns all parts, laid end to end along the dimension named above; an argument that names none is the same for every part. Nothing has to cross between parts.
All inputs are finite; a program needn't handle non-finite values.
Results may differ from a plain program's by a relative error of at most 0.0001.
Values sent between devices are 32-bit elements; how exact they have to be, the bound alone decides.
No kernel may reach another device: no remote copies, remote signals or barrier semaphores. Data moves between devices by JAX's collectives and lax.ppermute only.
A program may use at most 192 MiB of HBM per device.

v0:
```python
import jax
import jax.numpy as jnp
from jax import lax
from jax.sharding import PartitionSpec as P


def correlate(volume, kernel, along):
    length = kernel.shape[0]
    margin = length // 2
    extent = volume.shape[along]
    widths = [(0, 0)] * volume.ndim
    widths[along] = (margin, margin)
    padded = jnp.pad(volume, widths)
    total = kernel[0] * lax.slice_in_dim(padded, 0, extent, axis=along)
    for position in range(1, length):
        total = total + kernel[position] * lax.slice_in_dim(
            padded, position, position + extent, axis=along
        )
    return total


def banded(kernel, extent):
    length = kernel.shape[0]
    margin = length // 2
    places = jnp.arange(extent, dtype=jnp.int32)
    offsets = places[None, :] - places[:, None] + margin
    stencil = jnp.arange(length, dtype=jnp.int32)
    picked = (offsets[None, :, :] == stencil[:, None, None]).astype(jnp.float32)
    return jnp.sum(kernel[:, None, None] * picked, axis=0)


def normalized(kernel):
    return kernel / jnp.sum(kernel)


def backward(pencil_blur, pencil_data, matrix):
    along_depth = jnp.tensordot(matrix.T, pencil_blur, axes=(1, 0), precision=lax.Precision.HIGHEST)
    quotient = pencil_data / along_depth
    spread = jnp.tensordot(matrix, quotient, axes=(1, 0), precision=lax.Precision.HIGHEST)
    return lax.all_to_all(spread, "slab", split_axis=0, concat_axis=1, tiled=True)


def body(estimate, recorded, lateral, axial_taps):
    depth_count = estimate.shape[0] * lax.axis_size("slab")
    current = estimate
    for which_view in range(recorded.shape[0]):
        row_taps = normalized(lateral[which_view, 0])
        column_taps = normalized(lateral[which_view, 1])
        depth_taps = normalized(axial_taps[which_view])
        matrix = banded(depth_taps, depth_count)
        blurred = correlate(correlate(current, row_taps[::-1], 1), column_taps[::-1], 2)
        returned = backward(
            lax.all_to_all(blurred, "slab", split_axis=1, concat_axis=0, tiled=True),
            lax.all_to_all(recorded[which_view], "slab", split_axis=1, concat_axis=0, tiled=True),
            matrix,
        )
        returned = correlate(correlate(returned, column_taps, 2), row_taps, 1)
        current = current * returned
    return current


def solution(mesh):
    in_specs = (P("slab", "groups", None), P(None, "slab", "groups", None), P(), P())
    out_specs = P("slab", "groups", None)
    return jax.shard_map(body, mesh=mesh, in_specs=in_specs, out_specs=out_specs, check_vma=False)
```

profile of v0, /device:TPU:1, one launch (start us, length us, event | category | flops | bytes accessed | tf_op | source)
XLA Modules:
  0.0 1995.9 jit_solution(12030532060642041085)
XLA Ops:
  6.6 4.6 copy.87
  11.2 40.7 %multiply_add_fusion.3 = f32[8,1024,128]{2,0,1:T(8,128)S(1)} fusion(f32[8,1024,128]{2,0,1:T(8,128)S(1)} %copy.87, f32[]{:T(128)} %bitcast.42, f32[]{:T(128)} %bitcast.41, f32[]{:T(128)} %bitcast.40, f32[]{:T(128)} %bitcast.39, f32[]{:T(128)} %bitcast.38, f32[]{:T(128)} %bitcast.37, f32[]{:T(128)} %bitcast.36, f32[]{:T(128)} %bitcast.35, f32[]{:T(128)} %bitcast.34, ...), kind=kLoop, calls=%fused_computation.980 | loop fusion | flops 63963136 | bytes 8388732 | tf_op jit(solution)/shard_map/add | solution.py:16
  51.9 53.4 %fusion.52 = f32[8,1024,128]{2,0,1:T(8,128)} fusion(f32[8,1024,128]{2,0,1:T(8,128)S(1)} %multiply_add_fusion.3, f32[]{:T(128)} %bitcast.72, f32[]{:T(128)} %bitcast.71, f32[]{:T(128)} %bitcast.70, f32[]{:T(128)} %bitcast.69, f32[]{:T(128)} %bitcast.68, f32[]{:T(128)} %bitcast.67, f32[]{:T(128)} %bitcast.66, f32[]{:T(128)} %bitcast.65, f32[]{:T(128)} %bitcast.64, ...), kind=kLoop, calls=%fused_computation.297 | loop fusion | flops 63963136 | bytes 8388732 | tf_op jit(solution)/shard_map/add | solution.py:16
  105.3 7.6 all-to-all-start.1
  112.9 10.8 fusion.672
  123.7 4.5 copy.161
  128.2 62.6 %all-to-all-done.1 = f32[8,1024,128]{2,0,1:T(8,128)} async-done(((f32[8,1024,128]{2,0,1:T(8,128)}), f32[8,1024,128]{2,0,1:T(8,128)}, u32[]{:S(2)}, u32[]{:S(2)}) %all-to-all-start.1) | async-done | bytes 4194336 | tf_op jit(solution)/shard_map/all_to_all | solution.py:53
  190.8 19.4 all-to-all-start
  213.3 3.7 select_reduce_fusion
  219.9 9.0 fusion.493
  228.9 59.4 %all-to-all-done = f32[8,1024,128]{2,0,1:T(8,128)} async-done(((f32[8,1024,128]{2,0,1:T(8,128)}), f32[8,1024,128]{2,0,1:T(8,128)}, u32[]{:S(2)}, u32[]{:S(2)}) %all-to-all-start) | async-done | bytes 4194336 | tf_op jit(solution)/shard_map/all_to_all | solution.py:54
  288.3 6.1 fusion.483
  294.4 4.4 copy.85
  298.9 19.8 all-to-all-start.2
  319.0 4.9 broadcast_divide_fusion.3
  330.8 65.8 %all-to-all-done.2 = f32[128,64,128]{2,1,0:T(8,128)} async-done(((f32[128,64,128]{2,1,0:T(8,128)}), f32[128,64,128]{2,1,0:T(8,128)}, u32[]{:S(2)}, u32[]{:S(2)}) %all-to-all-start.2) | async-done | bytes 4194336 | tf_op jit(solution)/shard_map/all_to_all | solution.py:40
  396.6 5.5 copy.86
  402.1 53.0 %fusion.112 = f32[8,1024,128]{2,0,1:T(8,128)S(1)} fusion(f32[8,1024,128]{2,0,1:T(8,128)S(1)} %bitcast.629, f32[]{:T(128)} %bitcast.109, f32[]{:T(128)} %bitcast.108, f32[]{:T(128)} %bitcast.107, f32[]{:T(128)} %bitcast.106, f32[]{:T(128)} %bitcast.105, f32[]{:T(128)} %bitcast.104, f32[]{:T(128)} %bitcast.103, f32[]{:T(128)} %bitcast.102, f32[]{:T(128)} %bitcast.101, ...), kind=kLoop, calls=%fused_computation.357 | loop fusion | flops 63963136 | bytes 8388732 | tf_op jit(solution)/shard_map/add | solution.py:16
  455.1 45.1 %add_multiply_fusion.3 = f32[8,1024,128]{2,0,1:T(8,128)S(1)} fusion(f32[8,1024,128]{2,0,1:T(8,128)S(1)} %fusion.112, f32[]{:T(128)} %bitcast.139, f32[]{:T(128)} %bitcast.138, f32[]{:T(128)} %bitcast.137, f32[]{:T(128)} %bitcast.136, f32[]{:T(128)} %bitcast.135, f32[]{:T(128)} %bitcast.134, f32[]{:T(128)} %bitcast.133, f32[]{:T(128)} %bitcast.132, ...), kind=kLoop, calls=%fused_computation.947 | loop fusion | flops 65011712 | bytes 12583036 | tf_op jit(solution)/shard_map/mul | solution.py:58
  500.2 41.1 %multiply_add_fusion.2 = f32[8,1024,128]{2,0,1:T(8,128)S(1)} fusion(f32[8,1024,128]{2,0,1:T(8,128)S(1)} %add_multiply_fusion.3, f32[]{:T(128)} %bitcast.182, f32[]{:T(128)} %bitcast.181, f32[]{:T(128)} %bitcast.180, f32[]{:T(128)} %bitcast.179, f32[]{:T(128)} %bitcast.178, f32[]{:T(128)} %bitcast.177, f32[]{:T(128)} %bitcast.176, f32[]{:T(128)} %bitcast.175, ...), kind=kLoop, calls=%fused_computation.914 | loop fusion | flops 63963136 | bytes 8388732 | tf_op jit(solution)/shard_map/add | solution.py:16
  541.3 53.5 %fusion.172 = f32[8,1024,128]{2,0,1:T(8,128)} fusion(f32[8,1024,128]{2,0,1:T(8,128)S(1)} %multiply_add_fusion.2, f32[]{:T(128)} %bitcast.212, f32[]{:T(128)} %bitcast.211, f32[]{:T(128)} %bitcast.210, f32[]{:T(128)} %bitcast.209, f32[]{:T(128)} %bitcast.208, f32[]{:T(128)} %bitcast.207, f32[]{:T(128)} %bitcast.206, f32[]{:T(128)} %bitcast.205, ...), kind=kLoop, calls=%fused_computation.417 | loop fusion | flops 63963136 | bytes 8388732 | tf_op jit(solution)/shard_map/add | solution.py:16
  594.8 19.3 all-to-all-start.4
  614.1 6.6 copy.160
  620.7 71.5 %all-to-all-done.4 = f32[8,1024,128]{2,0,1:T(8,128)} async-done(((f32[8,1024,128]{2,0,1:T(8,128)}), f32[8,1024,128]{2,0,1:T(8,128)}, u32[]{:S(2)}, u32[]{:S(2)}) %all-to-all-start.4) | async-done | bytes 4194336 | tf_op jit(solution)/shard_map/all_to_all | solution.py:53
  692.2 19.6 all-to-all-start.3
  714.7 9.0 fusion.490
  723.7 66.0 %all-to-all-done.3 = f32[8,1024,128]{2,0,1:T(8,128)} async-done(((f32[8,1024,128]{2,0,1:T(8,128)}), f32[8,1024,128]{2,0,1:T(8,128)}, u32[]{:S(2)}, u32[]{:S(2)}) %all-to-all-start.3) | async-done | bytes 4194336 | tf_op jit(solution)/shard_map/all_to_all | solution.py:54
  789.7 6.1 fusion.482
  795.8 4.4 copy.94
  800.2 19.6 all-to-all-start.5
  825.5 72.2 %all-to-all-done.5 = f32[128,64,128]{2,1,0:T(8,128)} async-done(((f32[128,64,128]{2,1,0:T(8,128)}), f32[128,64,128]{2,1,0:T(8,128)}, u32[]{:S(2)}, u32[]{:S(2)}) %all-to-all-start.5) | async-done | bytes 4194336 | tf_op jit(solution)/shard_map/all_to_all | solution.py:40
  897.7 5.5 copy.95
  903.2 53.1 %fusion.232 = f32[8,1024,128]{2,0,1:T(8,128)S(1)} fusion(f32[8,1024,128]{2,0,1:T(8,128)S(1)} %bitcast.630, f32[]{:T(128)} %bitcast.250, f32[]{:T(128)} %bitcast.249, f32[]{:T(128)} %bitcast.248, f32[]{:T(128)} %bitcast.247, f32[]{:T(128)} %bitcast.246, f32[]{:T(128)} %bitcast.245, f32[]{:T(128)} %bitcast.244, f32[]{:T(128)} %bitcast.243, f32[]{:T(128)} %bitcast.242, ...), kind=kLoop, calls=%fused_computation.477 | loop fusion | flops 63963136 | bytes 8388732 | tf_op jit(solution)/shard_map/add | solution.py:16
  956.3 41.4 %add_multiply_fusion.2 = f32[8,1024,128]{2,0,1:T(8,128)S(1)} fusion(f32[8,1024,128]{2,0,1:T(8,128)S(1)} %copy-done.3, f32[8,1024,128]{2,0,1:T(8,128)S(1)} %fusion.232, f32[]{:T(128)} %bitcast.280, f32[]{:T(128)} %bitcast.279, f32[]{:T(128)} %bitcast.278, f32[]{:T(128)} %bitcast.277, f32[]{:T(128)} %bitcast.276, f32[]{:T(128)} %bitcast.275, f32[]{:T(128)} %bitcast.274, ...), kind=kLoop, calls=%fused_computation.881 | loop fusion | flops 65011712 | bytes 12583036 | tf_op jit(solution)/shard_map/mul | solution.py:58
  997.8 40.7 %multiply_add_fusion.1 = f32[8,1024,128]{2,0,1:T(8,128)S(1)} fusion(f32[8,1024,128]{2,0,1:T(8,128)S(1)} %add_multiply_fusion.2, f32[]{:T(128)} %bitcast.323, f32[]{:T(128)} %bitcast.322, f32[]{:T(128)} %bitcast.321, f32[]{:T(128)} %bitcast.320, f32[]{:T(128)} %bitcast.319, f32[]{:T(128)} %bitcast.318, f32[]{:T(128)} %bitcast.317, f32[]{:T(128)} %bitcast.316, ...), kind=kLoop, calls=%fused_computation.848 | loop fusion | flops 63963136 | bytes 8388732 | tf_op jit(solution)/shard_map/add | solution.py:16
  1038.5 53.8 %fusion.292 = f32[8,1024,128]{2,0,1:T(8,128)} fusion(f32[8,1024,128]{2,0,1:T(8,128)S(1)} %multiply_add_fusion.1, f32[]{:T(128)} %bitcast.353, f32[]{:T(128)} %bitcast.352, f32[]{:T(128)} %bitcast.351, f32[]{:T(128)} %bitcast.350, f32[]{:T(128)} %bitcast.349, f32[]{:T(128)} %bitcast.348, f32[]{:T(128)} %bitcast.347, f32[]{:T(128)} %bitcast.346, ...), kind=kLoop, calls=%fused_computation.537 | loop fusion | flops 63963136 | bytes 8388732 | tf_op jit(solution)/shard_map/add | solution.py:16
  1092.3 19.3 all-to-all-start.7
  1111.6 6.6 copy.159
  1118.2 71.5 %all-to-all-done.7 = f32[8,1024,128]{2,0,1:T(8,128)} async-done(((f32[8,1024,128]{2,0,1:T(8,128)}), f32[8,1024,128]{2,0,1:T(8,128)}, u32[]{:S(2)}, u32[]{:S(2)}) %all-to-all-start.7) | async-done | bytes 4194336 | tf_op jit(solution)/shard_map/all_to_all | solution.py:53
  1189.7 19.6 all-to-all-start.6
  1212.2 9.0 fusion.487
  1221.2 66.0 %all-to-all-done.6 = f32[8,1024,128]{2,0,1:T(8,128)} async-done(((f32[8,1024,128]{2,0,1:T(8,128)}), f32[8,1024,128]{2,0,1:T(8,128)}, u32[]{:S(2)}, u32[]{:S(2)}) %all-to-all-start.6) | async-done | bytes 4194336 | tf_op jit(solution)/shard_map/all_to_all | solution.py:54
  1287.2 6.1 fusion.481
  1293.3 4.4 copy.102
  1297.7 19.6 all-to-all-start.8
  1324.5 70.7 %all-to-all-done.8 = f32[128,64,128]{2,1,0:T(8,128)} async-done(((f32[128,64,128]{2,1,0:T(8,128)}), f32[128,64,128]{2,1,0:T(8,128)}, u32[]{:S(2)}, u32[]{:S(2)}) %all-to-all-start.8) | async-done | bytes 4194336 | tf_op jit(solution)/shard_map/all_to_all | solution.py:40
  1395.3 5.5 copy.103
  1400.8 53.2 %fusion.352 = f32[8,1024,128]{2,0,1:T(8,128)S(1)} fusion(f32[8,1024,128]{2,0,1:T(8,128)S(1)} %bitcast.631, f32[]{:T(128)} %bitcast.391, f32[]{:T(128)} %bitcast.390, f32[]{:T(128)} %bitcast.389, f32[]{:T(128)} %bitcast.388, f32[]{:T(128)} %bitcast.387, f32[]{:T(128)} %bitcast.386, f32[]{:T(128)} %bitcast.385, f32[]{:T(128)} %bitcast.384, f32[]{:T(128)} %bitcast.383, ...), kind=kLoop, calls=%fused_computation.597 | loop fusion | flops 63963136 | bytes 8388732 | tf_op jit(solution)/shard_map/add | solution.py:16
  1453.9 41.5 %add_multiply_fusion.1 = f32[8,1024,128]{2,0,1:T(8,128)S(1)} fusion(f32[8,1024,128]{2,0,1:T(8,128)S(1)} %copy-done.1, f32[8,1024,128]{2,0,1:T(8,128)S(1)} %fusion.352, f32[]{:T(128)} %bitcast.421, f32[]{:T(128)} %bitcast.420, f32[]{:T(128)} %bitcast.419, f32[]{:T(128)} %bitcast.418, f32[]{:T(128)} %bitcast.417, f32[]{:T(128)} %bitcast.416, f32[]{:T(128)} %bitcast.415, ...), kind=kLoop, calls=%fused_computation.815 | loop fusion | flops 65011712 | bytes 12583036 | tf_op jit(solution)/shard_map/mul | solution.py:58
  1495.5 40.8 %multiply_add_fusion = f32[8,1024,128]{2,0,1:T(8,128)S(1)} fusion(f32[8,1024,128]{2,0,1:T(8,128)S(1)} %add_multiply_fusion.1, f32[]{:T(128)} %bitcast.464, f32[]{:T(128)} %bitcast.463, f32[]{:T(128)} %bitcast.462, f32[]{:T(128)} %bitcast.461, f32[]{:T(128)} %bitcast.460, f32[]{:T(128)} %bitcast.459, f32[]{:T(128)} %bitcast.458, f32[]{:T(128)} %bitcast.457, ...), kind=kLoop, calls=%fused_computation.782 | loop fusion | flops 63963136 | bytes 8388732 | tf_op jit(solution)/shard_map/add | solution.py:16
  1536.3 53.7 %fusion.412 = f32[8,1024,128]{2,0,1:T(8,128)} fusion(f32[8,1024,128]{2,0,1:T(8,128)S(1)} %multiply_add_fusion, f32[]{:T(128)} %bitcast.494, f32[]{:T(128)} %bitcast.493, f32[]{:T(128)} %bitcast.492, f32[]{:T(128)} %bitcast.491, f32[]{:T(128)} %bitcast.490, f32[]{:T(128)} %bitcast.489, f32[]{:T(128)} %bitcast.488, f32[]{:T(128)} %bitcast.487, f32[]{:T(128)} %bitcast.486, ...), kind=kLoop, calls=%fused_computation.657 | loop fusion | flops 63963136 | bytes 8388732 | tf_op jit(solution)/shard_map/add | solution.py:16
  1590.0 19.3 all-to-all-start.10
  1609.3 6.6 copy.158
  1615.9 71.5 %all-to-all-done.10 = f32[8,1024,128]{2,0,1:T(8,128)} async-done(((f32[8,1024,128]{2,0,1:T(8,128)}), f32[8,1024,128]{2,0,1:T(8,128)}, u32[]{:S(2)}, u32[]{:S(2)}) %all-to-all-start.10) | async-done | bytes 4194336 | tf_op jit(solution)/shard_map/all_to_all | solution.py:53
  1687.4 19.6 all-to-all-start.9
  1709.9 9.1 fusion.484
  1719.0 65.9 %all-to-all-done.9 = f32[8,1024,128]{2,0,1:T(8,128)} async-done(((f32[8,1024,128]{2,0,1:T(8,128)}), f32[8,1024,128]{2,0,1:T(8,128)}, u32[]{:S(2)}, u32[]{:S(2)}) %all-to-all-start.9) | async-done | bytes 4194336 | tf_op jit(solution)/shard_map/all_to_all | solution.py:54
  1784.9 6.1 fusion.480
  1791.0 4.5 copy.110
  1795.4 19.6 all-to-all-start.11
  1818.0 75.0 %all-to-all-done.11 = f32[128,64,128]{2,1,0:T(8,128)} async-done(((f32[128,64,128]{2,1,0:T(8,128)}), f32[128,64,128]{2,1,0:T(8,128)}, u32[]{:S(2)}, u32[]{:S(2)}) %all-to-all-start.11) | async-done | bytes 4194336 | tf_op jit(solution)/shard_map/all_to_all | solution.py:40
  1893.0 5.5 copy.111
  1898.5 52.9 %fusion.472 = f32[8,1024,128]{2,0,1:T(8,128)S(1)} fusion(f32[8,1024,128]{2,0,1:T(8,128)S(1)} %bitcast.632, f32[]{:T(128)} %bitcast.532, f32[]{:T(128)} %bitcast.531, f32[]{:T(128)} %bitcast.530, f32[]{:T(128)} %bitcast.529, f32[]{:T(128)} %bitcast.528, f32[]{:T(128)} %bitcast.527, f32[]{:T(128)} %bitcast.526, f32[]{:T(128)} %bitcast.525, f32[]{:T(128)} %bitcast.524, ...), kind=kLoop, calls=%fused_computation.717 | loop fusion | flops 63963136 | bytes 8388732 | tf_op jit(solution)/shard_map/add | solution.py:16
  1951.4 41.4 %add_multiply_fusion = f32[8,1024,128]{2,0,1:T(8,128)S(1)} fusion(f32[8,1024,128]{2,0,1:T(8,128)S(1)} %copy-done.5, f32[8,1024,128]{2,0,1:T(8,128)S(1)} %fusion.472, f32[]{:T(128)} %bitcast.562, f32[]{:T(128)} %bitcast.561, f32[]{:T(128)} %bitcast.560, f32[]{:T(128)} %bitcast.559, f32[]{:T(128)} %bitcast.558, f32[]{:T(128)} %bitcast.557, f32[]{:T(128)} %bitcast.556, ...), kind=kLoop, calls=%fused_computation.749 | loop fusion | flops 65011712 | bytes 12583036 | tf_op jit(solution)/shard_map/mul | solution.py:58
  (71 shorter events, 47.0 us)
Async XLA Ops:
  105.3 85.6 %all-to-all-start.1 = ((f32[8,1024,128]{2,0,1:T(8,128)}), f32[8,1024,128]{2,0,1:T(8,128)}, u32[]{:S(2)}, u32[]{:S(2)}) async-start(f32[8,1024,128]{2,0,1:T(8,128)} %fusion.52), calls=%async_computation.1 | async-start | bytes 8388608 | tf_op jit(solution)/shard_map/all_to_all | solution.py:53
  190.8 19.4 copy-start.8
  190.8 97.5 %all-to-all-start = ((f32[8,1024,128]{2,0,1:T(8,128)}), f32[8,1024,128]{2,0,1:T(8,128)}, u32[]{:S(2)}, u32[]{:S(2)}) async-start(f32[8,1024,128]{2,0,1:T(8,128)} %bitcast.628), calls=%async_computation | async-start | bytes 8388608 | tf_op jit(solution)/shard_map/all_to_all | solution.py:54
  298.9 20.1 %copy-start.7 = (f32[4,2,31]{2,1,0:T(2,128)S(1)}, f32[4,2,31]{2,1,0:T(2,128)}, u32[]{:S(2)}) copy-start(f32[4,2,31]{2,1,0:T(2,128)} %param.6) | copy-start | bytes 2980
  298.9 97.7 %all-to-all-start.2 = ((f32[128,64,128]{2,1,0:T(8,128)}), f32[128,64,128]{2,1,0:T(8,128)}, u32[]{:S(2)}, u32[]{:S(2)}) async-start(f32[128,64,128]{2,1,0:T(8,128)} %copy.85), calls=%async_computation.2 | async-start | bytes 8388608 | tf_op jit(solution)/shard_map/all_to_all | solution.py:40
  402.1 53.0 %copy-start.6 = (f32[8,1024,128]{2,1,0:T(8,128)S(1)}, f32[8,1024,128]{2,1,0:T(8,128)}, u32[]{:S(2)}) copy-start(f32[8,1024,128]{2,1,0:T(8,128)} %param.4) | copy-start | bytes 12582916
  500.2 41.1 %copy-start.2 = (f32[8,1024,128]{2,0,1:T(8,128)}, f32[8,1024,128]{2,0,1:T(8,128)S(1)}, u32[]{:S(2)}) copy-start(f32[8,1024,128]{2,0,1:T(8,128)S(1)} %add_multiply_fusion.3) | copy-start | bytes 12582916
  594.8 97.4 %all-to-all-start.4 = ((f32[8,1024,128]{2,0,1:T(8,128)}), f32[8,1024,128]{2,0,1:T(8,128)}, u32[]{:S(2)}, u32[]{:S(2)}) async-start(f32[8,1024,128]{2,0,1:T(8,128)} %fusion.172), calls=%async_computation.4 | async-start | bytes 8388608 | tf_op jit(solution)/shard_map/all_to_all | solution.py:53
  692.2 97.5 %all-to-all-start.3 = ((f32[8,1024,128]{2,0,1:T(8,128)}), f32[8,1024,128]{2,0,1:T(8,128)}, u32[]{:S(2)}, u32[]{:S(2)}) async-start(f32[8,1024,128]{2,0,1:T(8,128)} %bitcast.634), calls=%async_computation.3 | async-start | bytes 8388608 | tf_op jit(solution)/shard_map/all_to_all | solution.py:54
  800.2 97.6 %all-to-all-start.5 = ((f32[128,64,128]{2,1,0:T(8,128)}), f32[128,64,128]{2,1,0:T(8,128)}, u32[]{:S(2)}, u32[]{:S(2)}) async-start(f32[128,64,128]{2,1,0:T(8,128)} %copy.94), calls=%async_computation.5 | async-start | bytes 8388608 | tf_op jit(solution)/shard_map/all_to_all | solution.py:40
  903.2 53.1 %copy-start.3 = (f32[8,1024,128]{2,0,1:T(8,128)S(1)}, f32[8,1024,128]{2,0,1:T(8,128)}, u32[]{:S(2)}) copy-start(f32[8,1024,128]{2,0,1:T(8,128)} %copy-done.2) | copy-start | bytes 12582916
  997.8 40.7 %copy-start = (f32[8,1024,128]{2,0,1:T(8,128)}, f32[8,1024,128]{2,0,1:T(8,128)S(1)}, u32[]{:S(2)}) copy-start(f32[8,1024,128]{2,0,1:T(8,128)S(1)} %add_multiply_fusion.2) | copy-start | bytes 12582916
  1092.3 97.4 %all-to-all-start.7 = ((f32[8,1024,128]{2,0,1:T(8,128)}), f32[8,1024,128]{2,0,1:T(8,128)}, u32[]{:S(2)}, u32[]{:S(2)}) async-start(f32[8,1024,128]{2,0,1:T(8,128)} %fusion.292), calls=%async_computation.7 | async-start | bytes 8388608 | tf_op jit(solution)/shard_map/all_to_all | solution.py:53
  1189.7 97.5 %all-to-all-start.6 = ((f32[8,1024,128]{2,0,1:T(8,128)}), f32[8,1024,128]{2,0,1:T(8,128)}, u32[]{:S(2)}, u32[]{:S(2)}) async-start(f32[8,1024,128]{2,0,1:T(8,128)} %bitcast.635), calls=%async_computation.6 | async-start | bytes 8388608 | tf_op jit(solution)/shard_map/all_to_all | solution.py:54
  1297.7 97.6 %all-to-all-start.8 = ((f32[128,64,128]{2,1,0:T(8,128)}), f32[128,64,128]{2,1,0:T(8,128)}, u32[]{:S(2)}, u32[]{:S(2)}) async-start(f32[128,64,128]{2,1,0:T(8,128)} %copy.102), calls=%async_computation.8 | async-start | bytes 8388608 | tf_op jit(solution)/shard_map/all_to_all | solution.py:40
  1400.8 53.2 %copy-start.1 = (f32[8,1024,128]{2,0,1:T(8,128)S(1)}, f32[8,1024,128]{2,0,1:T(8,128)}, u32[]{:S(2)}) copy-start(f32[8,1024,128]{2,0,1:T(8,128)} %copy-done) | copy-start | bytes 12582916
  1495.5 40.8 %copy-start.4 = (f32[8,1024,128]{2,0,1:T(8,128)}, f32[8,1024,128]{2,0,1:T(8,128)S(1)}, u32[]{:S(2)}) copy-start(f32[8,1024,128]{2,0,1:T(8,128)S(1)} %add_multiply_fusion.1) | copy-start | bytes 12582916
  1590.0 97.4 %all-to-all-start.10 = ((f32[8,1024,128]{2,0,1:T(8,128)}), f32[8,1024,128]{2,0,1:T(8,128)}, u32[]{:S(2)}, u32[]{:S(2)}) async-start(f32[8,1024,128]{2,0,1:T(8,128)} %fusion.412), calls=%async_computation.10 | async-start | bytes 8388608 | tf_op jit(solution)/shard_map/all_to_all | solution.py:53
  1687.4 97.5 %all-to-all-start.9 = ((f32[8,1024,128]{2,0,1:T(8,128)}), f32[8,1024,128]{2,0,1:T(8,128)}, u32[]{:S(2)}, u32[]{:S(2)}) async-start(f32[8,1024,128]{2,0,1:T(8,128)} %bitcast.633), calls=%async_computation.9 | async-start | bytes 8388608 | tf_op jit(solution)/shard_map/all_to_all | solution.py:54
  1795.4 97.6 %all-to-all-start.11 = ((f32[128,64,128]{2,1,0:T(8,128)}), f32[128,64,128]{2,1,0:T(8,128)}, u32[]{:S(2)}, u32[]{:S(2)}) async-start(f32[128,64,128]{2,1,0:T(8,128)} %copy.110), calls=%async_computation.11 | async-start | bytes 8388608 | tf_op jit(solution)/shard_map/all_to_all | solution.py:40
  1898.5 52.9 %copy-start.5 = (f32[8,1024,128]{2,0,1:T(8,128)S(1)}, f32[8,1024,128]{2,0,1:T(8,128)}, u32[]{:S(2)}) copy-start(f32[8,1024,128]{2,0,1:T(8,128)} %copy-done.4) | copy-start | bytes 12582916
where the time goes:
time: 2020 us; the launch traced here: 2000 us
  waiting for transfers between devices  818 us (40%)
  other arithmetic  777 us (38%)
  starting transfers between devices  222 us (11%)
  local copies, waits for them, and re-layouts  117 us (6%)
  matrix products  60.3 us (3%)
    add x12, other arithmetic, correlate(): total + kernel[position] * lax.slice_in_dim(padded, position, position +...  590 us
    all_to_all x4, waiting for transfers between devices, backward(): lax.all_to_all(spread, 'slab', split_axis=0, concat_axis=1, tiled=True)  284 us
    all_to_all x4, waiting for transfers between devices, body(): lax.all_to_all(blurred, 'slab', split_axis=1, concat_axis=0, tiled=True)  277 us
    all_to_all x4, waiting for transfers between devices, body(): lax.all_to_all(recorded[which_view], 'slab', split_axis=1, concat_axis=0,...  257 us
    mul x4, other arithmetic, body(): current = current * returned  170 us
    all_to_all x4, starting transfers between devices, backward(): lax.all_to_all(spread, 'slab', split_axis=0, concat_axis=1, tiled=True)  78.7 us
    all_to_all x4, starting transfers between devices, body(): lax.all_to_all(recorded[which_view], 'slab', split_axis=1, concat_axis=0,...  78.2 us
    all_to_all x4, starting transfers between devices, body(): lax.all_to_all(blurred, 'slab', split_axis=1, concat_axis=0, tiled=True)  65.5 us
  transfers between devices with their start and end apart: 12, of which 12 were waited for; matrix products, arithmetic and copies ran while one was open for 6% of the time, Pallas kernels for 0%

commit v1 on v0

v1 whole, which is shorter than its diff:
```python
import functools

import jax
import jax.numpy as jnp
from jax import lax
from jax.experimental import pallas as pl
from jax.experimental.pallas import tpu as pltpu
from jax.sharding import PartitionSpec as P

VMEM_LIMIT = 56 * 1024 * 1024
WHOLE = pl.BlockSpec(memory_space=pltpu.VMEM)
SCALARS = pl.BlockSpec(memory_space=pltpu.SMEM)


def banded(kernel, extent):
    length = kernel.shape[0]
    margin = length // 2
    places = jnp.arange(extent, dtype=jnp.int32)
    offsets = places[None, :] - places[:, None] + margin
    stencil = jnp.arange(length, dtype=jnp.int32)
    picked = (offsets[None, :, :] == stencil[:, None, None]).astype(jnp.float32)
    return jnp.sum(kernel[:, None, None] * picked, axis=0)


def normalized(kernel):
    return kernel / jnp.sum(kernel)


def halves(value):
    high = value.astype(jnp.bfloat16)
    low = (value - high.astype(jnp.float32)).astype(jnp.bfloat16)
    return high, low


def position(device, run):
    row, place = device // run, device % run
    return row * run + jnp.where(row % 2 == 0, place, run - 1 - place)


def device_order(count, run):
    return [r * run + (p if r % 2 == 0 else run - 1 - p) for r in range(count // run) for p in range(run)]


def along_yz(load, store, matrix_y, matrix_z, rows):
    depth, width = matrix_z.shape[0], matrix_y.shape[0]
    right_high, right_low = halves(matrix_y)
    right = jnp.concatenate([right_high, right_low], axis=1)
    right = jnp.concatenate([right, right], axis=0)
    left_high, left_low = halves(matrix_z)
    left = jnp.concatenate([left_high, left_low], axis=0)
    left = jnp.concatenate([left, left], axis=1)

    def pair(index, _):
        row = 2 * index
        planes = jnp.concatenate([load(row), load(row + 1)], axis=0)
        product = jnp.dot(
            jnp.concatenate(halves(planes), axis=1), right, preferred_element_type=jnp.float32
        )
        mixed = product[:, :width] + product[:, width:]
        sides = jnp.concatenate([mixed[:depth], mixed[depth:]], axis=1)
        product = jnp.dot(
            left, jnp.concatenate(halves(sides), axis=0), preferred_element_type=jnp.float32
        )
        mixed = product[:depth] + product[depth:]
        store(row, mixed[:, :width])
        store(row + 1, mixed[:, width:])
        return 0

    lax.fori_loop(0, rows // 2, pair, 0, unroll=4)


def along_x(center, above, below, taps, emit):
    blocks, rows, planes, _ = center.shape
    margin = above.shape[1]
    tiles = planes // 8
    group = 16 if rows % 16 == 0 else 8

    def column(index, _):
        block, start = index // tiles, pl.multiple_of((index % tiles) * 8, 8)

        def row(place):
            if place < 0:
                return above[block, margin + place, pl.ds(start, 8), :]
            if place < rows:
                return center[block, place, pl.ds(start, 8), :]
            return below[block, place - rows, pl.ds(start, 8), :]

        for first in range(0, rows, group):
            sums = [None] * group
            for place in range(first - margin, first + group + margin):
                value = row(place)
                for slot in range(group):
                    tap = place - (first + slot) + margin
                    if 0 <= tap <= 2 * margin:
                        term = taps[tap] * value
                        sums[slot] = term if sums[slot] is None else sums[slot] + term
            for slot in range(group):
                emit(block, start, first + slot, sums[slot])
        return 0

    lax.fori_loop(0, blocks * tiles, column, 0)


def plane_loader(ref):
    blocks, _, planes, width = ref.shape
    return lambda row: ref[:, row].reshape(blocks * planes, width)


def plane_storer(ref):
    blocks, _, planes, width = ref.shape

    def store(row, value):
        ref[:, row] = value.reshape(blocks, planes, width)

    return store


def copy_ends(ref, head, tail):
    rows, kept = ref.shape[1], head.shape[1]
    head[...] = ref[:, :kept]
    tail[...] = ref[:, rows - kept :]


def blur_kernel(current, matrix_y, matrix_z, out, head, tail):
    along_yz(plane_loader(current), plane_storer(out), matrix_y[...], matrix_z[...], out.shape[1])
    copy_ends(out, head, tail)


def quotient_kernel(taps, center, above, below, data, matrix_y, matrix_z, out, head, tail, blurred):
    length = taps.shape[0]
    weights = [taps[length - 1 - k] for k in range(length)]

    def emit(block, start, row, value):
        blurred[block, row, pl.ds(start, 8), :] = value

    along_x(center, above, below, weights, emit)
    data_of, blurred_of = plane_loader(data), plane_loader(blurred)
    along_yz(
        lambda row: data_of(row) / blurred_of(row),
        plane_storer(out),
        matrix_y[...],
        matrix_z[...],
        out.shape[1],
    )
    copy_ends(out, head, tail)


def update_kernel(taps, center, above, below, current, matrix_y, matrix_z, updated, out, head, tail):
    weights = [taps[k] for k in range(taps.shape[0])]

    def emit(block, start, row, value):
        updated[block, row, pl.ds(start, 8), :] = current[block, row, pl.ds(start, 8), :] * value

    along_x(center, above, below, weights, emit)
    along_yz(plane_loader(updated), plane_storer(out), matrix_y[...], matrix_z[...], out.shape[1])
    copy_ends(out, head, tail)


def finish_kernel(taps, center, above, below, current, updated):
    weights = [taps[k] for k in range(taps.shape[0])]

    def emit(block, start, row, value):
        updated[block, row, pl.ds(start, 8), :] = current[block, row, pl.ds(start, 8), :] * value

    along_x(center, above, below, weights, emit)


def call(kernel, name, outs, in_specs, scratch=()):
    return pl.pallas_call(
        kernel,
        out_shape=outs,
        in_specs=in_specs,
        out_specs=jax.tree.map(lambda _: WHOLE, outs),
        scratch_shapes=list(scratch),
        compiler_params=pltpu.CompilerParams(vmem_limit_bytes=VMEM_LIMIT),
        name=name,
    )


def turn_kernel(source, target):
    target[0] = jnp.swapaxes(source[...], 0, 1)


def turn_back_kernel(source, target):
    target[...] = jnp.swapaxes(source[0], 0, 1)


def to_pencils(planes, count, run):
    depth, extent, width = planes.shape
    rows = extent // count
    if depth % 8 == 0:
        blocks = pl.pallas_call(
            turn_kernel,
            grid=(count,),
            out_shape=jax.ShapeDtypeStruct((count, rows, depth, width), planes.dtype),
            in_specs=[pl.BlockSpec((depth, rows, width), lambda g: (0, position(g, run), 0))],
            out_specs=pl.BlockSpec((1, rows, depth, width), lambda g: (g, 0, 0, 0)),
            name="turn",
        )(planes)
        return lax.all_to_all(blocks, "slab", split_axis=0, concat_axis=0, tiled=True)
    order = device_order(count, run)
    blocks = planes.reshape(depth, count, rows, width).transpose(1, 0, 2, 3)
    blocks = jnp.stack([blocks[order.index(d)] for d in range(count)])
    blocks = lax.all_to_all(blocks, "slab", split_axis=0, concat_axis=0, tiled=True)
    return blocks.reshape(1, count * depth, rows, width).swapaxes(1, 2)


def to_planes(pencils, count, run, depth):
    rows, width = pencils.shape[1], pencils.shape[3]
    if depth % 8 == 0:
        blocks = lax.all_to_all(pencils, "slab", split_axis=0, concat_axis=0, tiled=True)
        return pl.pallas_call(
            turn_back_kernel,
            grid=(count,),
            out_shape=jax.ShapeDtypeStruct((depth, rows * count, width), pencils.dtype),
            in_specs=[pl.BlockSpec((1, rows, depth, width), lambda g: (g, 0, 0, 0))],
            out_specs=pl.BlockSpec((depth, rows, width), lambda g: (0, position(g, run), 0)),
            name="turn_back",
        )(blocks)
    order = device_order(count, run)
    blocks = pencils.swapaxes(1, 2).reshape(count, depth, rows, width)
    blocks = lax.all_to_all(blocks, "slab", split_axis=0, concat_axis=0, tiled=True)
    blocks = jnp.stack([blocks[d] for d in order])
    return blocks.transpose(1, 0, 2, 3).reshape(depth, rows * count, width)


def halos(head, tail, margin, count, run):
    order = device_order(count, run)
    rows = head.shape[1]
    above, below, need, hop = [], [], margin, 1
    while need > 0:
        size = min(rows, need)
        forth = [(order[p], order[p + hop]) for p in range(count - hop)]
        back = [(order[p + hop], order[p]) for p in range(count - hop)]
        above.insert(0, lax.ppermute(tail[:, rows - size :], "slab", forth))
        below.append(lax.ppermute(head[:, :size], "slab", back))
        need, hop = need - size, hop + 1
    if len(above) == 1:
        return above[0], below[0]
    return jnp.concatenate(above, axis=1), jnp.concatenate(below, axis=1)


def body(estimate, recorded, lateral, axial_taps):
    count = lax.axis_size("slab")
    run = max(count // 4, 1)
    depth = estimate.shape[0]
    views, margin = recorded.shape[0], lateral.shape[2] // 2

    current = to_pencils(estimate, count, run)
    data = [to_pencils(recorded[v], count, run) for v in range(views)]
    blocks, rows, planes, width = current.shape
    taps = [normalized(lateral[v, 0]) for v in range(views)]
    columns = [banded(normalized(lateral[v, 1]), width) for v in range(views)]
    depths = [banded(normalized(axial_taps[v]), blocks * planes) for v in range(views)]

    volume = jax.ShapeDtypeStruct(current.shape, jnp.float32)
    end = jax.ShapeDtypeStruct((blocks, min(margin, rows), planes, width), jnp.float32)
    held = pltpu.VMEM(current.shape, jnp.float32)
    blur = call(blur_kernel, "blur", (volume, end, end), [WHOLE] * 3)
    quotient = call(quotient_kernel, "quotient", (volume, end, end), [SCALARS] + [WHOLE] * 6, [held])
    update = call(update_kernel, "update", (volume, volume, end, end), [SCALARS] + [WHOLE] * 6)
    finish = call(finish_kernel, "finish", volume, [SCALARS] + [WHOLE] * 4)

    center, head, tail = blur(current, columns[0], depths[0].T)
    for v in range(views):
        above, below = halos(head, tail, margin, count, run)
        center, head, tail = quotient(taps[v], center, above, below, data[v], columns[v].T, depths[v])
        above, below = halos(head, tail, margin, count, run)
        if v + 1 < views:
            current, center, head, tail = update(
                taps[v], center, above, below, current, columns[v + 1], depths[v + 1].T
            )
        else:
            current = finish(taps[v], center, above, below, current)
    return to_planes(current, count, run, depth)


def solution(mesh):
    in_specs = (P("slab", "groups", None), P(None, "slab", "groups", None), P(), P())
    out_specs = P("slab", "groups", None)
    return jax.shard_map(body, mesh=mesh, in_specs=in_specs, out_specs=out_specs, check_vma=False)
```

time: 2020 us -> 914 us (0.45); the launches traced: 2000 us -> 911 us
  other arithmetic: 777 us -> 14.6 us
  waiting for transfers between devices: 818 us -> 420 us
  Pallas kernels: 0 us -> 231 us
  starting transfers between devices: 222 us -> 121 us
  blocking collectives: 0 us -> 99.3 us
  local copies, waits for them, and re-layouts: 117 us -> 25.6 us
  matrix products: 60.3 us -> 0 us
    add x12 -> x0, other arithmetic: 590 us -> none  [correlate(): total + kernel[position] * lax.slice_in_dim(padded, position, position +...]
    all_to_all x12 -> x5, waiting for transfers between devices: 818 us -> 256 us  [to_pencils(): lax.all_to_all(blocks, 'slab', split_axis=0, concat_axis=0, tiled=True)]
    pallas_call x0 -> x15, Pallas kernels: none -> 231 us  [the longest x4 81 us: body(): quotient(taps[v], center, above, below, data[v], columns[v].T, depths[v])]
    mul x4 -> x0, other arithmetic: 170 us -> none  [body(): current = current * returned]
    ppermute x0 -> x16, waiting for transfers between devices: none -> 164 us  [the longest x8 86.8 us: halos(): below.append(lax.ppermute(head[:, :size], 'slab', back))]
    all_to_all x12 -> x5, starting transfers between devices: 222 us -> 84.5 us  [to_pencils(): lax.all_to_all(blocks, 'slab', split_axis=0, concat_axis=0, tiled=True)]
    all_to_all x0 -> x1, blocking collectives: none -> 99.3 us  [to_planes(): lax.all_to_all(pencils, 'slab', split_axis=0, concat_axis=0, tiled=True)]
    dot_general x8 -> x0, matrix products: 60.3 us -> none  [the longest x4 36 us: backward(): jnp.tensordot(matrix.T, pencil_blur, axes=(1, 0), precision=lax.Precision...]
  transfers between devices with their start and end apart: 12 -> 21, of which waited for: 12 -> 20; matrix products, arithmetic and copies ran while one was open for 6% -> 4% of each run, Pallas kernels for 0% -> 19%
where the time goes in v1:
time: 914 us; the launch traced here: 911 us
  waiting for transfers between devices  420 us (46%)
  Pallas kernels  231 us (25%)
  starting transfers between devices  121 us (13%)
  blocking collectives  99.3 us (11%)
  local copies, waits for them, and re-layouts  25.6 us (3%)
  other arithmetic  14.6 us (2%)
    all_to_all x5, waiting for transfers between devices, to_pencils(): lax.all_to_all(blocks, 'slab', split_axis=0, concat_axis=0, tiled=True)  256 us
    all_to_all x1, blocking collectives, to_planes(): lax.all_to_all(pencils, 'slab', split_axis=0, concat_axis=0, tiled=True)  99.3 us
    ppermute x8, waiting for transfers between devices, halos(): below.append(lax.ppermute(head[:, :size], 'slab', back))  86.8 us
    all_to_all x5, starting transfers between devices, to_pencils(): lax.all_to_all(blocks, 'slab', split_axis=0, concat_axis=0, tiled=True)  84.5 us
    pallas_call x4, Pallas kernels, body(): quotient(taps[v], center, above, below, data[v], columns[v].T, depths[v])  81 us
    ppermute x8, waiting for transfers between devices, halos(): above.insert(0, lax.ppermute(tail[:, rows - size:], 'slab', forth))  77.2 us
    pallas_call x3, Pallas kernels, body(): update(taps[v], center, above, below, current, columns[v + 1], depths[v +...  63.1 us
    pallas_call x5, Pallas kernels, to_pencils(): pl.pallas_call(turn_kernel, grid=(count,), out_shape=jax.ShapeDtypeStruct...  51.8 us
  transfers between devices with their start and end apart: 21, of which 20 were waited for; matrix products, arithmetic and copies ran while one was open for 4% of the time, Pallas kernels for 19%

profile of v1, /device:TPU:1, one launch (start us, length us, event | category | flops | bytes accessed | tf_op | source)
XLA Modules:
  0.0 911.1 jit_solution(17266806059218336951)
XLA Ops:
  0.0 10.3 %turn.5 = f32[16,64,8,128]{3,2,1,0:T(8,128)} custom-call(f32[8,1024,128]{2,1,0:T(8,128)} %source.1), custom_call_target="tpu_custom_call" | custom-call | tf_op jit(solution)/shard_map/turn/pallas_call | solution.py:192
  10.3 7.3 all-to-all-start
  17.7 12.2 %slice_bitcast_fusion = (f32[8,1024,128]{2,1,0:T(8,128)}, f32[8,1024,128]{2,1,0:T(8,128)}, f32[8,1024,128]{2,1,0:T(8,128)}, f32[8,1024,128]{2,1,0:T(8,128)}) fusion(f32[4,8,1024,128]{3,2,1,0:T(8,128)} %param.5), kind=kLoop, calls=%fused_computation.5 | loop fusion | bytes 33554432 | tf_op jit(solution)/shard_map/squeeze | solution.py:250
  29.8 10.4 %turn.6 = f32[16,64,8,128]{3,2,1,0:T(8,128)} custom-call(f32[8,1024,128]{2,1,0:T(8,128)} %get-tuple-element.81.source), custom_call_target="tpu_custom_call" | custom-call | tf_op jit(solution)/shard_map/turn/pallas_call | solution.py:192
  40.2 55.5 %all-to-all-done.current = f32[16,64,8,128]{3,2,1,0:T(8,128)} async-done(((f32[16,64,8,128]{3,2,1,0:T(8,128)}), f32[16,64,8,128]{3,2,1,0:T(8,128)}, u32[]{:S(2)}, u32[]{:S(2)}) %all-to-all-start) | async-done | bytes 4194336 | tf_op jit(solution)/shard_map/all_to_all | solution.py:200
  95.7 19.3 %all-to-all-start.1 = ((f32[16,64,8,128]{3,2,1,0:T(8,128)}), f32[16,64,8,128]{3,2,1,0:T(8,128)}, u32[]{:S(2)}, u32[]{:S(2)}) async-start(f32[16,64,8,128]{3,2,1,0:T(8,128)} %turn.6), calls=%async_computation.1 | async-start | bytes 8388608 | tf_op jit(solution)/shard_map/all_to_all | solution.py:200
  115.0 10.4 %turn.7 = f32[16,64,8,128]{3,2,1,0:T(8,128)} custom-call(f32[8,1024,128]{2,1,0:T(8,128)} %get-tuple-element.80.source), custom_call_target="tpu_custom_call" | custom-call | tf_op jit(solution)/shard_map/turn/pallas_call | solution.py:192
  125.4 67.7 %all-to-all-done.1.data = f32[16,64,8,128]{3,2,1,0:T(8,128)} async-done(((f32[16,64,8,128]{3,2,1,0:T(8,128)}), f32[16,64,8,128]{3,2,1,0:T(8,128)}, u32[]{:S(2)}, u32[]{:S(2)}) %all-to-all-start.1) | async-done | bytes 4194336 | tf_op jit(solution)/shard_map/all_to_all | solution.py:200
  193.1 19.3 %all-to-all-start.2 = ((f32[16,64,8,128]{3,2,1,0:T(8,128)}), f32[16,64,8,128]{3,2,1,0:T(8,128)}, u32[]{:S(2)}, u32[]{:S(2)}) async-start(f32[16,64,8,128]{3,2,1,0:T(8,128)} %turn.7), calls=%async_computation.2 | async-start | bytes 8388608 | tf_op jit(solution)/shard_map/all_to_all | solution.py:200
  212.4 10.4 %turn.8 = f32[16,64,8,128]{3,2,1,0:T(8,128)} custom-call(f32[8,1024,128]{2,1,0:T(8,128)} %get-tuple-element.82.source), custom_call_target="tpu_custom_call" | custom-call | tf_op jit(solution)/shard_map/turn/pallas_call | solution.py:192
  222.8 67.7 %all-to-all-done.2.data = f32[16,64,8,128]{3,2,1,0:T(8,128)} async-done(((f32[16,64,8,128]{3,2,1,0:T(8,128)}), f32[16,64,8,128]{3,2,1,0:T(8,128)}, u32[]{:S(2)}, u32[]{:S(2)}) %all-to-all-start.2) | async-done | bytes 4194336 | tf_op jit(solution)/shard_map/all_to_all | solution.py:200
  290.5 19.3 %all-to-all-start.3 = ((f32[16,64,8,128]{3,2,1,0:T(8,128)}), f32[16,64,8,128]{3,2,1,0:T(8,128)}, u32[]{:S(2)}, u32[]{:S(2)}) async-start(f32[16,64,8,128]{3,2,1,0:T(8,128)} %turn.8), calls=%async_computation.3 | async-start | bytes 8388608 | tf_op jit(solution)/shard_map/all_to_all | solution.py:200
  309.8 10.4 %turn.9 = f32[16,64,8,128]{3,2,1,0:T(8,128)} custom-call(f32[8,1024,128]{2,1,0:T(8,128)} %get-tuple-element.79.source), custom_call_target="tpu_custom_call" | custom-call | tf_op jit(solution)/shard_map/turn/pallas_call | solution.py:192
  320.8 2.4 divide_bitcast_fusion.6
  323.3 64.6 %all-to-all-done.3.data = f32[16,64,8,128]{3,2,1,0:T(8,128)} async-done(((f32[16,64,8,128]{3,2,1,0:T(8,128)}), f32[16,64,8,128]{3,2,1,0:T(8,128)}, u32[]{:S(2)}, u32[]{:S(2)}) %all-to-all-start.3) | async-done | bytes 4194336 | tf_op jit(solution)/shard_map/all_to_all | solution.py:200
  387.9 19.3 %all-to-all-start.4 = ((f32[16,64,8,128]{3,2,1,0:T(8,128)}), f32[16,64,8,128]{3,2,1,0:T(8,128)}, u32[]{:S(2)}, u32[]{:S(2)}) async-start(f32[16,64,8,128]{3,2,1,0:T(8,128)} %turn.9), calls=%async_computation.4 | async-start | bytes 8388608 | tf_op jit(solution)/shard_map/all_to_all | solution.py:200
  407.2 3.7 select_reduce_fusion
  412.3 5.5 divide_bitcast_fusion.7
  417.8 1.7 select_reduce_fusion.4
  419.5 9.9 %blur.1 = (f32[16,64,8,128]{3,2,1,0:T(8,128)}, f32[16,15,8,128]{3,2,1,0:T(8,128)}, f32[16,15,8,128]{3,2,1,0:T(8,128)}) custom-call(f32[16,64,8,128]{3,2,1,0:T(8,128)} %all-to-all-done.current, f32[128,128]{1,0:T(8,128)} %get-tuple-element.66.matrix_y, f32[128,128]{1,0:T(8,128)} %bitcast.40), custom_call_target="tpu_custom_call" | custom-call | tf_op jit(solution)/shard_map/blur/pallas_call | solution.py:264
  429.4 3.5 collective-permute-start
  432.9 1.9 collective-permute-start.1
  435.6 14.3 %collective-permute-done.above = f32[16,15,8,128]{3,2,1,0:T(8,128)S(1)} collective-permute-done((f32[16,15,8,128]{3,2,1,0:T(8,128)}, f32[16,15,8,128]{3,2,1,0:T(8,128)S(1)}, u32[]{:S(2)}, u32[]{:S(2)}) %collective-permute-start) | collective-permute-done | bytes 983072 | tf_op jit(solution)/shard_map/ppermute | solution.py:235
  449.9 9.3 %collective-permute-done.1.below = f32[16,15,8,128]{3,2,1,0:T(8,128)S(1)} collective-permute-done((f32[16,15,8,128]{3,2,1,0:T(8,128)}, f32[16,15,8,128]{3,2,1,0:T(8,128)S(1)}, u32[]{:S(2)}, u32[]{:S(2)}) %collective-permute-start.1) | collective-permute-done | bytes 983072 | tf_op jit(solution)/shard_map/ppermute | solution.py:236
  460.2 20.3 %quotient.4 = (f32[16,64,8,128]{3,2,1,0:T(8,128)}, f32[16,15,8,128]{3,2,1,0:T(8,128)}, f32[16,15,8,128]{3,2,1,0:T(8,128)}) custom-call(f32[31]{0:T(128)} %get-tuple-element.88.taps, f32[16,64,8,128]{3,2,1,0:T(8,128)} %get-tuple-element.32.center, f32[16,15,8,128]{3,2,1,0:T(8,128)} %copy-done.6, f32[16,15,8,128]{3,2,1,0:T(8,128)} %copy-done.12, ...), custom_call_target="tpu_custom_call" | custom-call | tf_op jit(solution)/shard_map/quotient/pallas_call | solution.py:267
  480.4 1.9 collective-permute-start.2
  482.3 2.5 collective-permute-start.3
  485.5 13.6 %collective-permute-done.2.above = f32[16,15,8,128]{3,2,1,0:T(8,128)S(1)} collective-permute-done((f32[16,15,8,128]{3,2,1,0:T(8,128)}, f32[16,15,8,128]{3,2,1,0:T(8,128)S(1)}, u32[]{:S(2)}, u32[]{:S(2)}) %collective-permute-start.2) | collective-permute-done | bytes 983072 | tf_op jit(solution)/shard_map/ppermute | solution.py:235
  499.1 27.2 %collective-permute-done.3.below = f32[16,15,8,128]{3,2,1,0:T(8,128)S(1)} collective-permute-done((f32[16,15,8,128]{3,2,1,0:T(8,128)}, f32[16,15,8,128]{3,2,1,0:T(8,128)S(1)}, u32[]{:S(2)}, u32[]{:S(2)}) %collective-permute-start.3) | collective-permute-done | bytes 983072 | tf_op jit(solution)/shard_map/ppermute | solution.py:236
  527.3 21.0 %update.3 = (f32[16,64,8,128]{3,2,1,0:T(8,128)}, f32[16,64,8,128]{3,2,1,0:T(8,128)}, f32[16,15,8,128]{3,2,1,0:T(8,128)}, f32[16,15,8,128]{3,2,1,0:T(8,128)}) custom-call(f32[31]{0:T(128)} %get-tuple-element.88.taps, f32[16,64,8,128]{3,2,1,0:T(8,128)} %get-tuple-element.35.center, f32[16,15,8,128]{3,2,1,0:T(8,128)} %copy-done.7, ...), custom_call_target="tpu_custom_call" | custom-call | tf_op jit(solution)/shard_map/update/pallas_call | solution.py:270
  548.3 1.9 collective-permute-start.4
  550.3 2.5 collective-permute-start.5
  553.5 8.1 collective-permute-done.4.above
  561.6 5.5 collective-permute-done.5.below
  568.0 20.3 %quotient.5 = (f32[16,64,8,128]{3,2,1,0:T(8,128)}, f32[16,15,8,128]{3,2,1,0:T(8,128)}, f32[16,15,8,128]{3,2,1,0:T(8,128)}) custom-call(f32[31]{0:T(128)} %get-tuple-element.87.taps, f32[16,64,8,128]{3,2,1,0:T(8,128)} %get-tuple-element.38.center, f32[16,15,8,128]{3,2,1,0:T(8,128)} %copy-done.9, f32[16,15,8,128]{3,2,1,0:T(8,128)} %copy-done.14, ...), custom_call_target="tpu_custom_call" | custom-call | tf_op jit(solution)/shard_map/quotient/pallas_call | solution.py:267
  588.3 1.9 collective-permute-start.6
  590.2 2.6 collective-permute-start.7
  593.6 8.0 collective-permute-done.6.above
  601.6 24.4 %collective-permute-done.7.below = f32[16,15,8,128]{3,2,1,0:T(8,128)S(1)} collective-permute-done((f32[16,15,8,128]{3,2,1,0:T(8,128)}, f32[16,15,8,128]{3,2,1,0:T(8,128)S(1)}, u32[]{:S(2)}, u32[]{:S(2)}) %collective-permute-start.7) | collective-permute-done | bytes 983072 | tf_op jit(solution)/shard_map/ppermute | solution.py:236
  626.9 21.1 %update.4 = (f32[16,64,8,128]{3,2,1,0:T(8,128)}, f32[16,64,8,128]{3,2,1,0:T(8,128)}, f32[16,15,8,128]{3,2,1,0:T(8,128)}, f32[16,15,8,128]{3,2,1,0:T(8,128)}) custom-call(f32[31]{0:T(128)} %get-tuple-element.87.taps, f32[16,64,8,128]{3,2,1,0:T(8,128)} %get-tuple-element.41.center, f32[16,15,8,128]{3,2,1,0:T(8,128)} %copy-done.5, ...), custom_call_target="tpu_custom_call" | custom-call | tf_op jit(solution)/shard_map/update/pallas_call | solution.py:270
  648.0 1.9 collective-permute-start.8
  649.9 2.5 collective-permute-start.9
  653.1 8.1 collective-permute-done.8.above
  661.2 5.7 collective-permute-done.9.below
  667.9 20.3 %quotient.6 = (f32[16,64,8,128]{3,2,1,0:T(8,128)}, f32[16,15,8,128]{3,2,1,0:T(8,128)}, f32[16,15,8,128]{3,2,1,0:T(8,128)}) custom-call(f32[31]{0:T(128)} %get-tuple-element.86.taps, f32[16,64,8,128]{3,2,1,0:T(8,128)} %get-tuple-element.45.center, f32[16,15,8,128]{3,2,1,0:T(8,128)} %copy-done.10, f32[16,15,8,128]{3,2,1,0:T(8,128)} %copy-done.15, ...), custom_call_target="tpu_custom_call" | custom-call | tf_op jit(solution)/shard_map/quotient/pallas_call | solution.py:267
  688.2 1.9 collective-permute-start.10
  690.1 2.5 collective-permute-start.11
  693.3 8.1 collective-permute-done.10.above
  701.4 4.9 collective-permute-done.11.below
  707.2 21.0 %update.5 = (f32[16,64,8,128]{3,2,1,0:T(8,128)}, f32[16,64,8,128]{3,2,1,0:T(8,128)}, f32[16,15,8,128]{3,2,1,0:T(8,128)}, f32[16,15,8,128]{3,2,1,0:T(8,128)}) custom-call(f32[31]{0:T(128)} %get-tuple-element.86.taps, f32[16,64,8,128]{3,2,1,0:T(8,128)} %get-tuple-element.48.center, f32[16,15,8,128]{3,2,1,0:T(8,128)} %copy-done.3, ...), custom_call_target="tpu_custom_call" | custom-call | tf_op jit(solution)/shard_map/update/pallas_call | solution.py:270
  728.2 1.9 collective-permute-start.12
  730.2 2.5 collective-permute-start.13
  733.4 8.1 collective-permute-done.12.above
  741.5 4.9 collective-permute-done.13.below
  746.4 1.0 copy-done.4
  747.3 20.2 %quotient.7 = (f32[16,64,8,128]{3,2,1,0:T(8,128)}, f32[16,15,8,128]{3,2,1,0:T(8,128)}, f32[16,15,8,128]{3,2,1,0:T(8,128)}) custom-call(f32[31]{0:T(128)} %get-tuple-element.85.taps, f32[16,64,8,128]{3,2,1,0:T(8,128)} %get-tuple-element.52.center, f32[16,15,8,128]{3,2,1,0:T(8,128)} %copy-done.2, f32[16,15,8,128]{3,2,1,0:T(8,128)} %copy-done.4, ...), custom_call_target="tpu_custom_call" | custom-call | tf_op jit(solution)/shard_map/quotient/pallas_call | solution.py:267
  767.6 1.9 collective-permute-start.14
  769.5 2.5 collective-permute-start.15
  772.0 8.9 collective-permute-done.14.above
  780.8 4.9 collective-permute-done.15.below
  785.7 1.0 copy-done.1
  786.7 14.8 %finish.1 = f32[16,64,8,128]{3,2,1,0:T(8,128)} custom-call(f32[31]{0:T(128)} %get-tuple-element.85.taps, f32[16,64,8,128]{3,2,1,0:T(8,128)} %get-tuple-element.55.center, f32[16,15,8,128]{3,2,1,0:T(8,128)} %copy-done, f32[16,15,8,128]{3,2,1,0:T(8,128)} %copy-done.1, f32[16,64,8,128]{3,2,1,0:T(8,128)} %get-tuple-element.58.current), custom_call_target="tpu_custom_call" | custom-call | tf_op jit(solution)/shard_map/finish/pallas_call | solution.py:274
  801.5 99.3 %all_to_all.30.source = f32[16,64,8,128]{3,2,1,0:T(8,128)} all-to-all(f32[16,64,8,128]{3,2,1,0:T(8,128)} %finish.1), channel_id=1, replica_groups=mesh['groups'=2,'slab'=16] {'slab'}, dimensions={0} | all-to-all | bytes 8388608 | tf_op jit(solution)/shard_map/all_to_all | solution.py:211
  900.7 10.3 %turn_back.1 = f32[8,1024,128]{2,1,0:T(8,128)} custom-call(f32[16,64,8,128]{3,2,1,0:T(8,128)} %all_to_all.30.source), custom_call_target="tpu_custom_call" | custom-call | tf_op jit(solution)/shard_map/turn_back/pallas_call | solution.py:212
  (63 shorter events, 12.8 us)
Async XLA Ops:
  10.3 85.4 %all-to-all-start = ((f32[16,64,8,128]{3,2,1,0:T(8,128)}), f32[16,64,8,128]{3,2,1,0:T(8,128)}, u32[]{:S(2)}, u32[]{:S(2)}) async-start(f32[16,64,8,128]{3,2,1,0:T(8,128)} %turn.5), calls=%async_computation | async-start | bytes 8388608 | tf_op jit(solution)/shard_map/all_to_all | solution.py:200
  95.7 97.4 %all-to-all-start.1 = ((f32[16,64,8,128]{3,2,1,0:T(8,128)}), f32[16,64,8,128]{3,2,1,0:T(8,128)}, u32[]{:S(2)}, u32[]{:S(2)}) async-start(f32[16,64,8,128]{3,2,1,0:T(8,128)} %turn.6), calls=%async_computation.1 | async-start | bytes 8388608 | tf_op jit(solution)/shard_map/all_to_all | solution.py:200
  193.1 97.4 %all-to-all-start.2 = ((f32[16,64,8,128]{3,2,1,0:T(8,128)}), f32[16,64,8,128]{3,2,1,0:T(8,128)}, u32[]{:S(2)}, u32[]{:S(2)}) async-start(f32[16,64,8,128]{3,2,1,0:T(8,128)} %turn.7), calls=%async_computation.2 | async-start | bytes 8388608 | tf_op jit(solution)/shard_map/all_to_all | solution.py:200
  290.5 97.4 %all-to-all-start.3 = ((f32[16,64,8,128]{3,2,1,0:T(8,128)}), f32[16,64,8,128]{3,2,1,0:T(8,128)}, u32[]{:S(2)}, u32[]{:S(2)}) async-start(f32[16,64,8,128]{3,2,1,0:T(8,128)} %turn.8), calls=%async_computation.3 | async-start | bytes 8388608 | tf_op jit(solution)/shard_map/all_to_all | solution.py:200
  309.8 10.4 %copy-start.25 = (f32[4,101]{1,0:T(4,128)S(1)}, f32[4,101]{1,0:T(4,128)}, u32[]{:S(2)}) copy-start(f32[4,101]{1,0:T(4,128)} %param.7) | copy-start | bytes 4852
  323.2 88.3 %copy-start.24 = (f32[4,2,31]{2,1,0:T(2,128)S(1)}, f32[4,2,31]{2,1,0:T(2,128)}, u32[]{:S(2)}) copy-start(f32[4,2,31]{2,1,0:T(2,128)} %param.6) | copy-start | bytes 2980
  387.9 345.5 %all-to-all-start.4 = ((f32[16,64,8,128]{3,2,1,0:T(8,128)}), f32[16,64,8,128]{3,2,1,0:T(8,128)}, u32[]{:S(2)}, u32[]{:S(2)}) async-start(f32[16,64,8,128]{3,2,1,0:T(8,128)} %turn.9), calls=%async_computation.4 | async-start | bytes 8388608 | tf_op jit(solution)/shard_map/all_to_all | solution.py:200
  410.8 48.4 %copy-start.22 = (f32[128,128]{1,0:T(8,128)}, f32[128,128]{1,0:T(8,128)S(1)}, u32[]{:S(2)}) copy-start(f32[128,128]{1,0:T(8,128)S(1)} %get-tuple-element.62.matrix_z) | copy-start | bytes 196612
  410.8 74.0 %copy-start.20 = (f32[128,128]{1,0:T(8,128)}, f32[128,128]{1,0:T(8,128)S(1)}, u32[]{:S(2)}) copy-start(f32[128,128]{1,0:T(8,128)S(1)} %get-tuple-element.61.matrix_z) | copy-start | bytes 196612
  410.8 182.0 %copy-start.18 = (f32[128,128]{1,0:T(8,128)}, f32[128,128]{1,0:T(8,128)S(1)}, u32[]{:S(2)}) copy-start(f32[128,128]{1,0:T(8,128)S(1)} %get-tuple-element.60.matrix_z) | copy-start | bytes 196612
  410.9 281.7 %copy-start.16 = (f32[128,128]{1,0:T(8,128)}, f32[128,128]{1,0:T(8,128)S(1)}, u32[]{:S(2)}) copy-start(f32[128,128]{1,0:T(8,128)S(1)} %get-tuple-element.59.matrix_z) | copy-start | bytes 196612
  419.5 15.4 %copy-start.23 = (f32[128,128]{1,0:T(8,128)S(1)}, f32[128,128]{1,0:T(8,128)}, u32[]{:S(2)}) copy-start(f32[128,128]{1,0:T(8,128)} %get-tuple-element.66.matrix_y) | copy-start | bytes 196612
  429.4 20.5 %collective-permute-start = (f32[16,15,8,128]{3,2,1,0:T(8,128)}, f32[16,15,8,128]{3,2,1,0:T(8,128)S(1)}, u32[]{:S(2)}, u32[]{:S(2)}) collective-permute-start(f32[16,15,8,128]{3,2,1,0:T(8,128)} %get-tuple-element.33), channel_id=1, source_target_pairs={{0,1},{1,2},{2,3},{3,7},{7,6},{6,5},{5,4},{4,8},{8,9},{9,10},{10,1... | collective-permute-start | bytes 2949128 | tf_op jit(solution)/shard_map/ppermute | solution.py:235
  432.9 26.3 %collective-permute-start.1 = (f32[16,15,8,128]{3,2,1,0:T(8,128)}, f32[16,15,8,128]{3,2,1,0:T(8,128)S(1)}, u32[]{:S(2)}, u32[]{:S(2)}) collective-permute-start(f32[16,15,8,128]{3,2,1,0:T(8,128)} %get-tuple-element.34), channel_id=1, source_target_pairs={{1,0},{2,1},{3,2},{7,3},{6,7},{5,6},{4,5},{8,4},{9,8},{10,9},{11,1... | collective-permute-start | bytes 2949128 | tf_op jit(solution)/shard_map/ppermute | solution.py:236
  449.9 9.3 %copy-start.6 = (f32[16,15,8,128]{3,2,1,0:T(8,128)}, f32[16,15,8,128]{3,2,1,0:T(8,128)S(1)}, u32[]{:S(2)}) copy-start(f32[16,15,8,128]{3,2,1,0:T(8,128)S(1)} %collective-permute-done.above) | copy-start | bytes 2949124
  459.2 1.0 copy-start.12
  480.4 18.7 %collective-permute-start.2 = (f32[16,15,8,128]{3,2,1,0:T(8,128)}, f32[16,15,8,128]{3,2,1,0:T(8,128)S(1)}, u32[]{:S(2)}, u32[]{:S(2)}) collective-permute-start(f32[16,15,8,128]{3,2,1,0:T(8,128)} %get-tuple-element.36), channel_id=1, source_target_pairs={{0,1},{1,2},{2,3},{3,7},{7,6},{6,5},{5,4},{4,8},{8,9},{9,10},{10,1... | collective-permute-start | bytes 2949128 | tf_op jit(solution)/shard_map/ppermute | solution.py:235
  482.3 44.0 %collective-permute-start.3 = (f32[16,15,8,128]{3,2,1,0:T(8,128)}, f32[16,15,8,128]{3,2,1,0:T(8,128)S(1)}, u32[]{:S(2)}, u32[]{:S(2)}) collective-permute-start(f32[16,15,8,128]{3,2,1,0:T(8,128)} %get-tuple-element.37), channel_id=1, source_target_pairs={{1,0},{2,1},{3,2},{7,3},{6,7},{5,6},{4,5},{8,4},{9,8},{10,9},{11,1... | collective-permute-start | bytes 2949128 | tf_op jit(solution)/shard_map/ppermute | solution.py:236
  499.1 27.2 %copy-start.7 = (f32[16,15,8,128]{3,2,1,0:T(8,128)}, f32[16,15,8,128]{3,2,1,0:T(8,128)S(1)}, u32[]{:S(2)}) copy-start(f32[16,15,8,128]{3,2,1,0:T(8,128)S(1)} %collective-permute-done.2.above) | copy-start | bytes 2949124
  526.3 1.0 copy-start.13
  527.3 25.4 %copy-start.21 = (f32[128,128]{1,0:T(8,128)S(1)}, f32[128,128]{1,0:T(8,128)}, u32[]{:S(2)}) copy-start(f32[128,128]{1,0:T(8,128)} %get-tuple-element.65.matrix_y) | copy-start | bytes 196612
  548.3 13.3 %collective-permute-start.4 = (f32[16,15,8,128]{3,2,1,0:T(8,128)}, f32[16,15,8,128]{3,2,1,0:T(8,128)S(1)}, u32[]{:S(2)}, u32[]{:S(2)}) collective-permute-start(f32[16,15,8,128]{3,2,1,0:T(8,128)} %get-tuple-element.39), channel_id=1, source_target_pairs={{0,1},{1,2},{2,3},{3,7},{7,6},{6,5},{5,4},{4,8},{8,9},{9,10},{10,1... | collective-permute-start | bytes 2949128 | tf_op jit(solution)/shard_map/ppermute | solution.py:235
  550.3 16.8 %collective-permute-start.5 = (f32[16,15,8,128]{3,2,1,0:T(8,128)}, f32[16,15,8,128]{3,2,1,0:T(8,128)S(1)}, u32[]{:S(2)}, u32[]{:S(2)}) collective-permute-start(f32[16,15,8,128]{3,2,1,0:T(8,128)} %get-tuple-element.40), channel_id=1, source_target_pairs={{1,0},{2,1},{3,2},{7,3},{6,7},{5,6},{4,5},{8,4},{9,8},{10,9},{11,1... | collective-permute-start | bytes 2949128 | tf_op jit(solution)/shard_map/ppermute | solution.py:236
  561.6 5.5 copy-start.9
  567.1 0.9 copy-start.14
  588.3 13.3 %collective-permute-start.6 = (f32[16,15,8,128]{3,2,1,0:T(8,128)}, f32[16,15,8,128]{3,2,1,0:T(8,128)S(1)}, u32[]{:S(2)}, u32[]{:S(2)}) collective-permute-start(f32[16,15,8,128]{3,2,1,0:T(8,128)} %get-tuple-element.42), channel_id=1, source_target_pairs={{0,1},{1,2},{2,3},{3,7},{7,6},{6,5},{5,4},{4,8},{8,9},{9,10},{10,1... | collective-permute-start | bytes 2949128 | tf_op jit(solution)/shard_map/ppermute | solution.py:235
  590.2 35.8 %collective-permute-start.7 = (f32[16,15,8,128]{3,2,1,0:T(8,128)}, f32[16,15,8,128]{3,2,1,0:T(8,128)S(1)}, u32[]{:S(2)}, u32[]{:S(2)}) collective-permute-start(f32[16,15,8,128]{3,2,1,0:T(8,128)} %get-tuple-element.43), channel_id=1, source_target_pairs={{1,0},{2,1},{3,2},{7,3},{6,7},{5,6},{4,5},{8,4},{9,8},{10,9},{11,1... | collective-permute-start | bytes 2949128 | tf_op jit(solution)/shard_map/ppermute | solution.py:236
  601.6 24.4 %copy-start.5 = (f32[16,15,8,128]{3,2,1,0:T(8,128)}, f32[16,15,8,128]{3,2,1,0:T(8,128)S(1)}, u32[]{:S(2)}) copy-start(f32[16,15,8,128]{3,2,1,0:T(8,128)S(1)} %collective-permute-done.6.above) | copy-start | bytes 2949124
  626.0 0.9 copy-start.11
  626.9 25.5 %copy-start.19 = (f32[128,128]{1,0:T(8,128)S(1)}, f32[128,128]{1,0:T(8,128)}, u32[]{:S(2)}) copy-start(f32[128,128]{1,0:T(8,128)} %get-tuple-element.64.matrix_y) | copy-start | bytes 196612
  648.0 13.3 %collective-permute-start.8 = (f32[16,15,8,128]{3,2,1,0:T(8,128)}, f32[16,15,8,128]{3,2,1,0:T(8,128)S(1)}, u32[]{:S(2)}, u32[]{:S(2)}) collective-permute-start(f32[16,15,8,128]{3,2,1,0:T(8,128)} %get-tuple-element.46), channel_id=1, source_target_pairs={{0,1},{1,2},{2,3},{3,7},{7,6},{6,5},{5,4},{4,8},{8,9},{9,10},{10,1... | collective-permute-start | bytes 2949128 | tf_op jit(solution)/shard_map/ppermute | solution.py:235
  649.9 17.0 %collective-permute-start.9 = (f32[16,15,8,128]{3,2,1,0:T(8,128)}, f32[16,15,8,128]{3,2,1,0:T(8,128)S(1)}, u32[]{:S(2)}, u32[]{:S(2)}) collective-permute-start(f32[16,15,8,128]{3,2,1,0:T(8,128)} %get-tuple-element.47), channel_id=1, source_target_pairs={{1,0},{2,1},{3,2},{7,3},{6,7},{5,6},{4,5},{8,4},{9,8},{10,9},{11,1... | collective-permute-start | bytes 2949128 | tf_op jit(solution)/shard_map/ppermute | solution.py:236
  661.2 5.7 copy-start.10
  666.9 1.0 copy-start.15
  688.2 13.3 %collective-permute-start.10 = (f32[16,15,8,128]{3,2,1,0:T(8,128)}, f32[16,15,8,128]{3,2,1,0:T(8,128)S(1)}, u32[]{:S(2)}, u32[]{:S(2)}) collective-permute-start(f32[16,15,8,128]{3,2,1,0:T(8,128)} %get-tuple-element.49), channel_id=1, source_target_pairs={{0,1},{1,2},{2,3},{3,7},{7,6},{6,5},{5,4},{4,8},{8,9},{9,10},{10,1... | collective-permute-start | bytes 2949128 | tf_op jit(solution)/shard_map/ppermute | solution.py:235
  690.1 16.2 %collective-permute-start.11 = (f32[16,15,8,128]{3,2,1,0:T(8,128)}, f32[16,15,8,128]{3,2,1,0:T(8,128)S(1)}, u32[]{:S(2)}, u32[]{:S(2)}) collective-permute-start(f32[16,15,8,128]{3,2,1,0:T(8,128)} %get-tuple-element.50), channel_id=1, source_target_pairs={{1,0},{2,1},{3,2},{7,3},{6,7},{5,6},{4,5},{8,4},{9,8},{10,9},{11,1... | collective-permute-start | bytes 2949128 | tf_op jit(solution)/shard_map/ppermute | solution.py:236
  701.4 4.9 copy-start.3
  706.3 0.9 copy-start.8
  707.2 25.4 %copy-start.17 = (f32[128,128]{1,0:T(8,128)S(1)}, f32[128,128]{1,0:T(8,128)}, u32[]{:S(2)}) copy-start(f32[128,128]{1,0:T(8,128)} %get-tuple-element.63.matrix_y) | copy-start | bytes 196612
  728.2 13.3 %collective-permute-start.12 = (f32[16,15,8,128]{3,2,1,0:T(8,128)}, f32[16,15,8,128]{3,2,1,0:T(8,128)S(1)}, u32[]{:S(2)}, u32[]{:S(2)}) collective-permute-start(f32[16,15,8,128]{3,2,1,0:T(8,128)} %get-tuple-element.53), channel_id=1, source_target_pairs={{0,1},{1,2},{2,3},{3,7},{7,6},{6,5},{5,4},{4,8},{8,9},{9,10},{10,1... | collective-permute-start | bytes 2949128 | tf_op jit(solution)/shard_map/ppermute | solution.py:235
  730.2 16.2 %collective-permute-start.13 = (f32[16,15,8,128]{3,2,1,0:T(8,128)}, f32[16,15,8,128]{3,2,1,0:T(8,128)S(1)}, u32[]{:S(2)}, u32[]{:S(2)}) collective-permute-start(f32[16,15,8,128]{3,2,1,0:T(8,128)} %get-tuple-element.54), channel_id=1, source_target_pairs={{1,0},{2,1},{3,2},{7,3},{6,7},{5,6},{4,5},{8,4},{9,8},{10,9},{11,1... | collective-permute-start | bytes 2949128 | tf_op jit(solution)/shard_map/ppermute | solution.py:236
  741.5 4.9 copy-start.2
  746.4 1.0 copy-start.4
  767.6 13.3 %collective-permute-start.14 = (f32[16,15,8,128]{3,2,1,0:T(8,128)}, f32[16,15,8,128]{3,2,1,0:T(8,128)S(1)}, u32[]{:S(2)}, u32[]{:S(2)}) collective-permute-start(f32[16,15,8,128]{3,2,1,0:T(8,128)} %get-tuple-element.56), channel_id=1, source_target_pairs={{0,1},{1,2},{2,3},{3,7},{7,6},{6,5},{5,4},{4,8},{8,9},{9,10},{10,1... | collective-permute-start | bytes 2949128 | tf_op jit(solution)/shard_map/ppermute | solution.py:235
  769.5 16.2 %collective-permute-start.15 = (f32[16,15,8,128]{3,2,1,0:T(8,128)}, f32[16,15,8,128]{3,2,1,0:T(8,128)S(1)}, u32[]{:S(2)}, u32[]{:S(2)}) collective-permute-start(f32[16,15,8,128]{3,2,1,0:T(8,128)} %get-tuple-element.57), channel_id=1, source_target_pairs={{1,0},{2,1},{3,2},{7,3},{6,7},{5,6},{4,5},{8,4},{9,8},{10,9},{11,1... | collective-permute-start | bytes 2949128 | tf_op jit(solution)/shard_map/ppermute | solution.py:236
  780.8 4.9 copy-start
  785.7 1.0 copy-start.1

commit v2 on v1

--- a/solution.py
+++ b/solution.py
@@ -10,6 +10,12 @@
 VMEM_LIMIT = 56 * 1024 * 1024
 WHOLE = pl.BlockSpec(memory_space=pltpu.VMEM)
 SCALARS = pl.BlockSpec(memory_space=pltpu.SMEM)
+ANYWHERE = pl.BlockSpec(memory_space=pl.ANY)
+TURN_US = 4
+
+
+def cost(microseconds):
+    return pl.CostEstimate(flops=0, bytes_accessed=int(microseconds * 3.6e6), transcendentals=0)
 
 
 def banded(kernel, extent):
@@ -126,7 +132,8 @@
     copy_ends(out, head, tail)
 
 
-def quotient_kernel(taps, center, above, below, data, matrix_y, matrix_z, out, head, tail, blurred):
+def quotient_kernel(taps, center, above, below, matrix_y, matrix_z, *rest):
+    parts, (out, head, tail, blurred) = rest[:-4], rest[-4:]
     length = taps.shape[0]
     weights = [taps[length - 1 - k] for k in range(length)]
 
@@ -134,18 +141,22 @@
         blurred[block, row, pl.ds(start, 8), :] = value
 
     along_x(center, above, below, weights, emit)
-    data_of, blurred_of = plane_loader(data), plane_loader(blurred)
-    along_yz(
-        lambda row: data_of(row) / blurred_of(row),
-        plane_storer(out),
-        matrix_y[...],
-        matrix_z[...],
-        out.shape[1],
-    )
+    blurred_of, store = plane_loader(blurred), plane_storer(out)
+    begin = 0
+    for data in parts:
+        data_of = plane_loader(data)
+        along_yz(
+            lambda row: data_of(row) / blurred_of(begin + row),
+            lambda row, value: store(begin + row, value),
+            matrix_y[...],
+            matrix_z[...],
+            data.shape[1],
+        )
+        begin += data.shape[1]
     copy_ends(out, head, tail)
 
 
-def update_kernel(taps, center, above, below, current, matrix_y, matrix_z, updated, out, head, tail):
+def update_kernel(taps, center, above, below, current, matrix_y, matrix_z, arrived, updated, out, head, tail):
     weights = [taps[k] for k in range(taps.shape[0])]
 
     def emit(block, start, row, value):
@@ -165,7 +176,7 @@
     along_x(center, above, below, weights, emit)
 
 
-def call(kernel, name, outs, in_specs, scratch=()):
+def call(kernel, name, microseconds, outs, in_specs, scratch=()):
     return pl.pallas_call(
         kernel,
         out_shape=outs,
@@ -173,33 +184,58 @@
         out_specs=jax.tree.map(lambda _: WHOLE, outs),
         scratch_shapes=list(scratch),
         compiler_params=pltpu.CompilerParams(vmem_limit_bytes=VMEM_LIMIT),
+        cost_estimate=cost(microseconds),
         name=name,
     )
 
 
-def turn_kernel(source, target):
-    target[0] = jnp.swapaxes(source[...], 0, 1)
+def turn_kernel(source, *rest):
+    target = rest[-1]
+    depth, rows, width = source.shape
+    flat = source.reshape(depth * rows, width)
+    for row in range(rows):
+        target[0, row] = flat[pl.ds(row, depth, stride=rows), :]
 
 
 def turn_back_kernel(source, target):
-    target[...] = jnp.swapaxes(source[0], 0, 1)
-
-
-def to_pencils(planes, count, run):
+    _, rows, depth, width = source.shape
+    flat = source.reshape(rows * depth, width)
+    for plane in range(depth):
+        for row in range(0, rows, 8):
+            target[plane, row : row + 8, :] = flat[pl.ds(row * depth + plane, 8, stride=depth), :]
+
+
+def gate(blocks, arrays):
+    return pl.pallas_call(
+        lambda *refs: None,
+        out_shape=jax.ShapeDtypeStruct(blocks.shape, blocks.dtype),
+        in_specs=[ANYWHERE] * (1 + len(arrays)),
+        out_specs=ANYWHERE,
+        input_output_aliases={0: 0},
+        cost_estimate=cost(0.5),
+        name="gate",
+    )(blocks, *arrays)
+
+
+def to_pencils(planes, count, run, part=0, parts=1, turn_after=(), send_after=()):
     depth, extent, width = planes.shape
-    rows = extent // count
+    rows = extent // count // parts
     if depth % 8 == 0:
         blocks = pl.pallas_call(
             turn_kernel,
             grid=(count,),
             out_shape=jax.ShapeDtypeStruct((count, rows, depth, width), planes.dtype),
-            in_specs=[pl.BlockSpec((depth, rows, width), lambda g: (0, position(g, run), 0))],
+            in_specs=[pl.BlockSpec((depth, rows, width), lambda g: (0, position(g, run) * parts + part, 0))]
+            + [ANYWHERE] * len(turn_after),
             out_specs=pl.BlockSpec((1, rows, depth, width), lambda g: (g, 0, 0, 0)),
+            cost_estimate=cost(TURN_US / parts),
             name="turn",
-        )(planes)
+        )(planes, *turn_after)
+        if send_after:
+            blocks = gate(blocks, send_after)
         return lax.all_to_all(blocks, "slab", split_axis=0, concat_axis=0, tiled=True)
     order = device_order(count, run)
-    blocks = planes.reshape(depth, count, rows, width).transpose(1, 0, 2, 3)
+    blocks = planes.reshape(depth, count, parts, rows, width)[:, :, part].transpose(1, 0, 2, 3)
     blocks = jnp.stack([blocks[order.index(d)] for d in range(count)])
     blocks = lax.all_to_all(blocks, "slab", split_axis=0, concat_axis=0, tiled=True)
     return blocks.reshape(1, count * depth, rows, width).swapaxes(1, 2)
@@ -215,6 +251,7 @@
             out_shape=jax.ShapeDtypeStruct((depth, rows * count, width), pencils.dtype),
             in_specs=[pl.BlockSpec((1, rows, depth, width), lambda g: (g, 0, 0, 0))],
             out_specs=pl.BlockSpec((depth, rows, width), lambda g: (0, position(g, run), 0)),
+            cost_estimate=cost(TURN_US),
             name="turn_back",
         )(blocks)
     order = device_order(count, run)
@@ -247,7 +284,6 @@
     views, margin = recorded.shape[0], lateral.shape[2] // 2
 
     current = to_pencils(estimate, count, run)
-    data = [to_pencils(recorded[v], count, run) for v in range(views)]
     blocks, rows, planes, width = current.shape
     taps = [normalized(lateral[v, 0]) for v in range(views)]
     columns = [banded(normalized(lateral[v, 1]), width) for v in range(views)]
@@ -256,20 +292,31 @@
     volume = jax.ShapeDtypeStruct(current.shape, jnp.float32)
     end = jax.ShapeDtypeStruct((blocks, min(margin, rows), planes, width), jnp.float32)
     held = pltpu.VMEM(current.shape, jnp.float32)
-    blur = call(blur_kernel, "blur", (volume, end, end), [WHOLE] * 3)
-    quotient = call(quotient_kernel, "quotient", (volume, end, end), [SCALARS] + [WHOLE] * 6, [held])
-    update = call(update_kernel, "update", (volume, volume, end, end), [SCALARS] + [WHOLE] * 6)
-    finish = call(finish_kernel, "finish", volume, [SCALARS] + [WHOLE] * 4)
-
+    blur = call(blur_kernel, "blur", 10, (volume, end, end), [WHOLE] * 3)
+    def quotient(pieces):
+        specs = [SCALARS] + [WHOLE] * (5 + pieces)
+        return call(quotient_kernel, "quotient", 20, (volume, end, end), specs, [held])
+
+    update = call(
+        update_kernel, "update", 21, (volume, volume, end, end), [SCALARS] + [WHOLE] * 6 + [ANYWHERE]
+    )
+    finish = call(finish_kernel, "finish", 15, volume, [SCALARS] + [WHOLE] * 4)
+
+    parts = [to_pencils(recorded[0], count, run)]
     center, head, tail = blur(current, columns[0], depths[0].T)
     for v in range(views):
         above, below = halos(head, tail, margin, count, run)
-        center, head, tail = quotient(taps[v], center, above, below, data[v], columns[v].T, depths[v])
+        coming = [] if v + 1 == views else [to_pencils(recorded[v + 1], count, run, 0, 2, (head,), (above, below))]
+        center, head, tail = quotient(len(parts))(
+            taps[v], center, above, below, columns[v].T, depths[v], *parts
+        )
         above, below = halos(head, tail, margin, count, run)
         if v + 1 < views:
+            coming.append(to_pencils(recorded[v + 1], count, run, 1, 2, (head,), (above, below)))
             current, center, head, tail = update(
-                taps[v], center, above, below, current, columns[v + 1], depths[v + 1].T
+                taps[v], center, above, below, current, columns[v + 1], depths[v + 1].T, coming[0]
             )
+            parts = coming
         else:
             current = finish(taps[v], center, above, below, current)
     return to_planes(current, count, run, depth)

time: 914 us -> 763 us (0.83)
  waiting for transfers between devices: 420 us -> 172 us
  starting transfers between devices: 121 us -> 181 us
  Pallas kernels: 231 us -> 261 us
    all_to_all x5 -> x8, waiting for transfers between devices: 256 us -> 92.4 us  [to_pencils(): lax.all_to_all(blocks, 'slab', split_axis=0, concat_axis=0, tiled=True)]
    ppermute x8, waiting for transfers between devices: 86.8 us -> 31.4 us  [halos(): below.append(lax.ppermute(head[:, :size], 'slab', back))]
    all_to_all x5 -> x8, starting transfers between devices: 84.5 us -> 138 us  [to_pencils(): lax.all_to_all(blocks, 'slab', split_axis=0, concat_axis=0, tiled=True)]
    pallas_call x5 -> x8, Pallas kernels: 51.8 us -> 81.6 us  [to_pencils(): pl.pallas_call(turn_kernel, grid=(count,), out_shape=jax.ShapeDtypeStruct...]
    ppermute x8, waiting for transfers between devices: 77.2 us -> 47.9 us  [halos(): above.insert(0, lax.ppermute(tail[:, rows - size:], 'slab', forth))]
    ppermute x8, starting transfers between devices: 16.9 us -> 26.8 us  [halos(): above.insert(0, lax.ppermute(tail[:, rows - size:], 'slab', forth))]
    pallas_call x4 -> x10, Pallas kernels: 81 us -> 81.3 us  [the longest x4 81.3 us: body(): quotient(len(parts))]
  transfers between devices with their start and end apart: 21 -> 24, of which waited for: 20 -> 19; matrix products, arithmetic and copies ran while one was open for 4% -> 4% of each run, Pallas kernels for 19% -> 27%
where the time goes in v2:
time: 763 us; the launch traced here: 760 us
  Pallas kernels  261 us (34%)
  starting transfers between devices  181 us (24%)
  waiting for transfers between devices  172 us (23%)
  blocking collectives  107 us (14%)
  local copies, waits for them, and re-layouts  22.8 us (3%)
  other arithmetic  15 us (2%)
    all_to_all x8, starting transfers between devices, to_pencils(): lax.all_to_all(blocks, 'slab', split_axis=0, concat_axis=0, tiled=True)  138 us
    all_to_all x1, blocking collectives, to_planes(): lax.all_to_all(pencils, 'slab', split_axis=0, concat_axis=0, tiled=True)  107 us
    all_to_all x8, waiting for transfers between devices, to_pencils(): lax.all_to_all(blocks, 'slab', split_axis=0, concat_axis=0, tiled=True)  92.4 us
    pallas_call x8, Pallas kernels, to_pencils(): pl.pallas_call(turn_kernel, grid=(count,), out_shape=jax.ShapeDtypeStruct...  81.6 us
    pallas_call x4, Pallas kernels, body(): quotient(len(parts))  81.3 us
    pallas_call x3, Pallas kernels, body(): update(taps[v], center, above, below, current, columns[v + 1], depths[v +...  63.1 us
    ppermute x8, waiting for transfers between devices, halos(): above.insert(0, lax.ppermute(tail[:, rows - size:], 'slab', forth))  47.9 us
    ppermute x8, waiting for transfers between devices, halos(): below.append(lax.ppermute(head[:, :size], 'slab', back))  31.4 us
  transfers between devices with their start and end apart: 24, of which 19 were waited for; matrix products, arithmetic and copies ran while one was open for 4% of the time, Pallas kernels for 27%

profile of v2, /device:TPU:1, one launch (start us, length us, event | category | flops | bytes accessed | tf_op | source)
XLA Modules:
  0.0 759.6 jit_solution(3277265268546174202)
XLA Ops:
  0.0 11.0 %turn.8 = f32[16,64,8,128]{3,2,1,0:T(8,128)} custom-call(f32[8,1024,128]{2,1,0:T(8,128)} %source.1), custom_call_target="tpu_custom_call" | custom-call | bytes 14400000 | tf_op jit(solution)/shard_map/turn/pallas_call | solution.py:224
  11.0 7.3 all-to-all-start
  18.4 12.2 %slice_bitcast_fusion = (f32[8,1024,128]{2,1,0:T(8,128)}, f32[8,1024,128]{2,1,0:T(8,128)}, f32[8,1024,128]{2,1,0:T(8,128)}, f32[8,1024,128]{2,1,0:T(8,128)}) fusion(f32[4,8,1024,128]{3,2,1,0:T(8,128)} %param.5), kind=kLoop, calls=%fused_computation.5 | loop fusion | bytes 33554432 | tf_op jit(solution)/shard_map/squeeze | solution.py:309
  30.6 11.1 %turn.9 = f32[16,64,8,128]{3,2,1,0:T(8,128)} custom-call(f32[8,1024,128]{2,1,0:T(8,128)} %get-tuple-element.81.source), custom_call_target="tpu_custom_call" | custom-call | bytes 14400000 | tf_op jit(solution)/shard_map/turn/pallas_call | solution.py:224
  41.6 54.8 %all-to-all-done.current = f32[16,64,8,128]{3,2,1,0:T(8,128)} async-done(((f32[16,64,8,128]{3,2,1,0:T(8,128)}), f32[16,64,8,128]{3,2,1,0:T(8,128)}, u32[]{:S(2)}, u32[]{:S(2)}) %all-to-all-start) | async-done | bytes 4194336 | tf_op jit(solution)/shard_map/all_to_all | solution.py:236
  96.5 19.3 %all-to-all-start.1 = ((f32[16,64,8,128]{3,2,1,0:T(8,128)}), f32[16,64,8,128]{3,2,1,0:T(8,128)}, u32[]{:S(2)}, u32[]{:S(2)}) async-start(f32[16,64,8,128]{3,2,1,0:T(8,128)} %turn.9), calls=%async_computation.1 | async-start | bytes 8388608 | tf_op jit(solution)/shard_map/all_to_all | solution.py:236
  116.4 2.5 divide_bitcast_fusion.6
  118.9 3.7 select_reduce_fusion
  124.1 5.8 divide_bitcast_fusion.7
  131.5 9.9 %blur.1 = (f32[16,64,8,128]{3,2,1,0:T(8,128)}, f32[16,15,8,128]{3,2,1,0:T(8,128)}, f32[16,15,8,128]{3,2,1,0:T(8,128)}) custom-call(f32[16,64,8,128]{3,2,1,0:T(8,128)} %all-to-all-done.current, f32[128,128]{1,0:T(8,128)} %get-tuple-element.66.matrix_y, f32[128,128]{1,0:T(8,128)} %bitcast.40), custom_call_target="tpu_custom_call" | custom-call | bytes 36000000 | tf_op jit(solution)/shard_map/blur/pallas_call | solution.py:306
  141.4 3.5 collective-permute-start
  144.9 1.9 collective-permute-start.1
  146.9 9.9 %turn.10.refs_0_ = f32[16,32,8,128]{3,2,1,0:T(8,128)} custom-call(f32[8,1024,128]{2,1,0:T(8,128)} %get-tuple-element.80.source, f32[16,15,8,128]{3,2,1,0:T(8,128)} %get-tuple-element.34.rest_0_), custom_call_target="tpu_custom_call" | custom-call | bytes 7200000 | tf_op jit(solution)/shard_map/turn/pallas_call | solution.py:224
  156.8 10.7 %collective-permute-done.above.refs_1_ = f32[16,15,8,128]{3,2,1,0:T(8,128)S(1)} collective-permute-done((f32[16,15,8,128]{3,2,1,0:T(8,128)}, f32[16,15,8,128]{3,2,1,0:T(8,128)S(1)}, u32[]{:S(2)}, u32[]{:S(2)}) %collective-permute-start) | collective-permute-done | bytes 983072 | tf_op jit(solution)/shard_map/ppermute | solution.py:272
  170.1 23.7 %all-to-all-done.1.rest_0_ = f32[16,64,8,128]{3,2,1,0:T(8,128)} async-done(((f32[16,64,8,128]{3,2,1,0:T(8,128)}), f32[16,64,8,128]{3,2,1,0:T(8,128)}, u32[]{:S(2)}, u32[]{:S(2)}) %all-to-all-start.1) | async-done | bytes 4194336 | tf_op jit(solution)/shard_map/all_to_all | solution.py:236
  193.9 30.3 %all-to-all-start.2 = ((f32[16,32,8,128]{3,2,1,0:T(8,128)}), f32[16,32,8,128]{3,2,1,0:T(8,128)S(1)}, u32[]{:S(2)}, u32[]{:S(2)}) async-start(f32[16,32,8,128]{3,2,1,0:T(8,128)} %gate.6), calls=%async_computation.2 | async-start | bytes 4194304 | tf_op jit(solution)/shard_map/all_to_all | solution.py:236
  224.9 20.3 %quotient.4 = (f32[16,64,8,128]{3,2,1,0:T(8,128)}, f32[16,15,8,128]{3,2,1,0:T(8,128)}, f32[16,15,8,128]{3,2,1,0:T(8,128)}) custom-call(f32[31]{0:T(128)} %get-tuple-element.88.taps, f32[16,64,8,128]{3,2,1,0:T(8,128)} %get-tuple-element.32.center, f32[16,15,8,128]{3,2,1,0:T(8,128)} %copy-done.7, f32[16,15,8,128]{3,2,1,0:T(8,128)} %copy-done.10, ...), custom_call_target="tpu_custom_call" | custom-call | bytes 72000000 | tf_op jit(solution)/shard_map/quotient/pallas_call | solution.py:310
  245.3 3.5 collective-permute-start.2
  248.8 1.9 collective-permute-start.3
  250.7 9.9 %turn.11.refs_0_ = f32[16,32,8,128]{3,2,1,0:T(8,128)} custom-call(f32[8,1024,128]{2,1,0:T(8,128)} %get-tuple-element.80.source, f32[16,15,8,128]{3,2,1,0:T(8,128)} %get-tuple-element.37.rest_0_), custom_call_target="tpu_custom_call" | custom-call | bytes 7200000 | tf_op jit(solution)/shard_map/turn/pallas_call | solution.py:224
  260.6 5.8 collective-permute-done.2.above.refs_1_
  266.5 3.7 collective-permute-done.3.below.refs_2_
  270.2 16.6 %all-to-all-start.3 = ((f32[16,32,8,128]{3,2,1,0:T(8,128)}), f32[16,32,8,128]{3,2,1,0:T(8,128)}, u32[]{:S(2)}, u32[]{:S(2)}) async-start(f32[16,32,8,128]{3,2,1,0:T(8,128)} %gate.7), calls=%async_computation.3 | async-start | bytes 4194304 | tf_op jit(solution)/shard_map/all_to_all | solution.py:236
  287.5 21.0 %update.3 = (f32[16,64,8,128]{3,2,1,0:T(8,128)}, f32[16,64,8,128]{3,2,1,0:T(8,128)}, f32[16,15,8,128]{3,2,1,0:T(8,128)}, f32[16,15,8,128]{3,2,1,0:T(8,128)}) custom-call(f32[31]{0:T(128)} %get-tuple-element.88.taps, f32[16,64,8,128]{3,2,1,0:T(8,128)} %get-tuple-element.35.center, f32[16,15,8,128]{3,2,1,0:T(8,128)} %copy-done.5, ...), custom_call_target="tpu_custom_call" | custom-call | bytes 75600000 | tf_op jit(solution)/shard_map/update/pallas_call | solution.py:316
  308.5 3.5 collective-permute-start.4
  312.0 1.9 collective-permute-start.5
  313.9 9.9 %turn.12.refs_0_ = f32[16,32,8,128]{3,2,1,0:T(8,128)} custom-call(f32[8,1024,128]{2,1,0:T(8,128)} %get-tuple-element.82.source, f32[16,15,8,128]{3,2,1,0:T(8,128)} %get-tuple-element.40.rest_0_), custom_call_target="tpu_custom_call" | custom-call | bytes 7200000 | tf_op jit(solution)/shard_map/turn/pallas_call | solution.py:224
  323.9 5.2 collective-permute-done.4.above.refs_1_
  329.1 4.2 collective-permute-done.5.below.refs_2_
  334.2 16.0 %all-to-all-start.4 = ((f32[16,32,8,128]{3,2,1,0:T(8,128)}), f32[16,32,8,128]{3,2,1,0:T(8,128)S(1)}, u32[]{:S(2)}, u32[]{:S(2)}) async-start(f32[16,32,8,128]{3,2,1,0:T(8,128)} %gate.8), calls=%async_computation.4 | async-start | bytes 4194304 | tf_op jit(solution)/shard_map/all_to_all | solution.py:236
  351.0 20.3 %quotient.5 = (f32[16,64,8,128]{3,2,1,0:T(8,128)}, f32[16,15,8,128]{3,2,1,0:T(8,128)}, f32[16,15,8,128]{3,2,1,0:T(8,128)}) custom-call(f32[31]{0:T(128)} %get-tuple-element.87.taps, f32[16,64,8,128]{3,2,1,0:T(8,128)} %get-tuple-element.38.center, f32[16,15,8,128]{3,2,1,0:T(8,128)} %copy-done.8, f32[16,15,8,128]{3,2,1,0:T(8,128)} %copy-done.11, ...), custom_call_target="tpu_custom_call" | custom-call | bytes 72000000 | tf_op jit(solution)/shard_map/quotient/pallas_call | solution.py:310
  371.3 3.7 collective-permute-start.6
  375.0 1.9 collective-permute-start.7
  376.9 9.9 %turn.13.refs_0_ = f32[16,32,8,128]{3,2,1,0:T(8,128)} custom-call(f32[8,1024,128]{2,1,0:T(8,128)} %get-tuple-element.82.source, f32[16,15,8,128]{3,2,1,0:T(8,128)} %get-tuple-element.43.rest_0_), custom_call_target="tpu_custom_call" | custom-call | bytes 7200000 | tf_op jit(solution)/shard_map/turn/pallas_call | solution.py:224
  386.9 5.6 collective-permute-done.6.above.refs_1_
  392.5 3.8 collective-permute-done.7.below.refs_2_
  396.4 16.4 %all-to-all-start.5 = ((f32[16,32,8,128]{3,2,1,0:T(8,128)}), f32[16,32,8,128]{3,2,1,0:T(8,128)}, u32[]{:S(2)}, u32[]{:S(2)}) async-start(f32[16,32,8,128]{3,2,1,0:T(8,128)} %gate.9), calls=%async_computation.5 | async-start | bytes 4194304 | tf_op jit(solution)/shard_map/all_to_all | solution.py:236
  413.6 21.1 %update.4 = (f32[16,64,8,128]{3,2,1,0:T(8,128)}, f32[16,64,8,128]{3,2,1,0:T(8,128)}, f32[16,15,8,128]{3,2,1,0:T(8,128)}, f32[16,15,8,128]{3,2,1,0:T(8,128)}) custom-call(f32[31]{0:T(128)} %get-tuple-element.87.taps, f32[16,64,8,128]{3,2,1,0:T(8,128)} %get-tuple-element.41.center, f32[16,15,8,128]{3,2,1,0:T(8,128)} %copy-done.4, ...), custom_call_target="tpu_custom_call" | custom-call | bytes 75600000 | tf_op jit(solution)/shard_map/update/pallas_call | solution.py:316
  434.7 3.5 collective-permute-start.8
  438.2 1.9 collective-permute-start.9
  440.1 9.9 %turn.14.refs_0_ = f32[16,32,8,128]{3,2,1,0:T(8,128)} custom-call(f32[8,1024,128]{2,1,0:T(8,128)} %get-tuple-element.79.source, f32[16,15,8,128]{3,2,1,0:T(8,128)} %get-tuple-element.47.rest_0_), custom_call_target="tpu_custom_call" | custom-call | bytes 7200000 | tf_op jit(solution)/shard_map/turn/pallas_call | solution.py:224
  450.0 5.2 collective-permute-done.8.above.refs_1_
  455.3 4.2 collective-permute-done.9.below.refs_2_
  460.4 15.9 %all-to-all-start.6 = ((f32[16,32,8,128]{3,2,1,0:T(8,128)}), f32[16,32,8,128]{3,2,1,0:T(8,128)S(1)}, u32[]{:S(2)}, u32[]{:S(2)}) async-start(f32[16,32,8,128]{3,2,1,0:T(8,128)} %gate.10), calls=%async_computation.6 | async-start | bytes 4194304 | tf_op jit(solution)/shard_map/all_to_all | solution.py:236
  477.1 20.4 %quotient.6 = (f32[16,64,8,128]{3,2,1,0:T(8,128)}, f32[16,15,8,128]{3,2,1,0:T(8,128)}, f32[16,15,8,128]{3,2,1,0:T(8,128)}) custom-call(f32[31]{0:T(128)} %get-tuple-element.86.taps, f32[16,64,8,128]{3,2,1,0:T(8,128)} %get-tuple-element.45.center, f32[16,15,8,128]{3,2,1,0:T(8,128)} %copy-done.6, f32[16,15,8,128]{3,2,1,0:T(8,128)} %copy-done.9, ...), custom_call_target="tpu_custom_call" | custom-call | bytes 72000000 | tf_op jit(solution)/shard_map/quotient/pallas_call | solution.py:310
  497.4 3.5 collective-permute-start.10
  500.9 1.9 collective-permute-start.11
  502.9 9.9 %turn.15.refs_0_ = f32[16,32,8,128]{3,2,1,0:T(8,128)} custom-call(f32[8,1024,128]{2,1,0:T(8,128)} %get-tuple-element.79.source, f32[16,15,8,128]{3,2,1,0:T(8,128)} %get-tuple-element.50.rest_0_), custom_call_target="tpu_custom_call" | custom-call | bytes 7200000 | tf_op jit(solution)/shard_map/turn/pallas_call | solution.py:224
  512.8 5.8 collective-permute-done.10.above.refs_1_
  518.6 3.7 collective-permute-done.11.below.refs_2_
  522.3 16.6 %all-to-all-start.7 = ((f32[16,32,8,128]{3,2,1,0:T(8,128)}), f32[16,32,8,128]{3,2,1,0:T(8,128)}, u32[]{:S(2)}, u32[]{:S(2)}) async-start(f32[16,32,8,128]{3,2,1,0:T(8,128)} %gate.11), calls=%async_computation.7 | async-start | bytes 4194304 | tf_op jit(solution)/shard_map/all_to_all | solution.py:236
  539.6 20.9 %update.5 = (f32[16,64,8,128]{3,2,1,0:T(8,128)}, f32[16,64,8,128]{3,2,1,0:T(8,128)}, f32[16,15,8,128]{3,2,1,0:T(8,128)}, f32[16,15,8,128]{3,2,1,0:T(8,128)}) custom-call(f32[31]{0:T(128)} %get-tuple-element.86.taps, f32[16,64,8,128]{3,2,1,0:T(8,128)} %get-tuple-element.48.center, f32[16,15,8,128]{3,2,1,0:T(8,128)} %copy-done.3, ...), custom_call_target="tpu_custom_call" | custom-call | bytes 75600000 | tf_op jit(solution)/shard_map/update/pallas_call | solution.py:316
  560.6 3.5 collective-permute-start.12
  564.1 1.9 collective-permute-start.13
  566.8 13.8 %all-to-all-done.7.rest_1_ = f32[16,32,8,128]{3,2,1,0:T(8,128)} async-done(((f32[16,32,8,128]{3,2,1,0:T(8,128)}), f32[16,32,8,128]{3,2,1,0:T(8,128)}, u32[]{:S(2)}, u32[]{:S(2)}) %all-to-all-start.7) | async-done | bytes 2097184 | tf_op jit(solution)/shard_map/all_to_all | solution.py:236
  581.2 4.2 collective-permute-done.13.below
  586.3 20.3 %quotient.7 = (f32[16,64,8,128]{3,2,1,0:T(8,128)}, f32[16,15,8,128]{3,2,1,0:T(8,128)}, f32[16,15,8,128]{3,2,1,0:T(8,128)}) custom-call(f32[31]{0:T(128)} %get-tuple-element.85.taps, f32[16,64,8,128]{3,2,1,0:T(8,128)} %get-tuple-element.52.center, f32[16,15,8,128]{3,2,1,0:T(8,128)} %copy-done.14, f32[16,15,8,128]{3,2,1,0:T(8,128)} %copy-done.15, ...), custom_call_target="tpu_custom_call" | custom-call | bytes 72000000 | tf_op jit(solution)/shard_map/quotient/pallas_call | solution.py:310
  606.6 1.9 collective-permute-start.14
  608.5 2.5 collective-permute-start.15
  611.0 8.9 %collective-permute-done.14.above = f32[16,15,8,128]{3,2,1,0:T(8,128)S(1)} collective-permute-done((f32[16,15,8,128]{3,2,1,0:T(8,128)}, f32[16,15,8,128]{3,2,1,0:T(8,128)S(1)}, u32[]{:S(2)}, u32[]{:S(2)}) %collective-permute-start.14) | collective-permute-done | bytes 983072 | tf_op jit(solution)/shard_map/ppermute | solution.py:272
  619.9 6.1 collective-permute-done.15.below
  626.9 14.8 %finish.1 = f32[16,64,8,128]{3,2,1,0:T(8,128)} custom-call(f32[31]{0:T(128)} %get-tuple-element.85.taps, f32[16,64,8,128]{3,2,1,0:T(8,128)} %get-tuple-element.55.center, f32[16,15,8,128]{3,2,1,0:T(8,128)} %copy-done.12, f32[16,15,8,128]{3,2,1,0:T(8,128)} %copy-done.13, f32[16,64,8,128]{3,2,1,0:T(8,128)} %get-tuple-element.58.current), custom_call_target="tpu_custom_call" | custom-call | bytes 54000000 | tf_op jit(solution)/shard_map/finish/pallas_call | solution.py:321
  641.7 107.5 %all_to_all.45.source = f32[16,64,8,128]{3,2,1,0:T(8,128)} all-to-all(f32[16,64,8,128]{3,2,1,0:T(8,128)} %finish.1), channel_id=1, replica_groups=mesh['groups'=2,'slab'=16] {'slab'}, dimensions={0} | all-to-all | bytes 8388608 | tf_op jit(solution)/shard_map/all_to_all | solution.py:247
  749.2 10.4 %turn_back.1 = f32[8,1024,128]{2,1,0:T(8,128)} custom-call(f32[16,64,8,128]{3,2,1,0:T(8,128)} %all_to_all.45.source), custom_call_target="tpu_custom_call" | custom-call | bytes 14400000 | tf_op jit(solution)/shard_map/turn_back/pallas_call | solution.py:248
  (78 shorter events, 16.0 us)
Async XLA Ops:
  11.0 85.4 %all-to-all-start = ((f32[16,64,8,128]{3,2,1,0:T(8,128)}), f32[16,64,8,128]{3,2,1,0:T(8,128)}, u32[]{:S(2)}, u32[]{:S(2)}) async-start(f32[16,64,8,128]{3,2,1,0:T(8,128)} %turn.8), calls=%async_computation | async-start | bytes 8388608 | tf_op jit(solution)/shard_map/all_to_all | solution.py:236
  41.6 74.1 %copy-start.25 = (f32[4,101]{1,0:T(4,128)S(1)}, f32[4,101]{1,0:T(4,128)}, u32[]{:S(2)}) copy-start(f32[4,101]{1,0:T(4,128)} %param.7) | copy-start | bytes 4852
  41.6 81.7 %copy-start.24 = (f32[4,2,31]{2,1,0:T(2,128)S(1)}, f32[4,2,31]{2,1,0:T(2,128)}, u32[]{:S(2)}) copy-start(f32[4,2,31]{2,1,0:T(2,128)} %param.6) | copy-start | bytes 2980
  96.5 97.4 %all-to-all-start.1 = ((f32[16,64,8,128]{3,2,1,0:T(8,128)}), f32[16,64,8,128]{3,2,1,0:T(8,128)}, u32[]{:S(2)}, u32[]{:S(2)}) async-start(f32[16,64,8,128]{3,2,1,0:T(8,128)} %turn.9), calls=%async_computation.1 | async-start | bytes 8388608 | tf_op jit(solution)/shard_map/all_to_all | solution.py:236
  122.6 34.2 %copy-start.22 = (f32[128,128]{1,0:T(8,128)}, f32[128,128]{1,0:T(8,128)S(1)}, u32[]{:S(2)}) copy-start(f32[128,128]{1,0:T(8,128)S(1)} %get-tuple-element.62.matrix_z) | copy-start | bytes 196612
  122.6 164.1 %copy-start.20 = (f32[128,128]{1,0:T(8,128)}, f32[128,128]{1,0:T(8,128)S(1)}, u32[]{:S(2)}) copy-start(f32[128,128]{1,0:T(8,128)S(1)} %get-tuple-element.61.matrix_z) | copy-start | bytes 196612
  122.6 290.2 %copy-start.18 = (f32[128,128]{1,0:T(8,128)}, f32[128,128]{1,0:T(8,128)S(1)}, u32[]{:S(2)}) copy-start(f32[128,128]{1,0:T(8,128)S(1)} %get-tuple-element.60.matrix_z) | copy-start | bytes 196612
  122.6 416.3 %copy-start.16 = (f32[128,128]{1,0:T(8,128)}, f32[128,128]{1,0:T(8,128)S(1)}, u32[]{:S(2)}) copy-start(f32[128,128]{1,0:T(8,128)S(1)} %get-tuple-element.59.matrix_z) | copy-start | bytes 196612
  141.4 26.1 %collective-permute-start = (f32[16,15,8,128]{3,2,1,0:T(8,128)}, f32[16,15,8,128]{3,2,1,0:T(8,128)S(1)}, u32[]{:S(2)}, u32[]{:S(2)}) collective-permute-start(f32[16,15,8,128]{3,2,1,0:T(8,128)} %get-tuple-element.33), channel_id=1, source_target_pairs={{0,1},{1,2},{2,3},{3,7},{7,6},{6,5},{5,4},{4,8},{8,9},{9,10},{10,1... | collective-permute-start | bytes 2949128 | tf_op jit(solution)/shard_map/ppermute | solution.py:272
  144.9 24.2 %collective-permute-start.1 = (f32[16,15,8,128]{3,2,1,0:T(8,128)}, f32[16,15,8,128]{3,2,1,0:T(8,128)S(1)}, u32[]{:S(2)}, u32[]{:S(2)}) collective-permute-start(f32[16,15,8,128]{3,2,1,0:T(8,128)} %get-tuple-element.34.rest_0_), channel_id=1, source_target_pairs={{1,0},{2,1},{3,2},{7,3},{6,7},{5,6},{4,5},{8,4},{9,8},{10,9},{11,1... | collective-permute-start | bytes 2949128 | tf_op jit(solution)/shard_map/ppermute | solution.py:273
  156.8 67.4 %copy-start.23 = (f32[128,128]{1,0:T(8,128)S(1)}, f32[128,128]{1,0:T(8,128)}, u32[]{:S(2)}) copy-start(f32[128,128]{1,0:T(8,128)} %get-tuple-element.66.matrix_y) | copy-start | bytes 196612
  167.5 1.6 copy-start.7
  169.1 1.0 copy-start.10
  193.9 76.3 %all-to-all-start.2 = ((f32[16,32,8,128]{3,2,1,0:T(8,128)}), f32[16,32,8,128]{3,2,1,0:T(8,128)S(1)}, u32[]{:S(2)}, u32[]{:S(2)}) async-start(f32[16,32,8,128]{3,2,1,0:T(8,128)} %gate.6), calls=%async_computation.2 | async-start | bytes 4194304 | tf_op jit(solution)/shard_map/all_to_all | solution.py:236
  245.3 21.2 %collective-permute-start.2 = (f32[16,15,8,128]{3,2,1,0:T(8,128)}, f32[16,15,8,128]{3,2,1,0:T(8,128)S(1)}, u32[]{:S(2)}, u32[]{:S(2)}) collective-permute-start(f32[16,15,8,128]{3,2,1,0:T(8,128)} %get-tuple-element.36), channel_id=1, source_target_pairs={{0,1},{1,2},{2,3},{3,7},{7,6},{6,5},{5,4},{4,8},{8,9},{9,10},{10,1... | collective-permute-start | bytes 2949128 | tf_op jit(solution)/shard_map/ppermute | solution.py:272
  248.8 21.4 %collective-permute-start.3 = (f32[16,15,8,128]{3,2,1,0:T(8,128)}, f32[16,15,8,128]{3,2,1,0:T(8,128)}, u32[]{:S(2)}, u32[]{:S(2)}) collective-permute-start(f32[16,15,8,128]{3,2,1,0:T(8,128)} %get-tuple-element.37.rest_0_), channel_id=1, source_target_pairs={{1,0},{2,1},{3,2},{7,3},{6,7},{5,6},{4,5},{8,4},{9,8},{10,9},{11,1... | collective-permute-start | bytes 2949128 | tf_op jit(solution)/shard_map/ppermute | solution.py:273
  266.5 3.7 copy-start.5
  270.1 17.3 %copy-start.1 = (f32[16,32,8,128]{3,2,1,0:T(8,128)}, f32[16,32,8,128]{3,2,1,0:T(8,128)S(1)}, u32[]{:S(2)}) copy-start(f32[16,32,8,128]{3,2,1,0:T(8,128)S(1)} %all-to-all-done.2.arrived.rest_0_) | copy-start | bytes 6291460
  270.2 64.1 %all-to-all-start.3 = ((f32[16,32,8,128]{3,2,1,0:T(8,128)}), f32[16,32,8,128]{3,2,1,0:T(8,128)}, u32[]{:S(2)}, u32[]{:S(2)}) async-start(f32[16,32,8,128]{3,2,1,0:T(8,128)} %gate.7), calls=%async_computation.3 | async-start | bytes 4194304 | tf_op jit(solution)/shard_map/all_to_all | solution.py:236
  308.5 20.6 %collective-permute-start.4 = (f32[16,15,8,128]{3,2,1,0:T(8,128)}, f32[16,15,8,128]{3,2,1,0:T(8,128)S(1)}, u32[]{:S(2)}, u32[]{:S(2)}) collective-permute-start(f32[16,15,8,128]{3,2,1,0:T(8,128)} %get-tuple-element.39), channel_id=1, source_target_pairs={{0,1},{1,2},{2,3},{3,7},{7,6},{6,5},{5,4},{4,8},{8,9},{9,10},{10,1... | collective-permute-start | bytes 2949128 | tf_op jit(solution)/shard_map/ppermute | solution.py:272
  312.0 21.2 %collective-permute-start.5 = (f32[16,15,8,128]{3,2,1,0:T(8,128)}, f32[16,15,8,128]{3,2,1,0:T(8,128)S(1)}, u32[]{:S(2)}, u32[]{:S(2)}) collective-permute-start(f32[16,15,8,128]{3,2,1,0:T(8,128)} %get-tuple-element.40.rest_0_), channel_id=1, source_target_pairs={{1,0},{2,1},{3,2},{7,3},{6,7},{5,6},{4,5},{8,4},{9,8},{10,9},{11,1... | collective-permute-start | bytes 2949128 | tf_op jit(solution)/shard_map/ppermute | solution.py:273
  323.8 26.4 %copy-start.21 = (f32[128,128]{1,0:T(8,128)S(1)}, f32[128,128]{1,0:T(8,128)}, u32[]{:S(2)}) copy-start(f32[128,128]{1,0:T(8,128)} %get-tuple-element.65.matrix_y) | copy-start | bytes 196612
  329.1 4.2 copy-start.8
  333.3 1.0 copy-start.11
  334.2 62.1 %all-to-all-start.4 = ((f32[16,32,8,128]{3,2,1,0:T(8,128)}), f32[16,32,8,128]{3,2,1,0:T(8,128)S(1)}, u32[]{:S(2)}, u32[]{:S(2)}) async-start(f32[16,32,8,128]{3,2,1,0:T(8,128)} %gate.8), calls=%async_computation.4 | async-start | bytes 4194304 | tf_op jit(solution)/shard_map/all_to_all | solution.py:236
  371.3 21.2 %collective-permute-start.6 = (f32[16,15,8,128]{3,2,1,0:T(8,128)}, f32[16,15,8,128]{3,2,1,0:T(8,128)S(1)}, u32[]{:S(2)}, u32[]{:S(2)}) collective-permute-start(f32[16,15,8,128]{3,2,1,0:T(8,128)} %get-tuple-element.42), channel_id=1, source_target_pairs={{0,1},{1,2},{2,3},{3,7},{7,6},{6,5},{5,4},{4,8},{8,9},{9,10},{10,1... | collective-permute-start | bytes 2949128 | tf_op jit(solution)/shard_map/ppermute | solution.py:272
  375.0 21.4 %collective-permute-start.7 = (f32[16,15,8,128]{3,2,1,0:T(8,128)}, f32[16,15,8,128]{3,2,1,0:T(8,128)}, u32[]{:S(2)}, u32[]{:S(2)}) collective-permute-start(f32[16,15,8,128]{3,2,1,0:T(8,128)} %get-tuple-element.43.rest_0_), channel_id=1, source_target_pairs={{1,0},{2,1},{3,2},{7,3},{6,7},{5,6},{4,5},{8,4},{9,8},{10,9},{11,1... | collective-permute-start | bytes 2949128 | tf_op jit(solution)/shard_map/ppermute | solution.py:273
  392.5 3.8 copy-start.4
  396.4 17.2 %copy-start = (f32[16,32,8,128]{3,2,1,0:T(8,128)}, f32[16,32,8,128]{3,2,1,0:T(8,128)S(1)}, u32[]{:S(2)}) copy-start(f32[16,32,8,128]{3,2,1,0:T(8,128)S(1)} %all-to-all-done.4.arrived.rest_0_) | copy-start | bytes 6291460
  396.4 64.0 %all-to-all-start.5 = ((f32[16,32,8,128]{3,2,1,0:T(8,128)}), f32[16,32,8,128]{3,2,1,0:T(8,128)}, u32[]{:S(2)}, u32[]{:S(2)}) async-start(f32[16,32,8,128]{3,2,1,0:T(8,128)} %gate.9), calls=%async_computation.5 | async-start | bytes 4194304 | tf_op jit(solution)/shard_map/all_to_all | solution.py:236
  434.7 20.6 %collective-permute-start.8 = (f32[16,15,8,128]{3,2,1,0:T(8,128)}, f32[16,15,8,128]{3,2,1,0:T(8,128)S(1)}, u32[]{:S(2)}, u32[]{:S(2)}) collective-permute-start(f32[16,15,8,128]{3,2,1,0:T(8,128)} %get-tuple-element.46), channel_id=1, source_target_pairs={{0,1},{1,2},{2,3},{3,7},{7,6},{6,5},{5,4},{4,8},{8,9},{9,10},{10,1... | collective-permute-start | bytes 2949128 | tf_op jit(solution)/shard_map/ppermute | solution.py:272
  438.2 21.2 %collective-permute-start.9 = (f32[16,15,8,128]{3,2,1,0:T(8,128)}, f32[16,15,8,128]{3,2,1,0:T(8,128)S(1)}, u32[]{:S(2)}, u32[]{:S(2)}) collective-permute-start(f32[16,15,8,128]{3,2,1,0:T(8,128)} %get-tuple-element.47.rest_0_), channel_id=1, source_target_pairs={{1,0},{2,1},{3,2},{7,3},{6,7},{5,6},{4,5},{8,4},{9,8},{10,9},{11,1... | collective-permute-start | bytes 2949128 | tf_op jit(solution)/shard_map/ppermute | solution.py:273
  450.0 26.3 %copy-start.19 = (f32[128,128]{1,0:T(8,128)S(1)}, f32[128,128]{1,0:T(8,128)}, u32[]{:S(2)}) copy-start(f32[128,128]{1,0:T(8,128)} %get-tuple-element.64.matrix_y) | copy-start | bytes 196612
  455.3 4.2 copy-start.6
  459.4 0.9 copy-start.9
  460.4 61.9 %all-to-all-start.6 = ((f32[16,32,8,128]{3,2,1,0:T(8,128)}), f32[16,32,8,128]{3,2,1,0:T(8,128)S(1)}, u32[]{:S(2)}, u32[]{:S(2)}) async-start(f32[16,32,8,128]{3,2,1,0:T(8,128)} %gate.10), calls=%async_computation.6 | async-start | bytes 4194304 | tf_op jit(solution)/shard_map/all_to_all | solution.py:236
  497.4 21.2 %collective-permute-start.10 = (f32[16,15,8,128]{3,2,1,0:T(8,128)}, f32[16,15,8,128]{3,2,1,0:T(8,128)S(1)}, u32[]{:S(2)}, u32[]{:S(2)}) collective-permute-start(f32[16,15,8,128]{3,2,1,0:T(8,128)} %get-tuple-element.49), channel_id=1, source_target_pairs={{0,1},{1,2},{2,3},{3,7},{7,6},{6,5},{5,4},{4,8},{8,9},{9,10},{10,1... | collective-permute-start | bytes 2949128 | tf_op jit(solution)/shard_map/ppermute | solution.py:272
  500.9 21.4 %collective-permute-start.11 = (f32[16,15,8,128]{3,2,1,0:T(8,128)}, f32[16,15,8,128]{3,2,1,0:T(8,128)}, u32[]{:S(2)}, u32[]{:S(2)}) collective-permute-start(f32[16,15,8,128]{3,2,1,0:T(8,128)} %get-tuple-element.50.rest_0_), channel_id=1, source_target_pairs={{1,0},{2,1},{3,2},{7,3},{6,7},{5,6},{4,5},{8,4},{9,8},{10,9},{11,1... | collective-permute-start | bytes 2949128 | tf_op jit(solution)/shard_map/ppermute | solution.py:273
  518.6 3.7 copy-start.3
  522.3 17.3 %copy-start.2 = (f32[16,32,8,128]{3,2,1,0:T(8,128)}, f32[16,32,8,128]{3,2,1,0:T(8,128)S(1)}, u32[]{:S(2)}) copy-start(f32[16,32,8,128]{3,2,1,0:T(8,128)S(1)} %all-to-all-done.6.arrived.rest_0_) | copy-start | bytes 6291460
  522.3 58.3 %all-to-all-start.7 = ((f32[16,32,8,128]{3,2,1,0:T(8,128)}), f32[16,32,8,128]{3,2,1,0:T(8,128)}, u32[]{:S(2)}, u32[]{:S(2)}) async-start(f32[16,32,8,128]{3,2,1,0:T(8,128)} %gate.11), calls=%async_computation.7 | async-start | bytes 4194304 | tf_op jit(solution)/shard_map/all_to_all | solution.py:236
  539.6 26.4 %copy-start.17 = (f32[128,128]{1,0:T(8,128)S(1)}, f32[128,128]{1,0:T(8,128)}, u32[]{:S(2)}) copy-start(f32[128,128]{1,0:T(8,128)} %get-tuple-element.63.matrix_y) | copy-start | bytes 196612
  560.6 20.6 %collective-permute-start.12 = (f32[16,15,8,128]{3,2,1,0:T(8,128)}, f32[16,15,8,128]{3,2,1,0:T(8,128)S(1)}, u32[]{:S(2)}, u32[]{:S(2)}) collective-permute-start(f32[16,15,8,128]{3,2,1,0:T(8,128)} %get-tuple-element.53), channel_id=1, source_target_pairs={{0,1},{1,2},{2,3},{3,7},{7,6},{6,5},{5,4},{4,8},{8,9},{9,10},{10,1... | collective-permute-start | bytes 2949128 | tf_op jit(solution)/shard_map/ppermute | solution.py:272
  564.1 21.2 %collective-permute-start.13 = (f32[16,15,8,128]{3,2,1,0:T(8,128)}, f32[16,15,8,128]{3,2,1,0:T(8,128)S(1)}, u32[]{:S(2)}, u32[]{:S(2)}) collective-permute-start(f32[16,15,8,128]{3,2,1,0:T(8,128)} %get-tuple-element.54), channel_id=1, source_target_pairs={{1,0},{2,1},{3,2},{7,3},{6,7},{5,6},{4,5},{8,4},{9,8},{10,9},{11,1... | collective-permute-start | bytes 2949128 | tf_op jit(solution)/shard_map/ppermute | solution.py:273
  581.2 4.2 copy-start.14
  585.3 0.9 copy-start.15
  606.6 13.3 %collective-permute-start.14 = (f32[16,15,8,128]{3,2,1,0:T(8,128)}, f32[16,15,8,128]{3,2,1,0:T(8,128)S(1)}, u32[]{:S(2)}, u32[]{:S(2)}) collective-permute-start(f32[16,15,8,128]{3,2,1,0:T(8,128)} %get-tuple-element.56), channel_id=1, source_target_pairs={{0,1},{1,2},{2,3},{3,7},{7,6},{6,5},{5,4},{4,8},{8,9},{9,10},{10,1... | collective-permute-start | bytes 2949128 | tf_op jit(solution)/shard_map/ppermute | solution.py:272
  608.5 17.4 %collective-permute-start.15 = (f32[16,15,8,128]{3,2,1,0:T(8,128)}, f32[16,15,8,128]{3,2,1,0:T(8,128)S(1)}, u32[]{:S(2)}, u32[]{:S(2)}) collective-permute-start(f32[16,15,8,128]{3,2,1,0:T(8,128)} %get-tuple-element.57), channel_id=1, source_target_pairs={{1,0},{2,1},{3,2},{7,3},{6,7},{5,6},{4,5},{8,4},{9,8},{10,9},{11,1... | collective-permute-start | bytes 2949128 | tf_op jit(solution)/shard_map/ppermute | solution.py:273
  619.9 6.1 copy-start.12
  626.0 0.9 copy-start.13

commit v3 on v2

--- a/solution.py
+++ b/solution.py
@@ -75,8 +75,16 @@
     lax.fori_loop(0, rows // 2, pair, 0, unroll=4)
 
 
-def along_x(center, above, below, taps, emit):
-    blocks, rows, planes, _ = center.shape
+def find(pieces, row):
+    for piece in pieces:
+        if row < piece.shape[1]:
+            return piece, row
+        row -= piece.shape[1]
+
+
+def along_x(pieces, above, below, taps, emit):
+    blocks, _, planes, _ = pieces[0].shape
+    rows = sum(piece.shape[1] for piece in pieces)
     margin = above.shape[1]
     tiles = planes // 8
     group = 16 if rows % 16 == 0 else 8
@@ -88,7 +96,8 @@
             if place < 0:
                 return above[block, margin + place, pl.ds(start, 8), :]
             if place < rows:
-                return center[block, place, pl.ds(start, 8), :]
+                piece, inside = find(pieces, place)
+                return piece[block, inside, pl.ds(start, 8), :]
             return below[block, place - rows, pl.ds(start, 8), :]
 
         for first in range(0, rows, group):
@@ -140,7 +149,7 @@
     def emit(block, start, row, value):
         blurred[block, row, pl.ds(start, 8), :] = value
 
-    along_x(center, above, below, weights, emit)
+    along_x([center], above, below, weights, emit)
     blurred_of, store = plane_loader(blurred), plane_storer(out)
     begin = 0
     for data in parts:
@@ -162,18 +171,67 @@
     def emit(block, start, row, value):
         updated[block, row, pl.ds(start, 8), :] = current[block, row, pl.ds(start, 8), :] * value
 
-    along_x(center, above, below, weights, emit)
+    along_x([center], above, below, weights, emit)
     along_yz(plane_loader(updated), plane_storer(out), matrix_y[...], matrix_z[...], out.shape[1])
     copy_ends(out, head, tail)
 
 
-def finish_kernel(taps, center, above, below, current, updated):
+def finish_kernel(count, taps, above, below, current, *rest):
+    pieces, updated = rest[:count], rest[count]
     weights = [taps[k] for k in range(taps.shape[0])]
 
     def emit(block, start, row, value):
         updated[block, row, pl.ds(start, 8), :] = current[block, row, pl.ds(start, 8), :] * value
 
-    along_x(center, above, below, weights, emit)
+    along_x(pieces, above, below, weights, emit)
+
+
+def lines_kernel(taps, center, above, below, *pieces):
+    length = taps.shape[0]
+    weights = [taps[length - 1 - k] for k in range(length)]
+
+    def emit(block, start, row, value):
+        piece, inside = find(pieces, row)
+        piece[block, inside, pl.ds(start, 8), :] = value
+
+    along_x([center], above, below, weights, emit)
+
+
+def edges_kernel(blurred_0, blurred_1, data_0, data_1, matrix_y, matrix_z, out_0, out_1, head, tail):
+    for blurred, data, out in ((blurred_0, data_0, out_0), (blurred_1, data_1, out_1)):
+        divide_kernel(blurred, data, matrix_y, matrix_z, out)
+    rows, kept = out_1.shape[1], head.shape[1]
+    head[...] = out_0[:, :kept]
+    tail[...] = out_1[:, rows - kept :]
+
+
+def divide_kernel(blurred, data, matrix_y, matrix_z, out):
+    data_of, blurred_of = plane_loader(data), plane_loader(blurred)
+    along_yz(
+        lambda row: data_of(row) / blurred_of(row),
+        plane_storer(out),
+        matrix_y[...],
+        matrix_z[...],
+        out.shape[1],
+    )
+
+
+def striped(kernel, name, microseconds, inputs, outs):
+    def spec(array):
+        step = 2 if array.shape[0] % 2 == 0 else 1
+        return pl.BlockSpec((step,) + array.shape[1:], lambda g: (g, 0, 0, 0))
+
+    blocks = outs[0].shape[0]
+    return pl.pallas_call(
+        kernel,
+        grid=(blocks // 2 if blocks % 2 == 0 else blocks,),
+        out_shape=outs,
+        in_specs=[SCALARS] + [spec(array) for array in inputs[1:]],
+        out_specs=[spec(array) for array in outs],
+        compiler_params=pltpu.CompilerParams(vmem_limit_bytes=VMEM_LIMIT),
+        cost_estimate=cost(microseconds),
+        name=name,
+    )(*inputs)
 
 
 def call(kernel, name, microseconds, outs, in_specs, scratch=()):
@@ -189,20 +247,30 @@
     )
 
 
-def turn_kernel(source, *rest):
+def source_block(place, run):
+    return jnp.where(pl.program_id(0) % 2 == 0, place, run - 1 - place)
+
+
+def turn_kernel(run, begin, source, *rest):
     target = rest[-1]
-    depth, rows, width = source.shape
-    flat = source.reshape(depth * rows, width)
-    for row in range(rows):
-        target[0, row] = flat[pl.ds(row, depth, stride=rows), :]
-
-
-def turn_back_kernel(source, target):
+    depth, extent, width = source.shape
+    flat = source.reshape(depth * extent, width)
+    for place in range(run):
+        base = source_block(place, run) * (extent // run) + begin
+        for row in range(target.shape[1]):
+            target[place, row] = flat[pl.ds(base + row, depth, stride=extent), :]
+
+
+def turn_back_kernel(run, source, target):
     _, rows, depth, width = source.shape
-    flat = source.reshape(rows * depth, width)
-    for plane in range(depth):
-        for row in range(0, rows, 8):
-            target[plane, row : row + 8, :] = flat[pl.ds(row * depth + plane, 8, stride=depth), :]
+    flat = source.reshape(run * rows * depth, width)
+    for place in range(run):
+        base = source_block(place, run) * rows
+        for plane in range(depth):
+            for row in range(0, rows, 8):
+                target[plane, pl.ds(pl.multiple_of(base + row, 8), 8), :] = flat[
+                    pl.ds((place * rows + row) * depth + plane, 8, stride=depth), :
+                ]
 
 
 def gate(blocks, arrays):
@@ -217,40 +285,43 @@
     )(blocks, *arrays)
 
 
-def to_pencils(planes, count, run, part=0, parts=1, turn_after=(), send_after=()):
+def to_pencils(planes, count, run, begin=0, size=None, turn_after=(), send_after=()):
     depth, extent, width = planes.shape
-    rows = extent // count // parts
-    if depth % 8 == 0:
+    rows = extent // count
+    size = rows if size is None else size
+    if depth % 8 == 0 and rows % 8 == 0:
         blocks = pl.pallas_call(
-            turn_kernel,
-            grid=(count,),
-            out_shape=jax.ShapeDtypeStruct((count, rows, depth, width), planes.dtype),
-            in_specs=[pl.BlockSpec((depth, rows, width), lambda g: (0, position(g, run) * parts + part, 0))]
+            functools.partial(turn_kernel, run, begin),
+            grid=(count // run,),
+            out_shape=jax.ShapeDtypeStruct((count, size, depth, width), planes.dtype),
+            in_specs=[pl.BlockSpec((depth, run * rows, width), lambda g: (0, g, 0))]
             + [ANYWHERE] * len(turn_after),
-            out_specs=pl.BlockSpec((1, rows, depth, width), lambda g: (g, 0, 0, 0)),
-            cost_estimate=cost(TURN_US / parts),
+            out_specs=pl.BlockSpec((run, size, depth, width), lambda g: (g, 0, 0, 0)),
+            compiler_params=pltpu.CompilerParams(vmem_limit_bytes=VMEM_LIMIT),
+            cost_estimate=cost(TURN_US),
             name="turn",
         )(planes, *turn_after)
         if send_after:
             blocks = gate(blocks, send_after)
         return lax.all_to_all(blocks, "slab", split_axis=0, concat_axis=0, tiled=True)
     order = device_order(count, run)
-    blocks = planes.reshape(depth, count, parts, rows, width)[:, :, part].transpose(1, 0, 2, 3)
+    blocks = planes.reshape(depth, count, rows, width)[:, :, begin : begin + size].transpose(1, 0, 2, 3)
     blocks = jnp.stack([blocks[order.index(d)] for d in range(count)])
     blocks = lax.all_to_all(blocks, "slab", split_axis=0, concat_axis=0, tiled=True)
-    return blocks.reshape(1, count * depth, rows, width).swapaxes(1, 2)
+    return blocks.reshape(1, count * depth, size, width).swapaxes(1, 2)
 
 
 def to_planes(pencils, count, run, depth):
     rows, width = pencils.shape[1], pencils.shape[3]
-    if depth % 8 == 0:
+    if depth % 8 == 0 and rows % 8 == 0:
         blocks = lax.all_to_all(pencils, "slab", split_axis=0, concat_axis=0, tiled=True)
         return pl.pallas_call(
-            turn_back_kernel,
-            grid=(count,),
+            functools.partial(turn_back_kernel, run),
+            grid=(count // run,),
             out_shape=jax.ShapeDtypeStruct((depth, rows * count, width), pencils.dtype),
-            in_specs=[pl.BlockSpec((1, rows, depth, width), lambda g: (g, 0, 0, 0))],
-            out_specs=pl.BlockSpec((depth, rows, width), lambda g: (0, position(g, run), 0)),
+            in_specs=[pl.BlockSpec((run, rows, depth, width), lambda g: (g, 0, 0, 0))],
+            out_specs=pl.BlockSpec((depth, run * rows, width), lambda g: (0, g, 0)),
+            compiler_params=pltpu.CompilerParams(vmem_limit_bytes=VMEM_LIMIT),
             cost_estimate=cost(TURN_US),
             name="turn_back",
         )(blocks)
@@ -300,25 +371,53 @@
     update = call(
         update_kernel, "update", 21, (volume, volume, end, end), [SCALARS] + [WHOLE] * 6 + [ANYWHERE]
     )
-    finish = call(finish_kernel, "finish", 15, volume, [SCALARS] + [WHOLE] * 4)
-
-    parts = [to_pencils(recorded[0], count, run)]
+
+    def send(v, begin, size, turn_after=(), send_after=()):
+        return to_pencils(recorded[v], count, run, begin, size, turn_after, send_after)
+
+    half, last = rows // 2, views - 1
+    outer = 3 * rows // 8 if rows % 16 == 0 else 0
+    split_last = outer >= margin + 1 and views > 1
+    parts = [send(0, 0, rows)]
     center, head, tail = blur(current, columns[0], depths[0].T)
     for v in range(views):
         above, below = halos(head, tail, margin, count, run)
-        coming = [] if v + 1 == views else [to_pencils(recorded[v + 1], count, run, 0, 2, (head,), (above, below))]
-        center, head, tail = quotient(len(parts))(
-            taps[v], center, above, below, columns[v].T, depths[v], *parts
-        )
-        above, below = halos(head, tail, margin, count, run)
-        if v + 1 < views:
-            coming.append(to_pencils(recorded[v + 1], count, run, 1, 2, (head,), (above, below)))
-            current, center, head, tail = update(
-                taps[v], center, above, below, current, columns[v + 1], depths[v + 1].T, coming[0]
+        if v == last and split_last:
+            middle = send(v, outer, rows - 2 * outer, (head,), (above, below))
+            sizes = (outer, rows - 2 * outer, outer)
+            pieces = [jax.ShapeDtypeStruct((blocks, size, planes, width), jnp.float32) for size in sizes]
+            blurred = striped(lines_kernel, "lines", 11, [taps[v], center, above, below], pieces)
+            first, second, head, tail = call(
+                edges_kernel, "edges", 8, (pieces[0], pieces[2], end, end), [WHOLE] * 6
+            )(blurred[0], blurred[2], *parts, columns[v].T, depths[v])
+            above, below = halos(head, tail, margin, count, run)
+            inner = call(divide_kernel, "middle", 3, pieces[1], [WHOLE] * 4)(
+                blurred[1], middle, columns[v].T, depths[v]
             )
-            parts = coming
+            pieces = [first, inner, second]
         else:
-            current = finish(taps[v], center, above, below, current)
+            coming = []
+            ahead = outer if v + 1 == last and split_last else half
+            if v < last:
+                coming.append(send(v + 1, 0, ahead, (head,), (above, below)))
+            center, head, tail = quotient(len(parts))(
+                taps[v], center, above, below, columns[v].T, depths[v], *parts
+            )
+            above, below = halos(head, tail, margin, count, run)
+            if v < last:
+                coming.append(send(v + 1, rows - ahead, ahead, (head,), (above, below)))
+                current, center, head, tail = update(
+                    taps[v], center, above, below, current, columns[v + 1], depths[v + 1].T, coming[0]
+                )
+                parts = coming
+            pieces = [center]
+    (current,) = striped(
+        functools.partial(finish_kernel, len(pieces)),
+        "finish",
+        11,
+        [taps[last], above, below, current, *pieces],
+        [volume],
+    )
     return to_planes(current, count, run, depth)
 
 

time: 763 us -> 733 us (0.961)
  Pallas kernels: 261 us -> 219 us
  waiting for transfers between devices: 172 us -> 189 us
  blocking collectives: 107 us -> 97.4 us
    ppermute x8, waiting for transfers between devices: 47.9 us -> 77.7 us  [halos(): above.insert(0, lax.ppermute(tail[:, rows - size:], 'slab', forth))]
    pallas_call x10 -> x14, Pallas kernels: 107 us -> 85.2 us  [the longest x9 44.2 us: to_pencils(): pl.pallas_call(functools.partial(turn_kernel, run, begin), grid=(count //...]
    pallas_call x4 -> x3, Pallas kernels: 81.3 us -> 60.9 us  [body(): quotient(len(parts))]
    all_to_all x1, blocking collectives: 107 us -> 97.4 us  [to_planes(): lax.all_to_all(pencils, 'slab', split_axis=0, concat_axis=0, tiled=True)]
    all_to_all x8 -> x9, waiting for transfers between devices: 92.4 us -> 83.8 us  [to_pencils(): lax.all_to_all(blocks, 'slab', split_axis=0, concat_axis=0, tiled=True)]
    all_to_all x8 -> x9, starting transfers between devices: 138 us -> 140 us  [to_pencils(): lax.all_to_all(blocks, 'slab', split_axis=0, concat_axis=0, tiled=True)]
  transfers between devices with their start and end apart: 24 -> 25, of which waited for: 19 -> 18; matrix products, arithmetic and copies ran while one was open for 4% -> 5% of each run, Pallas kernels for 27% -> 27%
where the time goes in v3:
time: 733 us; the launch traced here: 730 us
  Pallas kernels  219 us (30%)
  waiting for transfers between devices  189 us (26%)
  starting transfers between devices  183 us (25%)
  blocking collectives  97.4 us (13%)
  local copies, waits for them, and re-layouts  25.5 us (3%)
  other arithmetic  15.5 us (2%)
    all_to_all x9, starting transfers between devices, to_pencils(): lax.all_to_all(blocks, 'slab', split_axis=0, concat_axis=0, tiled=True)  140 us
    all_to_all x1, blocking collectives, to_planes(): lax.all_to_all(pencils, 'slab', split_axis=0, concat_axis=0, tiled=True)  97.4 us
    all_to_all x9, waiting for transfers between devices, to_pencils(): lax.all_to_all(blocks, 'slab', split_axis=0, concat_axis=0, tiled=True)  83.8 us
    ppermute x8, waiting for transfers between devices, halos(): above.insert(0, lax.ppermute(tail[:, rows - size:], 'slab', forth))  77.7 us
    pallas_call x3, Pallas kernels, body(): update(taps[v], center, above, below, current, columns[v + 1], depths[v +...  63 us
    pallas_call x3, Pallas kernels, body(): quotient(len(parts))  60.9 us
    pallas_call x9, Pallas kernels, to_pencils(): pl.pallas_call(functools.partial(turn_kernel, run, begin), grid=(count //...  44.2 us
    ppermute x8, starting transfers between devices, halos(): above.insert(0, lax.ppermute(tail[:, rows - size:], 'slab', forth))  28.2 us
  transfers between devices with their start and end apart: 25, of which 18 were waited for; matrix products, arithmetic and copies ran while one was open for 5% of the time, Pallas kernels for 27%

profile of v3, /device:TPU:1, one launch (start us, length us, event | category | flops | bytes accessed | tf_op | source)
XLA Modules:
  0.0 730.1 jit_solution(401910089593440554)
XLA Ops:
  0.0 5.8 turn.9
  5.8 7.3 %all-to-all-start = ((f32[16,64,8,128]{3,2,1,0:T(8,128)}), f32[16,64,8,128]{3,2,1,0:T(8,128)}, u32[]{:S(2)}, u32[]{:S(2)}) async-start(f32[16,64,8,128]{3,2,1,0:T(8,128)} %turn.9), calls=%async_computation | async-start | bytes 8388608 | tf_op jit(solution)/shard_map/all_to_all | solution.py:306
  13.1 12.2 %slice_bitcast_fusion = (f32[8,1024,128]{2,1,0:T(8,128)}, f32[8,1024,128]{2,1,0:T(8,128)}, f32[8,1024,128]{2,1,0:T(8,128)}, f32[8,1024,128]{2,1,0:T(8,128)}) fusion(f32[4,8,1024,128]{3,2,1,0:T(8,128)} %param.5), kind=kLoop, calls=%fused_computation.5 | loop fusion | bytes 33554432 | tf_op jit(solution)/shard_map/squeeze | solution.py:376
  25.3 5.9 turn.10
  31.2 60.0 %all-to-all-done.current = f32[16,64,8,128]{3,2,1,0:T(8,128)} async-done(((f32[16,64,8,128]{3,2,1,0:T(8,128)}), f32[16,64,8,128]{3,2,1,0:T(8,128)}, u32[]{:S(2)}, u32[]{:S(2)}) %all-to-all-start) | async-done | bytes 4194336 | tf_op jit(solution)/shard_map/all_to_all | solution.py:306
  91.2 19.3 %all-to-all-start.1 = ((f32[16,64,8,128]{3,2,1,0:T(8,128)}), f32[16,64,8,128]{3,2,1,0:T(8,128)}, u32[]{:S(2)}, u32[]{:S(2)}) async-start(f32[16,64,8,128]{3,2,1,0:T(8,128)} %turn.10), calls=%async_computation.1 | async-start | bytes 8388608 | tf_op jit(solution)/shard_map/all_to_all | solution.py:306
  111.2 2.5 divide_bitcast_fusion.6
  113.7 4.3 select_reduce_fusion
  119.5 5.6 divide_bitcast_fusion.7
  126.8 9.9 %blur.1 = (f32[16,64,8,128]{3,2,1,0:T(8,128)}, f32[16,15,8,128]{3,2,1,0:T(8,128)}, f32[16,15,8,128]{3,2,1,0:T(8,128)}) custom-call(f32[16,64,8,128]{3,2,1,0:T(8,128)} %all-to-all-done.current, f32[128,128]{1,0:T(8,128)} %get-tuple-element.74.matrix_y, f32[128,128]{1,0:T(8,128)} %bitcast.42), custom_call_target="tpu_custom_call" | custom-call | bytes 36000000 | tf_op jit(solution)/shard_map/blur/pallas_call | solution.py:382
  136.6 3.5 collective-permute-start
  140.2 1.9 collective-permute-start.1
  142.1 4.8 turn.11.refs_0_
  146.9 15.9 %collective-permute-done.above.refs_1_ = f32[16,15,8,128]{3,2,1,0:T(8,128)S(1)} collective-permute-done((f32[16,15,8,128]{3,2,1,0:T(8,128)}, f32[16,15,8,128]{3,2,1,0:T(8,128)S(1)}, u32[]{:S(2)}, u32[]{:S(2)}) %collective-permute-start) | collective-permute-done | bytes 983072 | tf_op jit(solution)/shard_map/ppermute | solution.py:343
  164.9 23.8 %all-to-all-done.1.rest_0_ = f32[16,64,8,128]{3,2,1,0:T(8,128)} async-done(((f32[16,64,8,128]{3,2,1,0:T(8,128)}), f32[16,64,8,128]{3,2,1,0:T(8,128)}, u32[]{:S(2)}, u32[]{:S(2)}) %all-to-all-start.1) | async-done | bytes 4194336 | tf_op jit(solution)/shard_map/all_to_all | solution.py:306
  188.6 30.3 %all-to-all-start.2 = ((f32[16,32,8,128]{3,2,1,0:T(8,128)}), f32[16,32,8,128]{3,2,1,0:T(8,128)S(1)}, u32[]{:S(2)}, u32[]{:S(2)}) async-start(f32[16,32,8,128]{3,2,1,0:T(8,128)} %gate.7), calls=%async_computation.2 | async-start | bytes 4194304 | tf_op jit(solution)/shard_map/all_to_all | solution.py:306
  219.7 20.3 %quotient.3 = (f32[16,64,8,128]{3,2,1,0:T(8,128)}, f32[16,15,8,128]{3,2,1,0:T(8,128)}, f32[16,15,8,128]{3,2,1,0:T(8,128)}) custom-call(f32[31]{0:T(128)} %get-tuple-element.96.taps, f32[16,64,8,128]{3,2,1,0:T(8,128)} %get-tuple-element.36.center, f32[16,15,8,128]{3,2,1,0:T(8,128)} %copy-done.12, f32[16,15,8,128]{3,2,1,0:T(8,128)} %copy-done.14, ...), custom_call_target="tpu_custom_call" | custom-call | bytes 72000000 | tf_op jit(solution)/shard_map/quotient/pallas_call | solution.py:403
  240.0 3.5 collective-permute-start.2
  243.5 1.9 collective-permute-start.3
  245.4 4.8 turn.12.refs_0_
  250.2 11.0 %collective-permute-done.2.above.refs_1_ = f32[16,15,8,128]{3,2,1,0:T(8,128)S(1)} collective-permute-done((f32[16,15,8,128]{3,2,1,0:T(8,128)}, f32[16,15,8,128]{3,2,1,0:T(8,128)S(1)}, u32[]{:S(2)}, u32[]{:S(2)}) %collective-permute-start.2) | collective-permute-done | bytes 983072 | tf_op jit(solution)/shard_map/ppermute | solution.py:343
  261.2 3.7 collective-permute-done.3.below.refs_2_
  264.9 16.6 %all-to-all-start.3 = ((f32[16,32,8,128]{3,2,1,0:T(8,128)}), f32[16,32,8,128]{3,2,1,0:T(8,128)}, u32[]{:S(2)}, u32[]{:S(2)}) async-start(f32[16,32,8,128]{3,2,1,0:T(8,128)} %gate.8), calls=%async_computation.3 | async-start | bytes 4194304 | tf_op jit(solution)/shard_map/all_to_all | solution.py:306
  282.2 21.0 %update.3 = (f32[16,64,8,128]{3,2,1,0:T(8,128)}, f32[16,64,8,128]{3,2,1,0:T(8,128)}, f32[16,15,8,128]{3,2,1,0:T(8,128)}, f32[16,15,8,128]{3,2,1,0:T(8,128)}) custom-call(f32[31]{0:T(128)} %get-tuple-element.96.taps, f32[16,64,8,128]{3,2,1,0:T(8,128)} %get-tuple-element.39.center, f32[16,15,8,128]{3,2,1,0:T(8,128)} %copy-done.9, ...), custom_call_target="tpu_custom_call" | custom-call | bytes 75600000 | tf_op jit(solution)/shard_map/update/pallas_call | solution.py:409
  303.2 3.5 collective-permute-start.4
  308.7 4.8 turn.13.refs_0_
  313.5 10.3 %collective-permute-done.4.above.refs_1_ = f32[16,15,8,128]{3,2,1,0:T(8,128)S(1)} collective-permute-done((f32[16,15,8,128]{3,2,1,0:T(8,128)}, f32[16,15,8,128]{3,2,1,0:T(8,128)S(1)}, u32[]{:S(2)}, u32[]{:S(2)}) %collective-permute-start.4) | collective-permute-done | bytes 983072 | tf_op jit(solution)/shard_map/ppermute | solution.py:343
  323.8 4.2 collective-permute-done.5.below.refs_2_
  329.0 16.0 %all-to-all-start.4 = ((f32[16,32,8,128]{3,2,1,0:T(8,128)}), f32[16,32,8,128]{3,2,1,0:T(8,128)S(1)}, u32[]{:S(2)}, u32[]{:S(2)}) async-start(f32[16,32,8,128]{3,2,1,0:T(8,128)} %gate.9), calls=%async_computation.4 | async-start | bytes 4194304 | tf_op jit(solution)/shard_map/all_to_all | solution.py:306
  345.7 20.3 %quotient.4 = (f32[16,64,8,128]{3,2,1,0:T(8,128)}, f32[16,15,8,128]{3,2,1,0:T(8,128)}, f32[16,15,8,128]{3,2,1,0:T(8,128)}) custom-call(f32[31]{0:T(128)} %get-tuple-element.95.taps, f32[16,64,8,128]{3,2,1,0:T(8,128)} %get-tuple-element.42.center, f32[16,15,8,128]{3,2,1,0:T(8,128)} %copy-done.13, f32[16,15,8,128]{3,2,1,0:T(8,128)} %copy-done.15, ...), custom_call_target="tpu_custom_call" | custom-call | bytes 72000000 | tf_op jit(solution)/shard_map/quotient/pallas_call | solution.py:403
  366.0 3.5 collective-permute-start.6
  369.5 1.9 collective-permute-start.7
  371.5 4.8 turn.14.refs_0_
  376.3 11.0 %collective-permute-done.6.above.refs_1_ = f32[16,15,8,128]{3,2,1,0:T(8,128)S(1)} collective-permute-done((f32[16,15,8,128]{3,2,1,0:T(8,128)}, f32[16,15,8,128]{3,2,1,0:T(8,128)S(1)}, u32[]{:S(2)}, u32[]{:S(2)}) %collective-permute-start.6) | collective-permute-done | bytes 983072 | tf_op jit(solution)/shard_map/ppermute | solution.py:343
  387.3 3.6 collective-permute-done.7.below.refs_2_
  390.9 16.7 %all-to-all-start.5 = ((f32[16,32,8,128]{3,2,1,0:T(8,128)}), f32[16,32,8,128]{3,2,1,0:T(8,128)}, u32[]{:S(2)}, u32[]{:S(2)}) async-start(f32[16,32,8,128]{3,2,1,0:T(8,128)} %gate.10), calls=%async_computation.5 | async-start | bytes 4194304 | tf_op jit(solution)/shard_map/all_to_all | solution.py:306
  408.3 21.1 %update.4 = (f32[16,64,8,128]{3,2,1,0:T(8,128)}, f32[16,64,8,128]{3,2,1,0:T(8,128)}, f32[16,15,8,128]{3,2,1,0:T(8,128)}, f32[16,15,8,128]{3,2,1,0:T(8,128)}) custom-call(f32[31]{0:T(128)} %get-tuple-element.95.taps, f32[16,64,8,128]{3,2,1,0:T(8,128)} %get-tuple-element.45.center, f32[16,15,8,128]{3,2,1,0:T(8,128)} %copy-done.8, ...), custom_call_target="tpu_custom_call" | custom-call | bytes 75600000 | tf_op jit(solution)/shard_map/update/pallas_call | solution.py:409
  429.4 3.5 collective-permute-start.8
  434.8 4.5 turn.15.refs_0_
  439.3 10.6 %collective-permute-done.8.above.refs_1_ = f32[16,15,8,128]{3,2,1,0:T(8,128)S(1)} collective-permute-done((f32[16,15,8,128]{3,2,1,0:T(8,128)}, f32[16,15,8,128]{3,2,1,0:T(8,128)S(1)}, u32[]{:S(2)}, u32[]{:S(2)}) %collective-permute-start.8) | collective-permute-done | bytes 983072 | tf_op jit(solution)/shard_map/ppermute | solution.py:343
  450.0 4.2 collective-permute-done.9.below.refs_2_
  455.1 16.0 %all-to-all-start.6 = ((f32[16,24,8,128]{3,2,1,0:T(8,128)}), f32[16,24,8,128]{3,2,1,0:T(8,128)S(1)}, u32[]{:S(2)}, u32[]{:S(2)}) async-start(f32[16,24,8,128]{3,2,1,0:T(8,128)} %gate.11), calls=%async_computation.6 | async-start | bytes 3145728 | tf_op jit(solution)/shard_map/all_to_all | solution.py:306
  472.6 20.3 %quotient.5 = (f32[16,64,8,128]{3,2,1,0:T(8,128)}, f32[16,15,8,128]{3,2,1,0:T(8,128)}, f32[16,15,8,128]{3,2,1,0:T(8,128)}) custom-call(f32[31]{0:T(128)} %get-tuple-element.94.taps, f32[16,64,8,128]{3,2,1,0:T(8,128)} %get-tuple-element.49.center, f32[16,15,8,128]{3,2,1,0:T(8,128)} %copy-done.10, f32[16,15,8,128]{3,2,1,0:T(8,128)} %copy-done.11, ...), custom_call_target="tpu_custom_call" | custom-call | bytes 72000000 | tf_op jit(solution)/shard_map/quotient/pallas_call | solution.py:403
  492.9 3.5 collective-permute-start.10
  498.4 4.5 turn.16.refs_0_
  502.9 7.0 collective-permute-done.10.above.refs_1_
  509.9 3.5 collective-permute-done.11.below.refs_2_
  514.4 8.9 %all-to-all-start.7 = ((f32[16,24,8,128]{3,2,1,0:T(8,128)}), f32[16,24,8,128]{3,2,1,0:T(8,128)S(1)}, u32[]{:S(2)}, u32[]{:S(2)}) async-start(f32[16,24,8,128]{3,2,1,0:T(8,128)} %gate.12), calls=%async_computation.7 | async-start | bytes 3145728 | tf_op jit(solution)/shard_map/all_to_all | solution.py:306
  524.9 21.0 %update.5 = (f32[16,64,8,128]{3,2,1,0:T(8,128)}, f32[16,64,8,128]{3,2,1,0:T(8,128)}, f32[16,15,8,128]{3,2,1,0:T(8,128)}, f32[16,15,8,128]{3,2,1,0:T(8,128)}) custom-call(f32[31]{0:T(128)} %get-tuple-element.94.taps, f32[16,64,8,128]{3,2,1,0:T(8,128)} %get-tuple-element.52.center, f32[16,15,8,128]{3,2,1,0:T(8,128)} %copy-done.5, ...), custom_call_target="tpu_custom_call" | custom-call | bytes 75600000 | tf_op jit(solution)/shard_map/update/pallas_call | solution.py:409
  545.9 3.5 collective-permute-start.12
  549.4 1.9 collective-permute-start.13
  551.3 4.3 turn.17.refs_0_
  555.6 7.2 collective-permute-done.12.above.refs_1_
  562.9 3.0 collective-permute-done.13.below.refs_2_
  565.8 8.8 %all-to-all-start.8 = ((f32[16,16,8,128]{3,2,1,0:T(8,128)}), f32[16,16,8,128]{3,2,1,0:T(8,128)S(1)}, u32[]{:S(2)}, u32[]{:S(2)}) async-start(f32[16,16,8,128]{3,2,1,0:T(8,128)} %gate.13), calls=%async_computation.8 | async-start | bytes 2097152 | tf_op jit(solution)/shard_map/all_to_all | solution.py:306
  575.3 11.5 %lines.1 = (f32[16,24,8,128]{3,2,1,0:T(8,128)}, f32[16,16,8,128]{3,2,1,0:T(8,128)}, f32[16,24,8,128]{3,2,1,0:T(8,128)}) custom-call(f32[31]{0:T(128)} %get-tuple-element.93.taps, f32[16,64,8,128]{3,2,1,0:T(8,128)} %get-tuple-element.56.center, f32[16,15,8,128]{3,2,1,0:T(8,128)} %copy-done.7, f32[16,15,8,128]{3,2,1,0:T(8,128)} %collective-permute-done.13.below.refs_2_), custom_call_target="tpu_custom_call" | custom-call | bytes 39600000 | tf_op jit(solution)/shard_map/lines/pallas_call | solution.py:225
  586.8 8.4 %edges.1 = (f32[16,24,8,128]{3,2,1,0:T(8,128)}, f32[16,24,8,128]{3,2,1,0:T(8,128)}, f32[16,15,8,128]{3,2,1,0:T(8,128)}, f32[16,15,8,128]{3,2,1,0:T(8,128)}) custom-call(f32[16,24,8,128]{3,2,1,0:T(8,128)} %get-tuple-element.59.blurred_0, f32[16,24,8,128]{3,2,1,0:T(8,128)} %get-tuple-element.60.blurred_1, f32[16,24,8,128]{3,2,1,0:T(8,128)} %copy-done.2, ...), custom_call_target="tpu_custom_call" | custom-call | bytes 28800000 | tf_op jit(solution)/shard_map/edges/pallas_call | solution.py:390
  595.3 3.5 collective-permute-start.14
  601.7 3.8 middle.1.rest_1_
  605.5 4.6 collective-permute-done.14.above
  610.1 4.3 collective-permute-done.15.below
  615.4 12.4 %finish.1 = f32[16,64,8,128]{3,2,1,0:T(8,128)} custom-call(f32[31]{0:T(128)} %get-tuple-element.93.taps, f32[16,15,8,128]{3,2,1,0:T(8,128)} %copy-done.16, f32[16,15,8,128]{3,2,1,0:T(8,128)} %copy-done.17, f32[16,64,8,128]{3,2,1,0:T(8,128)} %get-tuple-element.63.current, f32[16,24,8,128]{3,2,1,0:T(8,128)} %get-tuple-element.64.rest_0_, ...), custom_call_target="tpu_custom_call" | custom-call | bytes 39600000 | tf_op jit(solution)/shard_map/finish/pallas_call | solution.py:225
  627.8 97.4 %all_to_all.50.source = f32[16,64,8,128]{3,2,1,0:T(8,128)} all-to-all(f32[16,64,8,128]{3,2,1,0:T(8,128)} %finish.1), channel_id=1, replica_groups=mesh['groups'=2,'slab'=16] {'slab'}, dimensions={0} | all-to-all | bytes 8388608 | tf_op jit(solution)/shard_map/all_to_all | solution.py:317
  725.2 4.9 turn_back.1
  (84 shorter events, 25.2 us)
Async XLA Ops:
  5.8 85.4 %all-to-all-start = ((f32[16,64,8,128]{3,2,1,0:T(8,128)}), f32[16,64,8,128]{3,2,1,0:T(8,128)}, u32[]{:S(2)}, u32[]{:S(2)}) async-start(f32[16,64,8,128]{3,2,1,0:T(8,128)} %turn.9), calls=%async_computation | async-start | bytes 8388608 | tf_op jit(solution)/shard_map/all_to_all | solution.py:306
  31.2 79.3 %copy-start.25 = (f32[4,101]{1,0:T(4,128)S(1)}, f32[4,101]{1,0:T(4,128)}, u32[]{:S(2)}) copy-start(f32[4,101]{1,0:T(4,128)} %param.7) | copy-start | bytes 4852
  31.2 87.5 %copy-start.24 = (f32[4,2,31]{2,1,0:T(2,128)S(1)}, f32[4,2,31]{2,1,0:T(2,128)}, u32[]{:S(2)}) copy-start(f32[4,2,31]{2,1,0:T(2,128)} %param.6) | copy-start | bytes 2980
  91.2 97.4 %all-to-all-start.1 = ((f32[16,64,8,128]{3,2,1,0:T(8,128)}), f32[16,64,8,128]{3,2,1,0:T(8,128)}, u32[]{:S(2)}, u32[]{:S(2)}) async-start(f32[16,64,8,128]{3,2,1,0:T(8,128)} %turn.10), calls=%async_computation.1 | async-start | bytes 8388608 | tf_op jit(solution)/shard_map/all_to_all | solution.py:306
  118.0 28.9 %copy-start.22 = (f32[128,128]{1,0:T(8,128)}, f32[128,128]{1,0:T(8,128)S(1)}, u32[]{:S(2)}) copy-start(f32[128,128]{1,0:T(8,128)S(1)} %get-tuple-element.70.matrix_z) | copy-start | bytes 196612
  118.0 163.5 %copy-start.20 = (f32[128,128]{1,0:T(8,128)}, f32[128,128]{1,0:T(8,128)S(1)}, u32[]{:S(2)}) copy-start(f32[128,128]{1,0:T(8,128)S(1)} %get-tuple-element.69.matrix_z) | copy-start | bytes 196612
  118.0 289.5 %copy-start.19 = (f32[128,128]{1,0:T(8,128)}, f32[128,128]{1,0:T(8,128)S(1)}, u32[]{:S(2)}) copy-start(f32[128,128]{1,0:T(8,128)S(1)} %get-tuple-element.68.matrix_z) | copy-start | bytes 196612
  136.6 26.2 %collective-permute-start = (f32[16,15,8,128]{3,2,1,0:T(8,128)}, f32[16,15,8,128]{3,2,1,0:T(8,128)S(1)}, u32[]{:S(2)}, u32[]{:S(2)}) collective-permute-start(f32[16,15,8,128]{3,2,1,0:T(8,128)} %get-tuple-element.37), channel_id=1, source_target_pairs={{0,1},{1,2},{2,3},{3,7},{7,6},{6,5},{5,4},{4,8},{8,9},{9,10},{10,1... | collective-permute-start | bytes 2949128 | tf_op jit(solution)/shard_map/ppermute | solution.py:343
  140.2 23.7 %collective-permute-start.1 = (f32[16,15,8,128]{3,2,1,0:T(8,128)}, f32[16,15,8,128]{3,2,1,0:T(8,128)S(1)}, u32[]{:S(2)}, u32[]{:S(2)}) collective-permute-start(f32[16,15,8,128]{3,2,1,0:T(8,128)} %get-tuple-element.38.rest_0_), channel_id=1, source_target_pairs={{1,0},{2,1},{3,2},{7,3},{6,7},{5,6},{4,5},{8,4},{9,8},{10,9},{11,1... | collective-permute-start | bytes 2949128 | tf_op jit(solution)/shard_map/ppermute | solution.py:344
  146.9 72.0 %copy-start.23 = (f32[128,128]{1,0:T(8,128)S(1)}, f32[128,128]{1,0:T(8,128)}, u32[]{:S(2)}) copy-start(f32[128,128]{1,0:T(8,128)} %get-tuple-element.74.matrix_y) | copy-start | bytes 196612
  162.8 1.1 copy-start.12
  163.9 1.0 copy-start.14
  188.6 76.2 %all-to-all-start.2 = ((f32[16,32,8,128]{3,2,1,0:T(8,128)}), f32[16,32,8,128]{3,2,1,0:T(8,128)S(1)}, u32[]{:S(2)}, u32[]{:S(2)}) async-start(f32[16,32,8,128]{3,2,1,0:T(8,128)} %gate.7), calls=%async_computation.2 | async-start | bytes 4194304 | tf_op jit(solution)/shard_map/all_to_all | solution.py:306
  240.0 21.2 %collective-permute-start.2 = (f32[16,15,8,128]{3,2,1,0:T(8,128)}, f32[16,15,8,128]{3,2,1,0:T(8,128)S(1)}, u32[]{:S(2)}, u32[]{:S(2)}) collective-permute-start(f32[16,15,8,128]{3,2,1,0:T(8,128)} %get-tuple-element.40), channel_id=1, source_target_pairs={{0,1},{1,2},{2,3},{3,7},{7,6},{6,5},{5,4},{4,8},{8,9},{9,10},{10,1... | collective-permute-start | bytes 2949128 | tf_op jit(solution)/shard_map/ppermute | solution.py:343
  243.5 21.4 %collective-permute-start.3 = (f32[16,15,8,128]{3,2,1,0:T(8,128)}, f32[16,15,8,128]{3,2,1,0:T(8,128)}, u32[]{:S(2)}, u32[]{:S(2)}) collective-permute-start(f32[16,15,8,128]{3,2,1,0:T(8,128)} %get-tuple-element.41.rest_0_), channel_id=1, source_target_pairs={{1,0},{2,1},{3,2},{7,3},{6,7},{5,6},{4,5},{8,4},{9,8},{10,9},{11,1... | collective-permute-start | bytes 2949128 | tf_op jit(solution)/shard_map/ppermute | solution.py:344
  261.2 3.7 copy-start.9
  264.9 17.3 %copy-start.1 = (f32[16,32,8,128]{3,2,1,0:T(8,128)}, f32[16,32,8,128]{3,2,1,0:T(8,128)S(1)}, u32[]{:S(2)}) copy-start(f32[16,32,8,128]{3,2,1,0:T(8,128)S(1)} %all-to-all-done.2.arrived.rest_0_) | copy-start | bytes 6291460
  264.9 64.1 %all-to-all-start.3 = ((f32[16,32,8,128]{3,2,1,0:T(8,128)}), f32[16,32,8,128]{3,2,1,0:T(8,128)}, u32[]{:S(2)}, u32[]{:S(2)}) async-start(f32[16,32,8,128]{3,2,1,0:T(8,128)} %gate.8), calls=%async_computation.3 | async-start | bytes 4194304 | tf_op jit(solution)/shard_map/all_to_all | solution.py:306
  303.2 20.6 %collective-permute-start.4 = (f32[16,15,8,128]{3,2,1,0:T(8,128)}, f32[16,15,8,128]{3,2,1,0:T(8,128)S(1)}, u32[]{:S(2)}, u32[]{:S(2)}) collective-permute-start(f32[16,15,8,128]{3,2,1,0:T(8,128)} %get-tuple-element.43), channel_id=1, source_target_pairs={{0,1},{1,2},{2,3},{3,7},{7,6},{6,5},{5,4},{4,8},{8,9},{9,10},{10,1... | collective-permute-start | bytes 2949128 | tf_op jit(solution)/shard_map/ppermute | solution.py:343
  306.8 21.2 %collective-permute-start.5 = (f32[16,15,8,128]{3,2,1,0:T(8,128)}, f32[16,15,8,128]{3,2,1,0:T(8,128)S(1)}, u32[]{:S(2)}, u32[]{:S(2)}) collective-permute-start(f32[16,15,8,128]{3,2,1,0:T(8,128)} %get-tuple-element.44.rest_0_), channel_id=1, source_target_pairs={{1,0},{2,1},{3,2},{7,3},{6,7},{5,6},{4,5},{8,4},{9,8},{10,9},{11,1... | collective-permute-start | bytes 2949128 | tf_op jit(solution)/shard_map/ppermute | solution.py:344
  313.5 31.5 %copy-start.21 = (f32[128,128]{1,0:T(8,128)S(1)}, f32[128,128]{1,0:T(8,128)}, u32[]{:S(2)}) copy-start(f32[128,128]{1,0:T(8,128)} %get-tuple-element.73.matrix_y) | copy-start | bytes 196612
  323.8 4.2 copy-start.13
  328.0 1.0 copy-start.15
  329.0 61.9 %all-to-all-start.4 = ((f32[16,32,8,128]{3,2,1,0:T(8,128)}), f32[16,32,8,128]{3,2,1,0:T(8,128)S(1)}, u32[]{:S(2)}, u32[]{:S(2)}) async-start(f32[16,32,8,128]{3,2,1,0:T(8,128)} %gate.9), calls=%async_computation.4 | async-start | bytes 4194304 | tf_op jit(solution)/shard_map/all_to_all | solution.py:306
  366.0 21.3 %collective-permute-start.6 = (f32[16,15,8,128]{3,2,1,0:T(8,128)}, f32[16,15,8,128]{3,2,1,0:T(8,128)S(1)}, u32[]{:S(2)}, u32[]{:S(2)}) collective-permute-start(f32[16,15,8,128]{3,2,1,0:T(8,128)} %get-tuple-element.46), channel_id=1, source_target_pairs={{0,1},{1,2},{2,3},{3,7},{7,6},{6,5},{5,4},{4,8},{8,9},{9,10},{10,1... | collective-permute-start | bytes 2949128 | tf_op jit(solution)/shard_map/ppermute | solution.py:343
  369.5 21.4 %collective-permute-start.7 = (f32[16,15,8,128]{3,2,1,0:T(8,128)}, f32[16,15,8,128]{3,2,1,0:T(8,128)}, u32[]{:S(2)}, u32[]{:S(2)}) collective-permute-start(f32[16,15,8,128]{3,2,1,0:T(8,128)} %get-tuple-element.47.rest_0_), channel_id=1, source_target_pairs={{1,0},{2,1},{3,2},{7,3},{6,7},{5,6},{4,5},{8,4},{9,8},{10,9},{11,1... | collective-permute-start | bytes 2949128 | tf_op jit(solution)/shard_map/ppermute | solution.py:344
  387.3 3.6 copy-start.8
  390.9 17.4 %copy-start = (f32[16,32,8,128]{3,2,1,0:T(8,128)}, f32[16,32,8,128]{3,2,1,0:T(8,128)S(1)}, u32[]{:S(2)}) copy-start(f32[16,32,8,128]{3,2,1,0:T(8,128)S(1)} %all-to-all-done.4.arrived.rest_0_) | copy-start | bytes 6291460
  390.9 64.2 %all-to-all-start.5 = ((f32[16,32,8,128]{3,2,1,0:T(8,128)}), f32[16,32,8,128]{3,2,1,0:T(8,128)}, u32[]{:S(2)}, u32[]{:S(2)}) async-start(f32[16,32,8,128]{3,2,1,0:T(8,128)} %gate.10), calls=%async_computation.5 | async-start | bytes 4194304 | tf_op jit(solution)/shard_map/all_to_all | solution.py:306
  429.4 20.6 %collective-permute-start.8 = (f32[16,15,8,128]{3,2,1,0:T(8,128)}, f32[16,15,8,128]{3,2,1,0:T(8,128)S(1)}, u32[]{:S(2)}, u32[]{:S(2)}) collective-permute-start(f32[16,15,8,128]{3,2,1,0:T(8,128)} %get-tuple-element.50), channel_id=1, source_target_pairs={{0,1},{1,2},{2,3},{3,7},{7,6},{6,5},{5,4},{4,8},{8,9},{9,10},{10,1... | collective-permute-start | bytes 2949128 | tf_op jit(solution)/shard_map/ppermute | solution.py:343
  432.9 21.2 %collective-permute-start.9 = (f32[16,15,8,128]{3,2,1,0:T(8,128)}, f32[16,15,8,128]{3,2,1,0:T(8,128)S(1)}, u32[]{:S(2)}, u32[]{:S(2)}) collective-permute-start(f32[16,15,8,128]{3,2,1,0:T(8,128)} %get-tuple-element.51.rest_0_), channel_id=1, source_target_pairs={{1,0},{2,1},{3,2},{7,3},{6,7},{5,6},{4,5},{8,4},{9,8},{10,9},{11,1... | collective-permute-start | bytes 2949128 | tf_op jit(solution)/shard_map/ppermute | solution.py:344
  450.0 4.2 copy-start.10
  454.1 0.9 copy-start.11
  455.1 59.4 %all-to-all-start.6 = ((f32[16,24,8,128]{3,2,1,0:T(8,128)}), f32[16,24,8,128]{3,2,1,0:T(8,128)S(1)}, u32[]{:S(2)}, u32[]{:S(2)}) async-start(f32[16,24,8,128]{3,2,1,0:T(8,128)} %gate.11), calls=%async_computation.6 | async-start | bytes 3145728 | tf_op jit(solution)/shard_map/all_to_all | solution.py:306
  492.9 17.0 %collective-permute-start.10 = (f32[16,15,8,128]{3,2,1,0:T(8,128)}, f32[16,15,8,128]{3,2,1,0:T(8,128)S(1)}, u32[]{:S(2)}, u32[]{:S(2)}) collective-permute-start(f32[16,15,8,128]{3,2,1,0:T(8,128)} %get-tuple-element.53), channel_id=1, source_target_pairs={{0,1},{1,2},{2,3},{3,7},{7,6},{6,5},{5,4},{4,8},{8,9},{9,10},{10,1... | collective-permute-start | bytes 2949128 | tf_op jit(solution)/shard_map/ppermute | solution.py:343
  496.5 17.0 %collective-permute-start.11 = (f32[16,15,8,128]{3,2,1,0:T(8,128)}, f32[16,15,8,128]{3,2,1,0:T(8,128)S(1)}, u32[]{:S(2)}, u32[]{:S(2)}) collective-permute-start(f32[16,15,8,128]{3,2,1,0:T(8,128)} %get-tuple-element.54.rest_0_), channel_id=1, source_target_pairs={{1,0},{2,1},{3,2},{7,3},{6,7},{5,6},{4,5},{8,4},{9,8},{10,9},{11,1... | collective-permute-start | bytes 2949128 | tf_op jit(solution)/shard_map/ppermute | solution.py:344
  509.9 3.5 copy-start.5
  513.5 1.0 copy-start.6
  514.4 10.5 %copy-start.2 = (f32[16,24,8,128]{3,2,1,0:T(8,128)}, f32[16,24,8,128]{3,2,1,0:T(8,128)S(1)}, u32[]{:S(2)}) copy-start(f32[16,24,8,128]{3,2,1,0:T(8,128)S(1)} %all-to-all-done.6.arrived.data_0) | copy-start | bytes 4718596
  514.4 51.4 %all-to-all-start.7 = ((f32[16,24,8,128]{3,2,1,0:T(8,128)}), f32[16,24,8,128]{3,2,1,0:T(8,128)S(1)}, u32[]{:S(2)}, u32[]{:S(2)}) async-start(f32[16,24,8,128]{3,2,1,0:T(8,128)} %gate.12), calls=%async_computation.7 | async-start | bytes 3145728 | tf_op jit(solution)/shard_map/all_to_all | solution.py:306
  545.9 17.0 %collective-permute-start.12 = (f32[16,15,8,128]{3,2,1,0:T(8,128)}, f32[16,15,8,128]{3,2,1,0:T(8,128)S(1)}, u32[]{:S(2)}, u32[]{:S(2)}) collective-permute-start(f32[16,15,8,128]{3,2,1,0:T(8,128)} %get-tuple-element.57), channel_id=1, source_target_pairs={{0,1},{1,2},{2,3},{3,7},{7,6},{6,5},{5,4},{4,8},{8,9},{9,10},{10,1... | collective-permute-start | bytes 2949128 | tf_op jit(solution)/shard_map/ppermute | solution.py:343
  549.4 16.4 %collective-permute-start.13 = (f32[16,15,8,128]{3,2,1,0:T(8,128)}, f32[16,15,8,128]{3,2,1,0:T(8,128)}, u32[]{:S(2)}, u32[]{:S(2)}) collective-permute-start(f32[16,15,8,128]{3,2,1,0:T(8,128)} %get-tuple-element.58.rest_0_), channel_id=1, source_target_pairs={{1,0},{2,1},{3,2},{7,3},{6,7},{5,6},{4,5},{8,4},{9,8},{10,9},{11,1... | collective-permute-start | bytes 2949128 | tf_op jit(solution)/shard_map/ppermute | solution.py:344
  555.6 19.0 %copy-start.18 = (f32[128,128]{1,0:T(8,128)S(1)}, f32[128,128]{1,0:T(8,128)}, u32[]{:S(2)}) copy-start(f32[128,128]{1,0:T(8,128)} %get-tuple-element.71.matrix_y) | copy-start | bytes 196612
  562.9 3.0 copy-start.7
  565.8 21.0 %copy-start.3 = (f32[16,24,8,128]{3,2,1,0:T(8,128)}, f32[16,24,8,128]{3,2,1,0:T(8,128)S(1)}, u32[]{:S(2)}) copy-start(f32[16,24,8,128]{3,2,1,0:T(8,128)S(1)} %all-to-all-done.7.data_1) | copy-start | bytes 4718596
  565.8 34.9 %all-to-all-start.8 = ((f32[16,16,8,128]{3,2,1,0:T(8,128)}), f32[16,16,8,128]{3,2,1,0:T(8,128)S(1)}, u32[]{:S(2)}, u32[]{:S(2)}) async-start(f32[16,16,8,128]{3,2,1,0:T(8,128)} %gate.13), calls=%async_computation.8 | async-start | bytes 2097152 | tf_op jit(solution)/shard_map/all_to_all | solution.py:306
  595.3 14.9 %collective-permute-start.14 = (f32[16,15,8,128]{3,2,1,0:T(8,128)}, f32[16,15,8,128]{3,2,1,0:T(8,128)S(1)}, u32[]{:S(2)}, u32[]{:S(2)}) collective-permute-start(f32[16,15,8,128]{3,2,1,0:T(8,128)} %get-tuple-element.61), channel_id=1, source_target_pairs={{0,1},{1,2},{2,3},{3,7},{7,6},{6,5},{5,4},{4,8},{8,9},{9,10},{10,1... | collective-permute-start | bytes 2949128 | tf_op jit(solution)/shard_map/ppermute | solution.py:343
  598.8 15.6 %collective-permute-start.15 = (f32[16,15,8,128]{3,2,1,0:T(8,128)}, f32[16,15,8,128]{3,2,1,0:T(8,128)S(1)}, u32[]{:S(2)}, u32[]{:S(2)}) collective-permute-start(f32[16,15,8,128]{3,2,1,0:T(8,128)} %get-tuple-element.62), channel_id=1, source_target_pairs={{1,0},{2,1},{3,2},{7,3},{6,7},{5,6},{4,5},{8,4},{9,8},{10,9},{11,1... | collective-permute-start | bytes 2949128 | tf_op jit(solution)/shard_map/ppermute | solution.py:344
  600.7 1.0 copy-start.4
  610.1 4.3 copy-start.16
  614.4 1.0 copy-start.17

commit v4 on v3

v4 whole, which is shorter than its diff:
```python
import functools

import jax
import jax.numpy as jnp
import numpy as np
from jax import lax
from jax.experimental import pallas as pl
from jax.experimental.pallas import tpu as pltpu
from jax.sharding import PartitionSpec as P

VMEM_LIMIT = 56 * 1024 * 1024
WHOLE = pl.BlockSpec(memory_space=pltpu.VMEM)
ANYWHERE = pl.BlockSpec(memory_space=pl.ANY)
TURN_US = 4


def cost(microseconds):
    return pl.CostEstimate(flops=0, bytes_accessed=int(microseconds * 3.6e6), transcendentals=0)


def banded(kernel, extent):
    length = kernel.shape[0]
    margin = length // 2
    places = jnp.arange(extent, dtype=jnp.int32)
    offsets = places[None, :] - places[:, None] + margin
    stencil = jnp.arange(length, dtype=jnp.int32)
    picked = (offsets[None, :, :] == stencil[:, None, None]).astype(jnp.float32)
    return jnp.sum(kernel[:, None, None] * picked, axis=0)


def normalized(kernel):
    return kernel / jnp.sum(kernel)


def halves(value):
    high = value.astype(jnp.bfloat16)
    low = (value - high.astype(jnp.float32)).astype(jnp.bfloat16)
    return high, low


def position(device, run):
    row, place = device // run, device % run
    return row * run + jnp.where(row % 2 == 0, place, run - 1 - place)


def device_order(count, run):
    return [r * run + (p if r % 2 == 0 else run - 1 - p) for r in range(count // run) for p in range(run)]


def along_yz(load, store, matrix_y, matrix_z, rows):
    depth, width = matrix_z.shape[0], matrix_y.shape[0]
    right_high, right_low = halves(matrix_y)
    right = jnp.concatenate([right_high, right_low], axis=1)
    right = jnp.concatenate([right, right], axis=0)
    left_high, left_low = halves(matrix_z)
    left = jnp.concatenate([left_high, left_low], axis=0)
    left = jnp.concatenate([left, left], axis=1)

    def pair(index, _):
        row = 2 * index
        planes = jnp.concatenate([load(row), load(row + 1)], axis=0)
        product = jnp.dot(
            jnp.concatenate(halves(planes), axis=1), right, preferred_element_type=jnp.float32
        )
        mixed = product[:, :width] + product[:, width:]
        sides = jnp.concatenate([mixed[:depth], mixed[depth:]], axis=1)
        product = jnp.dot(
            left, jnp.concatenate(halves(sides), axis=0), preferred_element_type=jnp.float32
        )
        mixed = product[:depth] + product[depth:]
        store(row, mixed[:, :width])
        store(row + 1, mixed[:, width:])
        return 0

    lax.fori_loop(0, rows // 2, pair, 0, unroll=4)


def x_plane(ref, block, plane):
    blocks, rows, planes, width = ref.shape
    flat = ref.reshape(blocks * rows * planes, width)
    return flat[pl.ds(block * rows * planes + plane, rows, stride=planes), :]


def set_x_plane(ref, block, plane, value):
    blocks, rows, planes, width = ref.shape
    flat = ref.reshape(blocks * rows * planes, width)
    flat[pl.ds(block * rows * planes + plane, rows, stride=planes), :] = value


def padded(size):
    return -(-size // 16) * 16


def along_x(groups, matrix, emit):
    blocks, _, planes, width = groups[0][0].shape
    left_high, left_low = halves(matrix)
    left = jnp.concatenate([left_high, left_low], axis=0)
    left = jnp.concatenate([left, left], axis=1)

    def column(block, plane):
        parts = []
        for group in groups:
            parts += [x_plane(piece, block, plane) for piece in group]
            size = sum(piece.shape[1] for piece in group)
            if padded(size) > size:
                parts.append(jnp.zeros((padded(size) - size, width), jnp.float32))
        return jnp.concatenate(parts, axis=0)

    def pair(index, _):
        block, plane = index // (planes // 2), (index % (planes // 2)) * 2
        columns = jnp.concatenate([column(block, plane), column(block, plane + 1)], axis=1)
        product = jnp.dot(
            left, jnp.concatenate(halves(columns), axis=0), preferred_element_type=jnp.float32
        )
        mixed = product[: product.shape[0] // 2] + product[product.shape[0] // 2 :]
        emit(block, plane, mixed[:, :width])
        emit(block, plane + 1, mixed[:, width:])
        return 0

    lax.fori_loop(0, blocks * planes // 2, pair, 0, unroll=4)


def x_matrix(taps, groups, target):
    margin, nowhere = taps.shape[0] // 2, 1 << 20
    source = np.concatenate(
        [np.r_[np.arange(x, x + n), np.full(padded(n) - n, nowhere)] for x, n in groups]
    )
    rows = np.arange(padded(target[1]))
    offset = source[None, :] - (target[0] + rows)[:, None] + margin
    offset = np.where(rows[:, None] < target[1], offset, -1).astype(np.int32)
    stencil = jnp.arange(taps.shape[0], dtype=jnp.int32)
    picked = (jnp.asarray(offset)[None] == stencil[:, None, None]).astype(jnp.float32)
    return jnp.sum(taps[:, None, None] * picked, axis=0)


def plane_loader(ref):
    blocks, _, planes, width = ref.shape
    return lambda row: ref[:, row].reshape(blocks * planes, width)


def plane_storer(ref):
    blocks, _, planes, width = ref.shape

    def store(row, value):
        ref[:, row] = value.reshape(blocks, planes, width)

    return store


def copy_ends(first, second, head, tail):
    rows, kept = second.shape[1], head.shape[1]
    head[...] = first[:, :kept]
    tail[...] = second[:, rows - kept :]


def divide_yz(blurred, data, out, matrix_y, matrix_z, begin=0, place=0):
    data_of, blurred_of = plane_loader(data), plane_loader(blurred)
    along_yz(
        lambda row: data_of(place + row) / blurred_of(begin + row),
        plane_storer(out),
        matrix_y,
        matrix_z,
        out.shape[1],
    )


def blur(wide, mixed, blurred, blur_x, blur_y, blur_z):
    along_yz(plane_loader(wide), plane_storer(mixed), blur_y[...], blur_z[...], wide.shape[1])
    rows = blurred.shape[1]
    along_x([[mixed]], blur_x[...], lambda b, p, value: set_x_plane(blurred, b, p, value[:rows]))


def update(spread_x, above, center, below, before, wide):
    rows = wide.shape[1]

    def emit(block, plane, value):
        set_x_plane(wide, block, plane, x_plane(before, block, plane) * value[:rows])

    along_x([[above], [center], [below]], spread_x[...], emit)


def first_kernel(
    blur_x, blur_y, blur_z, back_y, back_z, above, own, below, data, wide, out, head, tail, mixed, blurred
):
    margin, rows = above.shape[1], own.shape[1]
    wide[:, :margin] = above[...]
    wide[:, margin : margin + rows] = own[...]
    wide[:, margin + rows : rows + 2 * margin] = below[...]
    if wide.shape[1] > rows + 2 * margin:
        wide[:, rows + 2 * margin :] = jnp.zeros_like(wide[:, rows + 2 * margin :])
    blur(wide, mixed, blurred, blur_x, blur_y, blur_z)
    divide_yz(blurred, data, out, back_y[...], back_z[...])
    copy_ends(out, out, head, tail)


def view_kernel(
    spread_x, blur_x, blur_y, blur_z, back_y, back_z, above, center, below, before, data,
    wide, out, head, tail, mixed, blurred,
):
    update(spread_x, above, center, below, before, wide)
    blur(wide, mixed, blurred, blur_x, blur_y, blur_z)
    divide_yz(blurred, data, out, back_y[...], back_z[...])
    copy_ends(out, out, head, tail)


def last_kernel(
    margin, spread_x, blur_x, blur_y, blur_z, back_y, back_z, above, center, below, before, data,
    own, inner, out_0, out_1, head, tail, wide, mixed, blurred,
):
    update(spread_x, above, center, below, before, wide)
    own[...] = wide[:, margin : margin + own.shape[1]]
    blur(wide, mixed, blurred, blur_x, blur_y, blur_z)
    outer, between = out_0.shape[1], inner.shape[1]
    inner[...] = blurred[:, outer : outer + between]
    divide_yz(blurred, data, out_0, back_y[...], back_z[...])
    divide_yz(blurred, data, out_1, back_y[...], back_z[...], outer + between, outer)
    copy_ends(out_0, out_1, head, tail)


def middle_kernel(back_y, back_z, blurred, data, out):
    divide_yz(blurred, data, out, back_y[...], back_z[...])


def finish_kernel(count, spread_x, above, below, current, *rest):
    pieces, updated = rest[:count], rest[count]
    rows = updated.shape[1]

    def emit(block, plane, value):
        set_x_plane(updated, block, plane, x_plane(current, block, plane) * value[:rows])

    along_x([[above], pieces, [below]], spread_x[...], emit)


def striped(kernel, name, microseconds, inputs, outs):
    blocks = outs[0].shape[0]
    step = 4 if blocks % 4 == 0 else 1

    def spec(array):
        return pl.BlockSpec((step,) + array.shape[1:], lambda g: (g, 0, 0, 0))

    return pl.pallas_call(
        kernel,
        grid=(blocks // step,),
        out_shape=outs,
        in_specs=[WHOLE] + [spec(array) for array in inputs[1:]],
        out_specs=[spec(array) for array in outs],
        compiler_params=pltpu.CompilerParams(vmem_limit_bytes=VMEM_LIMIT),
        cost_estimate=cost(microseconds),
        name=name,
    )(*inputs)


def call(kernel, name, microseconds, outs, in_specs, scratch=()):
    return pl.pallas_call(
        kernel,
        out_shape=outs,
        in_specs=in_specs,
        out_specs=jax.tree.map(lambda _: WHOLE, outs),
        scratch_shapes=list(scratch),
        compiler_params=pltpu.CompilerParams(vmem_limit_bytes=VMEM_LIMIT),
        cost_estimate=cost(microseconds),
        name=name,
    )


def source_block(place, run):
    return jnp.where(pl.program_id(0) % 2 == 0, place, run - 1 - place)


def turn_kernel(run, chosen, source, *rest):
    target = rest[-1]
    depth, extent, width = source.shape
    flat = source.reshape(depth * extent, width)
    for place in range(run):
        base = source_block(place, run) * (extent // run)
        for place_row, row in enumerate(chosen):
            target[place, place_row] = flat[pl.ds(base + row, depth, stride=extent), :]


def turn_back_kernel(run, source, target):
    _, rows, depth, width = source.shape
    flat = source.reshape(run * rows * depth, width)
    for place in range(run):
        base = source_block(place, run) * rows
        for plane in range(depth):
            for row in range(0, rows, 8):
                target[plane, pl.ds(pl.multiple_of(base + row, 8), 8), :] = flat[
                    pl.ds((place * rows + row) * depth + plane, 8, stride=depth), :
                ]


def gate(blocks, arrays):
    return pl.pallas_call(
        lambda *refs: None,
        out_shape=jax.ShapeDtypeStruct(blocks.shape, blocks.dtype),
        in_specs=[ANYWHERE] * (1 + len(arrays)),
        out_specs=ANYWHERE,
        input_output_aliases={0: 0},
        cost_estimate=cost(0.5),
        name="gate",
    )(blocks, *arrays)


def to_pencils(planes, count, run, chosen, turn_after=(), send_after=()):
    depth, extent, width = planes.shape
    rows = extent // count
    size = len(chosen)
    if depth % 8 == 0 and rows % 8 == 0:
        blocks = pl.pallas_call(
            functools.partial(turn_kernel, run, chosen),
            grid=(count // run,),
            out_shape=jax.ShapeDtypeStruct((count, size, depth, width), planes.dtype),
            in_specs=[pl.BlockSpec((depth, run * rows, width), lambda g: (0, g, 0))]
            + [ANYWHERE] * len(turn_after),
            out_specs=pl.BlockSpec((run, size, depth, width), lambda g: (g, 0, 0, 0)),
            compiler_params=pltpu.CompilerParams(vmem_limit_bytes=VMEM_LIMIT),
            cost_estimate=cost(TURN_US),
            name="turn",
        )(planes, *turn_after)
        if send_after:
            blocks = gate(blocks, send_after)
        return lax.all_to_all(blocks, "slab", split_axis=0, concat_axis=0, tiled=True)
    order = device_order(count, run)
    blocks = planes.reshape(depth, count, rows, width)[:, :, np.array(chosen)].transpose(1, 0, 2, 3)
    blocks = jnp.stack([blocks[order.index(d)] for d in range(count)])
    blocks = lax.all_to_all(blocks, "slab", split_axis=0, concat_axis=0, tiled=True)
    return blocks.reshape(1, count * depth, size, width).swapaxes(1, 2)


def to_planes(pencils, count, run, depth):
    rows, width = pencils.shape[1], pencils.shape[3]
    if depth % 8 == 0 and rows % 8 == 0:
        blocks = lax.all_to_all(pencils, "slab", split_axis=0, concat_axis=0, tiled=True)
        return pl.pallas_call(
            functools.partial(turn_back_kernel, run),
            grid=(count // run,),
            out_shape=jax.ShapeDtypeStruct((depth, rows * count, width), pencils.dtype),
            in_specs=[pl.BlockSpec((run, rows, depth, width), lambda g: (g, 0, 0, 0))],
            out_specs=pl.BlockSpec((depth, run * rows, width), lambda g: (0, g, 0)),
            compiler_params=pltpu.CompilerParams(vmem_limit_bytes=VMEM_LIMIT),
            cost_estimate=cost(TURN_US),
            name="turn_back",
        )(blocks)
    order = device_order(count, run)
    blocks = pencils.swapaxes(1, 2).reshape(count, depth, rows, width)
    blocks = lax.all_to_all(blocks, "slab", split_axis=0, concat_axis=0, tiled=True)
    blocks = jnp.stack([blocks[d] for d in order])
    return blocks.transpose(1, 0, 2, 3).reshape(depth, rows * count, width)


def halos(head, tail, margin, count, run):
    order = device_order(count, run)
    rows = head.shape[1]
    above, below, need, hop = [], [], margin, 1
    while need > 0:
        size = min(rows, need)
        forth = [(order[p], order[p + hop]) for p in range(count - hop)]
        back = [(order[p + hop], order[p]) for p in range(count - hop)]
        above.insert(0, lax.ppermute(tail[:, rows - size :], "slab", forth))
        below.append(lax.ppermute(head[:, :size], "slab", back))
        need, hop = need - size, hop + 1
    if len(above) == 1:
        return above[0], below[0]
    return jnp.concatenate(above, axis=1), jnp.concatenate(below, axis=1)


def body(estimate, recorded, lateral, axial_taps):
    count = lax.axis_size("slab")
    run = max(count // 4, 1)
    depth, rows, width = estimate.shape[0], estimate.shape[1] // count, estimate.shape[2]
    views, margin = recorded.shape[0], lateral.shape[2] // 2
    last = views - 1
    every = tuple(range(rows))

    current = to_pencils(estimate, count, run, every)
    data = to_pencils(recorded[0], count, run, every)
    blocks, _, planes, _ = current.shape

    def volume(size):
        return jax.ShapeDtypeStruct((blocks, size, planes, width), jnp.float32)

    def held(size):
        return pltpu.VMEM((blocks, size, planes, width), jnp.float32)

    extent, double = padded(rows + 2 * margin), 2 * margin
    end = volume(min(double, rows))
    taps = [normalized(lateral[v, 0]) for v in range(views)]
    columns = [banded(normalized(lateral[v, 1]), width) for v in range(views)]
    depths = [banded(normalized(axial_taps[v]), blocks * planes) for v in range(views)]
    blur_x = [x_matrix(t[::-1], [(-margin, extent)], (0, rows)) for t in taps]
    sides = [(-double, double), (0, rows), (rows, double)]
    spread_x = [x_matrix(t, sides, (-margin, rows + double)) for t in taps[:last]]
    sides = [(-margin, margin), (0, rows), (rows, margin)]
    finish_x = x_matrix(taps[last], sides, (0, rows))

    def matrices(v):
        return blur_x[v], columns[v], depths[v].T, columns[v].T, depths[v]

    outer = 5 * rows // 16
    split = outer >= margin + 1 and outer % 2 == 0 and views > 1
    ends = tuple(r for r in every if r < outer or r >= rows - outer)
    inside = tuple(r for r in every if outer <= r < rows - outer)

    above, below = halos(current[:, :margin], current[:, rows - margin :] if rows > margin else current, margin, count, run)
    for v in range(views):
        if v < last:
            chosen = ends if split and v + 1 == last else every
            order = (head,) if v else ()
            coming = to_pencils(recorded[v + 1], count, run, chosen, order, (above, below))
        if v == 0:
            wide, center, head, tail = call(
                first_kernel, "first", 26, (volume(extent), volume(rows), end, end), [WHOLE] * 9,
                [held(extent), held(rows)],
            )(*matrices(v), above, current, below, data)
        elif v == last and split:
            coming = to_pencils(recorded[v], count, run, inside, (head,), (above, below))
            outs = [volume(n) for n in (rows, rows - 2 * outer, outer, outer, margin, margin)]
            own, blurred, first, second, head, tail = call(
                functools.partial(last_kernel, margin), "last", 30, tuple(outs), [WHOLE] * 11,
                [held(extent), held(extent), held(rows)],
            )(spread_x[v - 1], *matrices(v), above, center, below, wide, data)
        else:
            wide, center, head, tail = call(
                view_kernel, "view", 33, (volume(extent), volume(rows), end, end), [WHOLE] * 11,
                [held(extent), held(rows)],
            )(spread_x[v - 1], *matrices(v), above, center, below, wide, data)
        reach = double
        if v == last:
            reach = margin
            head, tail = head[:, :margin], tail[:, max(tail.shape[1] - margin, 0) :]
        above, below = halos(head, tail, reach, count, run)
        data = coming
    if split:
        inner = call(middle_kernel, "middle", 3, volume(rows - 2 * outer), [WHOLE] * 4)(
            columns[last].T, depths[last], blurred, data
        )
        pieces = [first, inner, second]
    else:
        own, pieces = wide[:, margin : margin + rows], [center]
    (current,) = striped(
        functools.partial(finish_kernel, len(pieces)),
        "finish",
        8,
        [finish_x, above, below, own, *pieces],
        [volume(rows)],
    )
    return to_planes(current, count, run, depth)


def solution(mesh):
    in_specs = (P("slab", "groups", None), P(None, "slab", "groups", None), P(), P())
    out_specs = P("slab", "groups", None)
    return jax.shard_map(body, mesh=mesh, in_specs=in_specs, out_specs=out_specs, check_vma=False)
```

time: 733 us -> 705 us (0.962)
  Pallas kernels: 219 us -> 175 us
  waiting for transfers between devices: 189 us -> 222 us
  starting transfers between devices: 183 us -> 168 us
    pallas_call x20 -> x12, Pallas kernels: 214 us -> 171 us  [the longest x2 66.7 us: body(): call(view_kernel, 'view', 33, (volume(extent), volume(rows), end, end), [...]
    ppermute x8 -> x5, waiting for transfers between devices: 77.7 us -> 95.2 us  [halos(): above.insert(0, lax.ppermute(tail[:, rows - size:], 'slab', forth))]
    ppermute x8 -> x5, starting transfers between devices: 28.2 us -> 17.7 us  [halos(): above.insert(0, lax.ppermute(tail[:, rows - size:], 'slab', forth))]
    all_to_all x9 -> x6, waiting for transfers between devices: 83.8 us -> 93.7 us  [to_pencils(): lax.all_to_all(blocks, 'slab', split_axis=0, concat_axis=0, tiled=True)]
    ppermute x8 -> x5, waiting for transfers between devices: 27.5 us -> 33.4 us  [halos(): below.append(lax.ppermute(head[:, :size], 'slab', back))]
    ppermute x8 -> x5, starting transfers between devices: 15.4 us -> 9.71 us  [halos(): below.append(lax.ppermute(head[:, :size], 'slab', back))]
    all_to_all x9 -> x6, starting transfers between devices: 140 us -> 140 us  [to_pencils(): lax.all_to_all(blocks, 'slab', split_axis=0, concat_axis=0, tiled=True)]
  transfers between devices with their start and end apart: 25 -> 16, of which waited for: 18 -> 12; matrix products, arithmetic and copies ran while one was open for 5% -> 5% of each run, Pallas kernels for 27% -> 22%
where the time goes in v4:
time: 705 us; the launch traced here: 703 us
  waiting for transfers between devices  222 us (31%)
  Pallas kernels  175 us (25%)
  starting transfers between devices  168 us (24%)
  blocking collectives  97.4 us (14%)
  local copies, waits for them, and re-layouts  22 us (3%)
  other arithmetic  18.2 us (3%)
    all_to_all x6, starting transfers between devices, to_pencils(): lax.all_to_all(blocks, 'slab', split_axis=0, concat_axis=0, tiled=True)  140 us
    all_to_all x1, blocking collectives, to_planes(): lax.all_to_all(pencils, 'slab', split_axis=0, concat_axis=0, tiled=True)  97.4 us
    ppermute x5, waiting for transfers between devices, halos(): above.insert(0, lax.ppermute(tail[:, rows - size:], 'slab', forth))  95.2 us
    all_to_all x6, waiting for transfers between devices, to_pencils(): lax.all_to_all(blocks, 'slab', split_axis=0, concat_axis=0, tiled=True)  93.7 us
    pallas_call x2, Pallas kernels, body(): call(view_kernel, 'view', 33, (volume(extent), volume(rows), end, end), [...  66.7 us
    ppermute x5, waiting for transfers between devices, halos(): below.append(lax.ppermute(head[:, :size], 'slab', back))  33.4 us
    pallas_call x6, Pallas kernels, to_pencils(): pl.pallas_call(functools.partial(turn_kernel, run, chosen), grid=(count /...  32.9 us
    pallas_call x1, Pallas kernels, body(): call(functools.partial(last_kernel, margin), 'last', 30, tuple(outs), [WH...  31.4 us
  transfers between devices with their start and end apart: 16, of which 12 were waited for; matrix products, arithmetic and copies ran while one was open for 5% of the time, Pallas kernels for 22%

profile of v4, /device:TPU:1, one launch (start us, length us, event | category | flops | bytes accessed | tf_op | source)
XLA Modules:
  0.0 703.4 jit_solution(14044506631424700703)
XLA Ops:
  0.0 5.8 turn.6
  5.8 7.3 %all-to-all-start = ((f32[16,64,8,128]{3,2,1,0:T(8,128)}), f32[16,64,8,128]{3,2,1,0:T(8,128)}, u32[]{:S(2)}, u32[]{:S(2)}) async-start(f32[16,64,8,128]{3,2,1,0:T(8,128)} %turn.6), calls=%async_computation | async-start | bytes 8388608 | tf_op jit(solution)/shard_map/all_to_all | solution.py:322
  13.1 12.2 %slice_bitcast_fusion = (f32[8,1024,128]{2,1,0:T(8,128)}, f32[8,1024,128]{2,1,0:T(8,128)}, f32[8,1024,128]{2,1,0:T(8,128)}, f32[8,1024,128]{2,1,0:T(8,128)}) fusion(f32[4,8,1024,128]{3,2,1,0:T(8,128)} %param.13), kind=kLoop, calls=%fused_computation.5 | loop fusion | bytes 33554432 | tf_op jit(solution)/shard_map/squeeze | solution.py:409
  25.3 5.8 turn.7
  31.2 60.1 %all-to-all-done.own = f32[16,64,8,128]{3,2,1,0:T(8,128)} async-done(((f32[16,64,8,128]{3,2,1,0:T(8,128)}), f32[16,64,8,128]{3,2,1,0:T(8,128)}, u32[]{:S(2)}, u32[]{:S(2)}) %all-to-all-start) | async-done | bytes 4194336 | tf_op jit(solution)/shard_map/all_to_all | solution.py:322
  91.2 19.3 %all-to-all-start.1 = ((f32[16,64,8,128]{3,2,1,0:T(8,128)}), f32[16,64,8,128]{3,2,1,0:T(8,128)}, u32[]{:S(2)}, u32[]{:S(2)}) async-start(f32[16,64,8,128]{3,2,1,0:T(8,128)} %turn.7), calls=%async_computation.1 | async-start | bytes 8388608 | tf_op jit(solution)/shard_map/all_to_all | solution.py:322
  110.5 1.6 fusion.2
  112.1 3.5 collective-permute-start
  115.7 1.9 collective-permute-start.1
  117.6 5.9 turn.8.refs_0_
  123.5 26.4 %collective-permute-done.above.refs_1_ = f32[16,15,8,128]{3,2,1,0:T(8,128)S(1)} collective-permute-done((f32[16,15,8,128]{3,2,1,0:T(8,128)S(1)}, f32[16,15,8,128]{3,2,1,0:T(8,128)S(1)}, u32[]{:S(2)}, u32[]{:S(2)}) %collective-permute-start) | collective-permute-done | bytes 983072 | tf_op jit(solution)/shard_map/ppermute | solution.py:359
  149.8 4.2 collective-permute-done.1.below.refs_2_
  154.0 0.9 copy-done.4
  155.0 33.7 %all-to-all-done.1.data = f32[16,64,8,128]{3,2,1,0:T(8,128)} async-done(((f32[16,64,8,128]{3,2,1,0:T(8,128)}), f32[16,64,8,128]{3,2,1,0:T(8,128)}, u32[]{:S(2)}, u32[]{:S(2)}) %all-to-all-start.1) | async-done | bytes 4194336 | tf_op jit(solution)/shard_map/all_to_all | solution.py:322
  188.6 30.5 %all-to-all-start.2 = ((f32[16,64,8,128]{3,2,1,0:T(8,128)}), f32[16,64,8,128]{3,2,1,0:T(8,128)}, u32[]{:S(2)}, u32[]{:S(2)}) async-start(f32[16,64,8,128]{3,2,1,0:T(8,128)} %gate.4), calls=%async_computation.2 | async-start | bytes 8388608 | tf_op jit(solution)/shard_map/all_to_all | solution.py:322
  219.1 0.7 slice_reduce_fusion.1
  219.8 2.5 divide_bitcast_fusion.7
  222.8 1.0 select_reduce_fusion.4
  223.8 0.7 copy.32
  225.2 2.5 divide_bitcast_fusion.6
  227.7 3.7 select_reduce_fusion
  231.4 0.7 copy.31
  232.7 1.2 broadcast_divide_fusion
  233.9 2.4 broadcast_divide_fusion.5
  236.3 1.1 select_reduce_fusion.11
  237.4 25.9 %first.1 = (f32[16,96,8,128]{3,2,1,0:T(8,128)}, f32[16,64,8,128]{3,2,1,0:T(8,128)}, f32[16,30,8,128]{3,2,1,0:T(8,128)}, f32[16,30,8,128]{3,2,1,0:T(8,128)}) custom-call(f32[64,96]{1,0:T(8,128)} %get-tuple-element.52.blur_x, f32[128,128]{1,0:T(8,128)} %copy-done.13, f32[128,128]{1,0:T(8,128)} %bitcast.56, f32[128,128]{1,0:T(8,128)} %bitcast.55, ...), custom_call_target="tpu_custom_call" | custom-call | bytes 93600000 | tf_op jit(solution)/shard_map/first/pallas_call | solution.py:411
  263.3 3.5 collective-permute-start.2
  266.8 1.9 collective-permute-start.3
  268.8 5.9 turn.9.refs_0_
  274.6 20.2 %collective-permute-done.2.above.refs_1_ = f32[16,30,8,128]{3,2,1,0:T(8,128)S(1)} collective-permute-done((f32[16,30,8,128]{3,2,1,0:T(8,128)}, f32[16,30,8,128]{3,2,1,0:T(8,128)S(1)}, u32[]{:S(2)}, u32[]{:S(2)}) %collective-permute-start.2) | collective-permute-done | bytes 1966112 | tf_op jit(solution)/shard_map/ppermute | solution.py:359
  294.8 9.5 %collective-permute-done.3.below.refs_2_ = f32[16,30,8,128]{3,2,1,0:T(8,128)} collective-permute-done((f32[16,30,8,128]{3,2,1,0:T(8,128)}, f32[16,30,8,128]{3,2,1,0:T(8,128)}, u32[]{:S(2)}, u32[]{:S(2)}) %collective-permute-start.3) | collective-permute-done | bytes 1966112 | tf_op jit(solution)/shard_map/ppermute | solution.py:360
  304.3 33.2 %all-to-all-start.3 = ((f32[16,64,8,128]{3,2,1,0:T(8,128)}), f32[16,64,8,128]{3,2,1,0:T(8,128)}, u32[]{:S(2)}, u32[]{:S(2)}) async-start(f32[16,64,8,128]{3,2,1,0:T(8,128)} %gate.5), calls=%async_computation.3 | async-start | bytes 8388608 | tf_op jit(solution)/shard_map/all_to_all | solution.py:322
  337.6 0.7 copy.30
  338.3 0.7 copy.29
  339.0 1.1 select_reduce_fusion.8
  340.1 33.3 %view.2 = (f32[16,96,8,128]{3,2,1,0:T(8,128)}, f32[16,64,8,128]{3,2,1,0:T(8,128)}, f32[16,30,8,128]{3,2,1,0:T(8,128)}, f32[16,30,8,128]{3,2,1,0:T(8,128)}) custom-call(f32[96,128]{1,0:T(8,128)} %get-tuple-element.49.spread_x, f32[64,96]{1,0:T(8,128)} %get-tuple-element.53.blur_x, f32[128,128]{1,0:T(8,128)} %copy-done.11, f32[128,128]{1,0:T(8,128)} %bitcast.51, ...), custom_call_target="tpu_custom_call" | custom-call | bytes 118800000 | tf_op jit(solution)/shard_map/view/pallas_call | solution.py:423
  373.5 3.5 collective-permute-start.4
  377.0 1.9 collective-permute-start.5
  378.9 5.0 turn.10.refs_0_
  383.9 26.2 %collective-permute-done.4.above.refs_1_ = f32[16,30,8,128]{3,2,1,0:T(8,128)S(1)} collective-permute-done((f32[16,30,8,128]{3,2,1,0:T(8,128)}, f32[16,30,8,128]{3,2,1,0:T(8,128)S(1)}, u32[]{:S(2)}, u32[]{:S(2)}) %collective-permute-start.4) | collective-permute-done | bytes 1966112 | tf_op jit(solution)/shard_map/ppermute | solution.py:359
  410.1 7.9 %collective-permute-done.5.below.refs_2_ = f32[16,30,8,128]{3,2,1,0:T(8,128)} collective-permute-done((f32[16,30,8,128]{3,2,1,0:T(8,128)}, f32[16,30,8,128]{3,2,1,0:T(8,128)}, u32[]{:S(2)}, u32[]{:S(2)}) %collective-permute-start.5) | collective-permute-done | bytes 1966112 | tf_op jit(solution)/shard_map/ppermute | solution.py:360
  418.1 37.8 %all-to-all-start.4 = ((f32[16,40,8,128]{3,2,1,0:T(8,128)}), f32[16,40,8,128]{3,2,1,0:T(8,128)S(1)}, u32[]{:S(2)}, u32[]{:S(2)}) async-start(f32[16,40,8,128]{3,2,1,0:T(8,128)} %gate.6), calls=%async_computation.4 | async-start | bytes 5242880 | tf_op jit(solution)/shard_map/all_to_all | solution.py:322
  455.9 0.7 copy.28
  456.6 0.7 copy.27
  457.3 33.4 %view.3 = (f32[16,96,8,128]{3,2,1,0:T(8,128)}, f32[16,64,8,128]{3,2,1,0:T(8,128)}, f32[16,30,8,128]{3,2,1,0:T(8,128)}, f32[16,30,8,128]{3,2,1,0:T(8,128)}) custom-call(f32[96,128]{1,0:T(8,128)} %get-tuple-element.50.spread_x, f32[64,96]{1,0:T(8,128)} %get-tuple-element.54.blur_x, f32[128,128]{1,0:T(8,128)} %copy-done.9, f32[128,128]{1,0:T(8,128)} %bitcast.54, ...), custom_call_target="tpu_custom_call" | custom-call | bytes 118800000 | tf_op jit(solution)/shard_map/view/pallas_call | solution.py:423
  490.7 3.5 collective-permute-start.6
  494.2 2.0 collective-permute-start.7
  496.3 4.5 turn.11.refs_0_
  500.8 18.8 %collective-permute-done.6.above.refs_1_ = f32[16,30,8,128]{3,2,1,0:T(8,128)} collective-permute-done((f32[16,30,8,128]{3,2,1,0:T(8,128)}, f32[16,30,8,128]{3,2,1,0:T(8,128)}, u32[]{:S(2)}, u32[]{:S(2)}) %collective-permute-start.6) | collective-permute-done | bytes 1966112 | tf_op jit(solution)/shard_map/ppermute | solution.py:359
  519.6 7.5 %collective-permute-done.7.below.refs_2_ = f32[16,30,8,128]{3,2,1,0:T(8,128)} collective-permute-done((f32[16,30,8,128]{3,2,1,0:T(8,128)}, f32[16,30,8,128]{3,2,1,0:T(8,128)}, u32[]{:S(2)}, u32[]{:S(2)}) %collective-permute-start.7) | collective-permute-done | bytes 1966112 | tf_op jit(solution)/shard_map/ppermute | solution.py:360
  527.1 12.3 %all-to-all-start.5 = ((f32[16,24,8,128]{3,2,1,0:T(8,128)}), f32[16,24,8,128]{3,2,1,0:T(8,128)}, u32[]{:S(2)}, u32[]{:S(2)}) async-start(f32[16,24,8,128]{3,2,1,0:T(8,128)} %gate.7), calls=%async_computation.5 | async-start | bytes 3145728 | tf_op jit(solution)/shard_map/all_to_all | solution.py:322
  539.5 0.7 copy.26
  540.2 0.7 copy.25
  540.9 31.4 %last.1 = (f32[16,64,8,128]{3,2,1,0:T(8,128)}, f32[16,24,8,128]{3,2,1,0:T(8,128)}, f32[16,20,8,128]{3,2,1,0:T(8,128)}, f32[16,20,8,128]{3,2,1,0:T(8,128)}, f32[1...) custom-call(f32[96,128]{1,0:T(8,128)} %get-tuple-element.51.spread_x, f32[64,96]{1,0:T(8,128)} %get-tuple-element.55.blur_x, ...), custom_call_target="tpu_custom_call" | custom-call | bytes 108000000 | tf_op jit(solution)/shard_map/last/pallas_call | solution.py:418
  572.3 3.5 collective-permute-start.8
  575.8 1.9 collective-permute-start.9
  577.8 0.8 select_reduce_fusion.15.spread_x
  578.6 5.0 middle.1.rest_1_
  583.6 3.6 collective-permute-done.8.above
  587.2 4.3 collective-permute-done.9.below
  591.5 1.0 copy-done.7
  592.5 8.6 %finish.1 = f32[16,64,8,128]{3,2,1,0:T(8,128)} custom-call(f32[64,96]{1,0:T(8,128)} %select_reduce_fusion.15.spread_x, f32[16,15,8,128]{3,2,1,0:T(8,128)} %copy-done.6, f32[16,15,8,128]{3,2,1,0:T(8,128)} %copy-done.7, f32[16,64,8,128]{3,2,1,0:T(8,128)} %get-tuple-element.37.current, f32[16,20,8,128]{3,2,1,0:T(8,128)} %get-tuple-element.38.rest_0_, ...), custom_call_target="tpu_custom_call" | custom-call | bytes 28800000 | tf_op jit(solution)/shard_map/finish/pallas_call | solution.py:241
  601.1 97.4 %all_to_all.35.source = f32[16,64,8,128]{3,2,1,0:T(8,128)} all-to-all(f32[16,64,8,128]{3,2,1,0:T(8,128)} %finish.1), channel_id=1, replica_groups=mesh['groups'=2,'slab'=16] {'slab'}, dimensions={0} | all-to-all | bytes 8388608 | tf_op jit(solution)/shard_map/all_to_all | solution.py:333
  698.5 4.9 turn_back.1
  (54 shorter events, 1.7 us)
Async XLA Ops:
  5.8 85.4 %all-to-all-start = ((f32[16,64,8,128]{3,2,1,0:T(8,128)}), f32[16,64,8,128]{3,2,1,0:T(8,128)}, u32[]{:S(2)}, u32[]{:S(2)}) async-start(f32[16,64,8,128]{3,2,1,0:T(8,128)} %turn.6), calls=%async_computation | async-start | bytes 8388608 | tf_op jit(solution)/shard_map/all_to_all | solution.py:322
  91.2 97.4 %all-to-all-start.1 = ((f32[16,64,8,128]{3,2,1,0:T(8,128)}), f32[16,64,8,128]{3,2,1,0:T(8,128)}, u32[]{:S(2)}, u32[]{:S(2)}) async-start(f32[16,64,8,128]{3,2,1,0:T(8,128)} %turn.7), calls=%async_computation.1 | async-start | bytes 8388608 | tf_op jit(solution)/shard_map/all_to_all | solution.py:322
  112.1 37.7 %collective-permute-start = (f32[16,15,8,128]{3,2,1,0:T(8,128)S(1)}, f32[16,15,8,128]{3,2,1,0:T(8,128)S(1)}, u32[]{:S(2)}, u32[]{:S(2)}) collective-permute-start(f32[16,15,8,128]{3,2,1,0:T(8,128)S(1)} %get-tuple-element.73), channel_id=1, source_target_pairs={{0,1},{1,2},{2,3},{3,7},{7,6},{6,5},{5,4},{4,8},{8,9},{9,10},{10,1... | collective-permute-start | bytes 2949128 | tf_op jit(solution)/shard_map/ppermute | solution.py:359
  115.7 38.3 %collective-permute-start.1 = (f32[16,15,8,128]{3,2,1,0:T(8,128)S(1)}, f32[16,15,8,128]{3,2,1,0:T(8,128)S(1)}, u32[]{:S(2)}, u32[]{:S(2)}) collective-permute-start(f32[16,15,8,128]{3,2,1,0:T(8,128)S(1)} %get-tuple-element.72), channel_id=1, source_target_pairs={{1,0},{2,1},{3,2},{7,3},{6,7},{5,6},{4,5},{8,4},{9,8},{10,9},{11,1... | collective-permute-start | bytes 2949128 | tf_op jit(solution)/shard_map/ppermute | solution.py:360
  149.8 4.2 copy-start.3
  154.0 0.9 copy-start.4
  155.0 64.1 %copy-start.18 = (f32[4,2,31]{2,1,0:T(2,128)S(1)}, f32[4,2,31]{2,1,0:T(2,128)}, u32[]{:S(2)}) copy-start(f32[4,2,31]{2,1,0:T(2,128)} %param.14) | copy-start | bytes 2980
  155.0 69.6 %copy-start.19 = (f32[4,101]{1,0:T(4,128)S(1)}, f32[4,101]{1,0:T(4,128)}, u32[]{:S(2)}) copy-start(f32[4,101]{1,0:T(4,128)} %param.15) | copy-start | bytes 4852
  155.0 81.3 %copy-start.17 = (s32[64,96]{1,0:T(8,128)S(1)}, s32[64,96]{1,0:T(8,128)}, u32[]{:S(2)}) copy-start(s32[64,96]{1,0:T(8,128)} %constant.28.clone) | copy-start | bytes 73732
  188.6 115.7 %all-to-all-start.2 = ((f32[16,64,8,128]{3,2,1,0:T(8,128)}), f32[16,64,8,128]{3,2,1,0:T(8,128)}, u32[]{:S(2)}, u32[]{:S(2)}) async-start(f32[16,64,8,128]{3,2,1,0:T(8,128)} %gate.4), calls=%async_computation.2 | async-start | bytes 8388608 | tf_op jit(solution)/shard_map/all_to_all | solution.py:322
  223.8 13.6 %copy-start.13 = (f32[128,128]{1,0:T(8,128)}, f32[128,128]{1,0:T(8,128)S(1)}, u32[]{:S(2)}) copy-start(f32[128,128]{1,0:T(8,128)S(1)} %get-tuple-element.45.blur_y) | copy-start | bytes 196612
  223.8 113.8 %copy-start.11 = (f32[128,128]{1,0:T(8,128)}, f32[128,128]{1,0:T(8,128)S(1)}, u32[]{:S(2)}) copy-start(f32[128,128]{1,0:T(8,128)S(1)} %get-tuple-element.46.blur_y) | copy-start | bytes 196612
  223.8 232.1 %copy-start.9 = (f32[128,128]{1,0:T(8,128)}, f32[128,128]{1,0:T(8,128)S(1)}, u32[]{:S(2)}) copy-start(f32[128,128]{1,0:T(8,128)S(1)} %get-tuple-element.47.blur_y) | copy-start | bytes 196612
  223.8 315.7 %copy-start.8 = (f32[128,128]{1,0:T(8,128)}, f32[128,128]{1,0:T(8,128)S(1)}, u32[]{:S(2)}) copy-start(f32[128,128]{1,0:T(8,128)S(1)} %get-tuple-element.48.blur_y) | copy-start | bytes 196612
  231.4 6.0 copy-start.14
  231.4 106.9 %copy-start.12 = (f32[128,128]{1,0:T(8,128)}, f32[128,128]{1,0:T(8,128)S(1)}, u32[]{:S(2)}) copy-start(f32[128,128]{1,0:T(8,128)S(1)} %get-tuple-element.42.back_z) | copy-start | bytes 196612
  231.4 225.2 %copy-start.10 = (f32[128,128]{1,0:T(8,128)}, f32[128,128]{1,0:T(8,128)S(1)}, u32[]{:S(2)}) copy-start(f32[128,128]{1,0:T(8,128)S(1)} %get-tuple-element.43.back_z) | copy-start | bytes 196612
  231.4 308.8 %copy-start.5 = (f32[128,128]{1,0:T(8,128)}, f32[128,128]{1,0:T(8,128)S(1)}, u32[]{:S(2)}) copy-start(f32[128,128]{1,0:T(8,128)S(1)} %get-tuple-element.44.back_z) | copy-start | bytes 196612
  263.3 31.5 %collective-permute-start.2 = (f32[16,30,8,128]{3,2,1,0:T(8,128)}, f32[16,30,8,128]{3,2,1,0:T(8,128)S(1)}, u32[]{:S(2)}, u32[]{:S(2)}) collective-permute-start(f32[16,30,8,128]{3,2,1,0:T(8,128)} %get-tuple-element.23), channel_id=1, source_target_pairs={{0,1},{1,2},{2,3},{3,7},{7,6},{6,5},{5,4},{4,8},{8,9},{9,10},{10,1... | collective-permute-start | bytes 5898248 | tf_op jit(solution)/shard_map/ppermute | solution.py:359
  266.8 37.5 %collective-permute-start.3 = (f32[16,30,8,128]{3,2,1,0:T(8,128)}, f32[16,30,8,128]{3,2,1,0:T(8,128)}, u32[]{:S(2)}, u32[]{:S(2)}) collective-permute-start(f32[16,30,8,128]{3,2,1,0:T(8,128)} %get-tuple-element.25.rest_0_), channel_id=1, source_target_pairs={{1,0},{2,1},{3,2},{7,3},{6,7},{5,6},{4,5},{8,4},{9,8},{10,9},{11,1... | collective-permute-start | bytes 5898248 | tf_op jit(solution)/shard_map/ppermute | solution.py:360
  294.8 9.5 %copy-start.1 = (f32[16,30,8,128]{3,2,1,0:T(8,128)}, f32[16,30,8,128]{3,2,1,0:T(8,128)S(1)}, u32[]{:S(2)}) copy-start(f32[16,30,8,128]{3,2,1,0:T(8,128)S(1)} %collective-permute-done.2.above.refs_1_) | copy-start | bytes 5898244
  304.3 34.7 %copy-start.15 = (s32[96,128]{1,0:T(8,128)S(1)}, s32[96,128]{1,0:T(8,128)}, u32[]{:S(2)}) copy-start(s32[96,128]{1,0:T(8,128)} %constant.29.clone) | copy-start | bytes 147460
  304.3 113.7 %all-to-all-start.3 = ((f32[16,64,8,128]{3,2,1,0:T(8,128)}), f32[16,64,8,128]{3,2,1,0:T(8,128)}, u32[]{:S(2)}, u32[]{:S(2)}) async-start(f32[16,64,8,128]{3,2,1,0:T(8,128)} %gate.5), calls=%async_computation.3 | async-start | bytes 8388608 | tf_op jit(solution)/shard_map/all_to_all | solution.py:322
  373.5 36.6 %collective-permute-start.4 = (f32[16,30,8,128]{3,2,1,0:T(8,128)}, f32[16,30,8,128]{3,2,1,0:T(8,128)S(1)}, u32[]{:S(2)}, u32[]{:S(2)}) collective-permute-start(f32[16,30,8,128]{3,2,1,0:T(8,128)} %get-tuple-element.27), channel_id=1, source_target_pairs={{0,1},{1,2},{2,3},{3,7},{7,6},{6,5},{5,4},{4,8},{8,9},{9,10},{10,1... | collective-permute-start | bytes 5898248 | tf_op jit(solution)/shard_map/ppermute | solution.py:359
  377.0 41.0 %collective-permute-start.5 = (f32[16,30,8,128]{3,2,1,0:T(8,128)}, f32[16,30,8,128]{3,2,1,0:T(8,128)}, u32[]{:S(2)}, u32[]{:S(2)}) collective-permute-start(f32[16,30,8,128]{3,2,1,0:T(8,128)} %get-tuple-element.29.rest_0_), channel_id=1, source_target_pairs={{1,0},{2,1},{3,2},{7,3},{6,7},{5,6},{4,5},{8,4},{9,8},{10,9},{11,1... | collective-permute-start | bytes 5898248 | tf_op jit(solution)/shard_map/ppermute | solution.py:360
  410.1 7.9 %copy-start.2 = (f32[16,30,8,128]{3,2,1,0:T(8,128)}, f32[16,30,8,128]{3,2,1,0:T(8,128)S(1)}, u32[]{:S(2)}) copy-start(f32[16,30,8,128]{3,2,1,0:T(8,128)S(1)} %collective-permute-done.4.above.refs_1_) | copy-start | bytes 5898244
  418.1 109.1 %all-to-all-start.4 = ((f32[16,40,8,128]{3,2,1,0:T(8,128)}), f32[16,40,8,128]{3,2,1,0:T(8,128)S(1)}, u32[]{:S(2)}, u32[]{:S(2)}) async-start(f32[16,40,8,128]{3,2,1,0:T(8,128)} %gate.6), calls=%async_computation.4 | async-start | bytes 5242880 | tf_op jit(solution)/shard_map/all_to_all | solution.py:322
  490.7 28.9 %collective-permute-start.6 = (f32[16,30,8,128]{3,2,1,0:T(8,128)}, f32[16,30,8,128]{3,2,1,0:T(8,128)}, u32[]{:S(2)}, u32[]{:S(2)}) collective-permute-start(f32[16,30,8,128]{3,2,1,0:T(8,128)} %get-tuple-element.31), channel_id=1, source_target_pairs={{0,1},{1,2},{2,3},{3,7},{7,6},{6,5},{5,4},{4,8},{8,9},{9,10},{10,1... | collective-permute-start | bytes 5898248 | tf_op jit(solution)/shard_map/ppermute | solution.py:359
  494.2 32.9 %collective-permute-start.7 = (f32[16,30,8,128]{3,2,1,0:T(8,128)}, f32[16,30,8,128]{3,2,1,0:T(8,128)}, u32[]{:S(2)}, u32[]{:S(2)}) collective-permute-start(f32[16,30,8,128]{3,2,1,0:T(8,128)} %get-tuple-element.33.rest_0_), channel_id=1, source_target_pairs={{1,0},{2,1},{3,2},{7,3},{6,7},{5,6},{4,5},{8,4},{9,8},{10,9},{11,1... | collective-permute-start | bytes 5898248 | tf_op jit(solution)/shard_map/ppermute | solution.py:360
  527.1 13.8 %copy-start = (f32[16,40,8,128]{3,2,1,0:T(8,128)}, f32[16,40,8,128]{3,2,1,0:T(8,128)S(1)}, u32[]{:S(2)}) copy-start(f32[16,40,8,128]{3,2,1,0:T(8,128)S(1)} %all-to-all-done.4.data) | copy-start | bytes 7864324
  527.1 51.5 %all-to-all-start.5 = ((f32[16,24,8,128]{3,2,1,0:T(8,128)}), f32[16,24,8,128]{3,2,1,0:T(8,128)}, u32[]{:S(2)}, u32[]{:S(2)}) async-start(f32[16,24,8,128]{3,2,1,0:T(8,128)} %gate.7), calls=%async_computation.5 | async-start | bytes 3145728 | tf_op jit(solution)/shard_map/all_to_all | solution.py:322
  540.9 36.9 %copy-start.16 = (s32[64,96]{1,0:T(8,128)S(1)}, s32[64,96]{1,0:T(8,128)}, u32[]{:S(2)}) copy-start(s32[64,96]{1,0:T(8,128)} %constant.30.clone) | copy-start | bytes 73732
  572.3 14.9 %collective-permute-start.8 = (f32[16,15,8,128]{3,2,1,0:T(8,128)}, f32[16,15,8,128]{3,2,1,0:T(8,128)S(1)}, u32[]{:S(2)}, u32[]{:S(2)}) collective-permute-start(f32[16,15,8,128]{3,2,1,0:T(8,128)} %get-tuple-element.35), channel_id=1, source_target_pairs={{0,1},{1,2},{2,3},{3,7},{7,6},{6,5},{5,4},{4,8},{8,9},{9,10},{10,1... | collective-permute-start | bytes 2949128 | tf_op jit(solution)/shard_map/ppermute | solution.py:359
  575.8 15.6 %collective-permute-start.9 = (f32[16,15,8,128]{3,2,1,0:T(8,128)}, f32[16,15,8,128]{3,2,1,0:T(8,128)S(1)}, u32[]{:S(2)}, u32[]{:S(2)}) collective-permute-start(f32[16,15,8,128]{3,2,1,0:T(8,128)} %get-tuple-element.36), channel_id=1, source_target_pairs={{1,0},{2,1},{3,2},{7,3},{6,7},{5,6},{4,5},{8,4},{9,8},{10,9},{11,1... | collective-permute-start | bytes 2949128 | tf_op jit(solution)/shard_map/ppermute | solution.py:360
  587.2 4.3 copy-start.6
  591.5 1.0 copy-start.7

commit v5 on v4

--- a/solution.py
+++ b/solution.py
@@ -396,7 +396,7 @@
     def matrices(v):
         return blur_x[v], columns[v], depths[v].T, columns[v].T, depths[v]
 
-    outer = 5 * rows // 16
+    outer = 9 * rows // 32
     split = outer >= margin + 1 and outer % 2 == 0 and views > 1
     ends = tuple(r for r in every if r < outer or r >= rows - outer)
     inside = tuple(r for r in every if outer <= r < rows - outer)

time: 705 us -> 700 us (level)
  no operation moved by 1% of the time
where the time goes in v5:
time: 700 us; the launch traced here: 698 us
  waiting for transfers between devices  217 us (31%)
  Pallas kernels  175 us (25%)
  starting transfers between devices  167 us (24%)
  blocking collectives  99.2 us (14%)
  local copies, waits for them, and re-layouts  21.9 us (3%)
  other arithmetic  18.2 us (3%)
    all_to_all x6, starting transfers between devices, to_pencils(): lax.all_to_all(blocks, 'slab', split_axis=0, concat_axis=0, tiled=True)  139 us
    all_to_all x1, blocking collectives, to_planes(): lax.all_to_all(pencils, 'slab', split_axis=0, concat_axis=0, tiled=True)  99.2 us
    ppermute x5, waiting for transfers between devices, halos(): above.insert(0, lax.ppermute(tail[:, rows - size:], 'slab', forth))  95.5 us
    all_to_all x6, waiting for transfers between devices, to_pencils(): lax.all_to_all(blocks, 'slab', split_axis=0, concat_axis=0, tiled=True)  93.7 us
    pallas_call x2, Pallas kernels, body(): call(view_kernel, 'view', 33, (volume(extent), volume(rows), end, end), [...  66.7 us
    pallas_call x6, Pallas kernels, to_pencils(): pl.pallas_call(functools.partial(turn_kernel, run, chosen), grid=(count /...  32.8 us
    pallas_call x1, Pallas kernels, body(): call(functools.partial(last_kernel, margin), 'last', 30, tuple(outs), [WH...  29.8 us
    ppermute x5, waiting for transfers between devices, halos(): below.append(lax.ppermute(head[:, :size], 'slab', back))  27.5 us
  transfers between devices with their start and end apart: 16, of which 12 were waited for; matrix products, arithmetic and copies ran while one was open for 5% of the time, Pallas kernels for 22%

profile of v5, /device:TPU:1, one launch (start us, length us, event | category | flops | bytes accessed | tf_op | source)
XLA Modules:
  0.0 697.9 jit_solution(5200017220423887467)
XLA Ops:
  0.0 5.8 turn.6
  5.8 7.3 %all-to-all-start = ((f32[16,64,8,128]{3,2,1,0:T(8,128)}), f32[16,64,8,128]{3,2,1,0:T(8,128)}, u32[]{:S(2)}, u32[]{:S(2)}) async-start(f32[16,64,8,128]{3,2,1,0:T(8,128)} %turn.6), calls=%async_computation | async-start | bytes 8388608 | tf_op jit(solution)/shard_map/all_to_all | solution.py:322
  13.1 12.2 %slice_bitcast_fusion = (f32[8,1024,128]{2,1,0:T(8,128)}, f32[8,1024,128]{2,1,0:T(8,128)}, f32[8,1024,128]{2,1,0:T(8,128)}, f32[8,1024,128]{2,1,0:T(8,128)}) fusion(f32[4,8,1024,128]{3,2,1,0:T(8,128)} %param.13), kind=kLoop, calls=%fused_computation.5 | loop fusion | bytes 33554432 | tf_op jit(solution)/shard_map/squeeze | solution.py:409
  25.3 5.8 turn.7
  31.2 60.1 %all-to-all-done.own = f32[16,64,8,128]{3,2,1,0:T(8,128)} async-done(((f32[16,64,8,128]{3,2,1,0:T(8,128)}), f32[16,64,8,128]{3,2,1,0:T(8,128)}, u32[]{:S(2)}, u32[]{:S(2)}) %all-to-all-start) | async-done | bytes 4194336 | tf_op jit(solution)/shard_map/all_to_all | solution.py:322
  91.2 19.3 %all-to-all-start.1 = ((f32[16,64,8,128]{3,2,1,0:T(8,128)}), f32[16,64,8,128]{3,2,1,0:T(8,128)}, u32[]{:S(2)}, u32[]{:S(2)}) async-start(f32[16,64,8,128]{3,2,1,0:T(8,128)} %turn.7), calls=%async_computation.1 | async-start | bytes 8388608 | tf_op jit(solution)/shard_map/all_to_all | solution.py:322
  110.5 1.6 fusion.2
  112.1 3.5 collective-permute-start
  115.7 1.9 collective-permute-start.1
  117.6 5.9 turn.8.refs_0_
  123.5 26.4 %collective-permute-done.above.refs_1_ = f32[16,15,8,128]{3,2,1,0:T(8,128)S(1)} collective-permute-done((f32[16,15,8,128]{3,2,1,0:T(8,128)S(1)}, f32[16,15,8,128]{3,2,1,0:T(8,128)S(1)}, u32[]{:S(2)}, u32[]{:S(2)}) %collective-permute-start) | collective-permute-done | bytes 983072 | tf_op jit(solution)/shard_map/ppermute | solution.py:359
  149.8 4.2 collective-permute-done.1.below.refs_2_
  154.0 0.9 copy-done.4
  155.0 33.7 %all-to-all-done.1.data = f32[16,64,8,128]{3,2,1,0:T(8,128)} async-done(((f32[16,64,8,128]{3,2,1,0:T(8,128)}), f32[16,64,8,128]{3,2,1,0:T(8,128)}, u32[]{:S(2)}, u32[]{:S(2)}) %all-to-all-start.1) | async-done | bytes 4194336 | tf_op jit(solution)/shard_map/all_to_all | solution.py:322
  188.6 30.5 %all-to-all-start.2 = ((f32[16,64,8,128]{3,2,1,0:T(8,128)}), f32[16,64,8,128]{3,2,1,0:T(8,128)}, u32[]{:S(2)}, u32[]{:S(2)}) async-start(f32[16,64,8,128]{3,2,1,0:T(8,128)} %gate.4), calls=%async_computation.2 | async-start | bytes 8388608 | tf_op jit(solution)/shard_map/all_to_all | solution.py:322
  219.1 0.7 slice_reduce_fusion.1
  219.8 2.5 divide_bitcast_fusion.7
  222.8 1.0 select_reduce_fusion.4
  223.8 0.7 copy.32
  225.2 2.5 divide_bitcast_fusion.6
  227.7 3.7 select_reduce_fusion
  231.4 0.7 copy.31
  232.7 1.2 broadcast_divide_fusion
  233.9 2.4 broadcast_divide_fusion.5
  236.3 1.1 select_reduce_fusion.11
  237.4 25.9 %first.1 = (f32[16,96,8,128]{3,2,1,0:T(8,128)}, f32[16,64,8,128]{3,2,1,0:T(8,128)}, f32[16,30,8,128]{3,2,1,0:T(8,128)}, f32[16,30,8,128]{3,2,1,0:T(8,128)}) custom-call(f32[64,96]{1,0:T(8,128)} %get-tuple-element.52.blur_x, f32[128,128]{1,0:T(8,128)} %copy-done.13, f32[128,128]{1,0:T(8,128)} %bitcast.56, f32[128,128]{1,0:T(8,128)} %bitcast.55, ...), custom_call_target="tpu_custom_call" | custom-call | bytes 93600000 | tf_op jit(solution)/shard_map/first/pallas_call | solution.py:411
  263.3 3.5 collective-permute-start.2
  266.8 1.9 collective-permute-start.3
  268.8 5.9 turn.9.refs_0_
  274.6 20.2 %collective-permute-done.2.above.refs_1_ = f32[16,30,8,128]{3,2,1,0:T(8,128)S(1)} collective-permute-done((f32[16,30,8,128]{3,2,1,0:T(8,128)}, f32[16,30,8,128]{3,2,1,0:T(8,128)S(1)}, u32[]{:S(2)}, u32[]{:S(2)}) %collective-permute-start.2) | collective-permute-done | bytes 1966112 | tf_op jit(solution)/shard_map/ppermute | solution.py:359
  294.8 9.5 %collective-permute-done.3.below.refs_2_ = f32[16,30,8,128]{3,2,1,0:T(8,128)} collective-permute-done((f32[16,30,8,128]{3,2,1,0:T(8,128)}, f32[16,30,8,128]{3,2,1,0:T(8,128)}, u32[]{:S(2)}, u32[]{:S(2)}) %collective-permute-start.3) | collective-permute-done | bytes 1966112 | tf_op jit(solution)/shard_map/ppermute | solution.py:360
  304.3 33.2 %all-to-all-start.3 = ((f32[16,64,8,128]{3,2,1,0:T(8,128)}), f32[16,64,8,128]{3,2,1,0:T(8,128)}, u32[]{:S(2)}, u32[]{:S(2)}) async-start(f32[16,64,8,128]{3,2,1,0:T(8,128)} %gate.5), calls=%async_computation.3 | async-start | bytes 8388608 | tf_op jit(solution)/shard_map/all_to_all | solution.py:322
  337.6 0.7 copy.30
  338.3 0.7 copy.29
  339.0 1.1 select_reduce_fusion.8
  340.1 33.3 %view.2 = (f32[16,96,8,128]{3,2,1,0:T(8,128)}, f32[16,64,8,128]{3,2,1,0:T(8,128)}, f32[16,30,8,128]{3,2,1,0:T(8,128)}, f32[16,30,8,128]{3,2,1,0:T(8,128)}) custom-call(f32[96,128]{1,0:T(8,128)} %get-tuple-element.49.spread_x, f32[64,96]{1,0:T(8,128)} %get-tuple-element.53.blur_x, f32[128,128]{1,0:T(8,128)} %copy-done.11, f32[128,128]{1,0:T(8,128)} %bitcast.51, ...), custom_call_target="tpu_custom_call" | custom-call | bytes 118800000 | tf_op jit(solution)/shard_map/view/pallas_call | solution.py:423
  373.5 3.5 collective-permute-start.4
  377.0 1.9 collective-permute-start.5
  378.9 4.9 turn.10.refs_0_
  383.8 26.3 %collective-permute-done.4.above.refs_1_ = f32[16,30,8,128]{3,2,1,0:T(8,128)S(1)} collective-permute-done((f32[16,30,8,128]{3,2,1,0:T(8,128)}, f32[16,30,8,128]{3,2,1,0:T(8,128)S(1)}, u32[]{:S(2)}, u32[]{:S(2)}) %collective-permute-start.4) | collective-permute-done | bytes 1966112 | tf_op jit(solution)/shard_map/ppermute | solution.py:359
  410.1 7.9 %collective-permute-done.5.below.refs_2_ = f32[16,30,8,128]{3,2,1,0:T(8,128)} collective-permute-done((f32[16,30,8,128]{3,2,1,0:T(8,128)}, f32[16,30,8,128]{3,2,1,0:T(8,128)}, u32[]{:S(2)}, u32[]{:S(2)}) %collective-permute-start.5) | collective-permute-done | bytes 1966112 | tf_op jit(solution)/shard_map/ppermute | solution.py:360
  418.1 37.8 %all-to-all-start.4 = ((f32[16,36,8,128]{3,2,1,0:T(8,128)}), f32[16,36,8,128]{3,2,1,0:T(8,128)S(1)}, u32[]{:S(2)}, u32[]{:S(2)}) async-start(f32[16,36,8,128]{3,2,1,0:T(8,128)} %gate.6), calls=%async_computation.4 | async-start | bytes 4718592 | tf_op jit(solution)/shard_map/all_to_all | solution.py:322
  455.9 0.7 copy.28
  456.6 0.7 copy.27
  457.3 33.4 %view.3 = (f32[16,96,8,128]{3,2,1,0:T(8,128)}, f32[16,64,8,128]{3,2,1,0:T(8,128)}, f32[16,30,8,128]{3,2,1,0:T(8,128)}, f32[16,30,8,128]{3,2,1,0:T(8,128)}) custom-call(f32[96,128]{1,0:T(8,128)} %get-tuple-element.50.spread_x, f32[64,96]{1,0:T(8,128)} %get-tuple-element.54.blur_x, f32[128,128]{1,0:T(8,128)} %copy-done.9, f32[128,128]{1,0:T(8,128)} %bitcast.54, ...), custom_call_target="tpu_custom_call" | custom-call | bytes 118800000 | tf_op jit(solution)/shard_map/view/pallas_call | solution.py:423
  490.7 3.5 collective-permute-start.6
  494.2 2.0 collective-permute-start.7
  496.3 4.6 turn.11.refs_0_
  500.9 18.4 %collective-permute-done.6.above.refs_1_ = f32[16,30,8,128]{3,2,1,0:T(8,128)} collective-permute-done((f32[16,30,8,128]{3,2,1,0:T(8,128)}, f32[16,30,8,128]{3,2,1,0:T(8,128)}, u32[]{:S(2)}, u32[]{:S(2)}) %collective-permute-start.6) | collective-permute-done | bytes 1966112 | tf_op jit(solution)/shard_map/ppermute | solution.py:359
  519.3 3.3 collective-permute-done.7.below.refs_2_
  522.6 11.1 %all-to-all-start.5 = ((f32[16,28,8,128]{3,2,1,0:T(8,128)}), f32[16,28,8,128]{3,2,1,0:T(8,128)}, u32[]{:S(2)}, u32[]{:S(2)}) async-start(f32[16,28,8,128]{3,2,1,0:T(8,128)} %gate.7), calls=%async_computation.5 | async-start | bytes 3670016 | tf_op jit(solution)/shard_map/all_to_all | solution.py:322
  533.8 0.7 copy.26
  534.5 0.7 copy.25
  535.2 29.8 %last.1 = (f32[16,64,8,128]{3,2,1,0:T(8,128)}, f32[16,28,8,128]{3,2,1,0:T(8,128)}, f32[16,18,8,128]{3,2,1,0:T(8,128)}, f32[16,18,8,128]{3,2,1,0:T(8,128)}, f32[1...) custom-call(f32[96,128]{1,0:T(8,128)} %get-tuple-element.51.spread_x, f32[64,96]{1,0:T(8,128)} %get-tuple-element.55.blur_x, ...), custom_call_target="tpu_custom_call" | custom-call | bytes 108000000 | tf_op jit(solution)/shard_map/last/pallas_call | solution.py:418
  565.0 3.5 collective-permute-start.8
  568.5 1.9 collective-permute-start.9
  570.5 0.8 select_reduce_fusion.15.spread_x
  571.3 6.1 middle.1.rest_1_
  577.3 4.3 collective-permute-done.8.above
  581.6 2.5 collective-permute-done.9.below
  584.2 0.9 copy-done.7
  585.1 8.6 %finish.1 = f32[16,64,8,128]{3,2,1,0:T(8,128)} custom-call(f32[64,96]{1,0:T(8,128)} %select_reduce_fusion.15.spread_x, f32[16,15,8,128]{3,2,1,0:T(8,128)} %copy-done.6, f32[16,15,8,128]{3,2,1,0:T(8,128)} %copy-done.7, f32[16,64,8,128]{3,2,1,0:T(8,128)} %get-tuple-element.37.current, f32[16,18,8,128]{3,2,1,0:T(8,128)} %get-tuple-element.38.rest_0_, ...), custom_call_target="tpu_custom_call" | custom-call | bytes 28800000 | tf_op jit(solution)/shard_map/finish/pallas_call | solution.py:241
  593.7 99.2 %all_to_all.35.source = f32[16,64,8,128]{3,2,1,0:T(8,128)} all-to-all(f32[16,64,8,128]{3,2,1,0:T(8,128)} %finish.1), channel_id=1, replica_groups=mesh['groups'=2,'slab'=16] {'slab'}, dimensions={0} | all-to-all | bytes 8388608 | tf_op jit(solution)/shard_map/all_to_all | solution.py:333
  693.0 4.9 turn_back.1
  (54 shorter events, 1.7 us)
Async XLA Ops:
  5.8 85.4 %all-to-all-start = ((f32[16,64,8,128]{3,2,1,0:T(8,128)}), f32[16,64,8,128]{3,2,1,0:T(8,128)}, u32[]{:S(2)}, u32[]{:S(2)}) async-start(f32[16,64,8,128]{3,2,1,0:T(8,128)} %turn.6), calls=%async_computation | async-start | bytes 8388608 | tf_op jit(solution)/shard_map/all_to_all | solution.py:322
  91.2 97.4 %all-to-all-start.1 = ((f32[16,64,8,128]{3,2,1,0:T(8,128)}), f32[16,64,8,128]{3,2,1,0:T(8,128)}, u32[]{:S(2)}, u32[]{:S(2)}) async-start(f32[16,64,8,128]{3,2,1,0:T(8,128)} %turn.7), calls=%async_computation.1 | async-start | bytes 8388608 | tf_op jit(solution)/shard_map/all_to_all | solution.py:322
  112.1 37.7 %collective-permute-start = (f32[16,15,8,128]{3,2,1,0:T(8,128)S(1)}, f32[16,15,8,128]{3,2,1,0:T(8,128)S(1)}, u32[]{:S(2)}, u32[]{:S(2)}) collective-permute-start(f32[16,15,8,128]{3,2,1,0:T(8,128)S(1)} %get-tuple-element.73), channel_id=1, source_target_pairs={{0,1},{1,2},{2,3},{3,7},{7,6},{6,5},{5,4},{4,8},{8,9},{9,10},{10,1... | collective-permute-start | bytes 2949128 | tf_op jit(solution)/shard_map/ppermute | solution.py:359
  115.7 38.3 %collective-permute-start.1 = (f32[16,15,8,128]{3,2,1,0:T(8,128)S(1)}, f32[16,15,8,128]{3,2,1,0:T(8,128)S(1)}, u32[]{:S(2)}, u32[]{:S(2)}) collective-permute-start(f32[16,15,8,128]{3,2,1,0:T(8,128)S(1)} %get-tuple-element.72), channel_id=1, source_target_pairs={{1,0},{2,1},{3,2},{7,3},{6,7},{5,6},{4,5},{8,4},{9,8},{10,9},{11,1... | collective-permute-start | bytes 2949128 | tf_op jit(solution)/shard_map/ppermute | solution.py:360
  149.8 4.2 copy-start.3
  154.0 0.9 copy-start.4
  155.0 64.1 %copy-start.18 = (f32[4,2,31]{2,1,0:T(2,128)S(1)}, f32[4,2,31]{2,1,0:T(2,128)}, u32[]{:S(2)}) copy-start(f32[4,2,31]{2,1,0:T(2,128)} %param.14) | copy-start | bytes 2980
  155.0 69.6 %copy-start.19 = (f32[4,101]{1,0:T(4,128)S(1)}, f32[4,101]{1,0:T(4,128)}, u32[]{:S(2)}) copy-start(f32[4,101]{1,0:T(4,128)} %param.15) | copy-start | bytes 4852
  155.0 81.3 %copy-start.17 = (s32[64,96]{1,0:T(8,128)S(1)}, s32[64,96]{1,0:T(8,128)}, u32[]{:S(2)}) copy-start(s32[64,96]{1,0:T(8,128)} %constant.28.clone) | copy-start | bytes 73732
  188.6 115.7 %all-to-all-start.2 = ((f32[16,64,8,128]{3,2,1,0:T(8,128)}), f32[16,64,8,128]{3,2,1,0:T(8,128)}, u32[]{:S(2)}, u32[]{:S(2)}) async-start(f32[16,64,8,128]{3,2,1,0:T(8,128)} %gate.4), calls=%async_computation.2 | async-start | bytes 8388608 | tf_op jit(solution)/shard_map/all_to_all | solution.py:322
  223.8 13.6 %copy-start.13 = (f32[128,128]{1,0:T(8,128)}, f32[128,128]{1,0:T(8,128)S(1)}, u32[]{:S(2)}) copy-start(f32[128,128]{1,0:T(8,128)S(1)} %get-tuple-element.45.blur_y) | copy-start | bytes 196612
  223.8 113.8 %copy-start.11 = (f32[128,128]{1,0:T(8,128)}, f32[128,128]{1,0:T(8,128)S(1)}, u32[]{:S(2)}) copy-start(f32[128,128]{1,0:T(8,128)S(1)} %get-tuple-element.46.blur_y) | copy-start | bytes 196612
  223.8 232.1 %copy-start.9 = (f32[128,128]{1,0:T(8,128)}, f32[128,128]{1,0:T(8,128)S(1)}, u32[]{:S(2)}) copy-start(f32[128,128]{1,0:T(8,128)S(1)} %get-tuple-element.47.blur_y) | copy-start | bytes 196612
  223.8 310.0 %copy-start.8 = (f32[128,128]{1,0:T(8,128)}, f32[128,128]{1,0:T(8,128)S(1)}, u32[]{:S(2)}) copy-start(f32[128,128]{1,0:T(8,128)S(1)} %get-tuple-element.48.blur_y) | copy-start | bytes 196612
  231.4 6.0 copy-start.14
  231.4 106.9 %copy-start.12 = (f32[128,128]{1,0:T(8,128)}, f32[128,128]{1,0:T(8,128)S(1)}, u32[]{:S(2)}) copy-start(f32[128,128]{1,0:T(8,128)S(1)} %get-tuple-element.42.back_z) | copy-start | bytes 196612
  231.4 225.2 %copy-start.10 = (f32[128,128]{1,0:T(8,128)}, f32[128,128]{1,0:T(8,128)S(1)}, u32[]{:S(2)}) copy-start(f32[128,128]{1,0:T(8,128)S(1)} %get-tuple-element.43.back_z) | copy-start | bytes 196612
  231.4 303.1 %copy-start.5 = (f32[128,128]{1,0:T(8,128)}, f32[128,128]{1,0:T(8,128)S(1)}, u32[]{:S(2)}) copy-start(f32[128,128]{1,0:T(8,128)S(1)} %get-tuple-element.44.back_z) | copy-start | bytes 196612
  263.3 31.5 %collective-permute-start.2 = (f32[16,30,8,128]{3,2,1,0:T(8,128)}, f32[16,30,8,128]{3,2,1,0:T(8,128)S(1)}, u32[]{:S(2)}, u32[]{:S(2)}) collective-permute-start(f32[16,30,8,128]{3,2,1,0:T(8,128)} %get-tuple-element.23), channel_id=1, source_target_pairs={{0,1},{1,2},{2,3},{3,7},{7,6},{6,5},{5,4},{4,8},{8,9},{9,10},{10,1... | collective-permute-start | bytes 5898248 | tf_op jit(solution)/shard_map/ppermute | solution.py:359
  266.8 37.5 %collective-permute-start.3 = (f32[16,30,8,128]{3,2,1,0:T(8,128)}, f32[16,30,8,128]{3,2,1,0:T(8,128)}, u32[]{:S(2)}, u32[]{:S(2)}) collective-permute-start(f32[16,30,8,128]{3,2,1,0:T(8,128)} %get-tuple-element.25.rest_0_), channel_id=1, source_target_pairs={{1,0},{2,1},{3,2},{7,3},{6,7},{5,6},{4,5},{8,4},{9,8},{10,9},{11,1... | collective-permute-start | bytes 5898248 | tf_op jit(solution)/shard_map/ppermute | solution.py:360
  294.8 9.5 %copy-start.1 = (f32[16,30,8,128]{3,2,1,0:T(8,128)}, f32[16,30,8,128]{3,2,1,0:T(8,128)S(1)}, u32[]{:S(2)}) copy-start(f32[16,30,8,128]{3,2,1,0:T(8,128)S(1)} %collective-permute-done.2.above.refs_1_) | copy-start | bytes 5898244
  304.3 34.7 %copy-start.15 = (s32[96,128]{1,0:T(8,128)S(1)}, s32[96,128]{1,0:T(8,128)}, u32[]{:S(2)}) copy-start(s32[96,128]{1,0:T(8,128)} %constant.29.clone) | copy-start | bytes 147460
  304.3 113.7 %all-to-all-start.3 = ((f32[16,64,8,128]{3,2,1,0:T(8,128)}), f32[16,64,8,128]{3,2,1,0:T(8,128)}, u32[]{:S(2)}, u32[]{:S(2)}) async-start(f32[16,64,8,128]{3,2,1,0:T(8,128)} %gate.5), calls=%async_computation.3 | async-start | bytes 8388608 | tf_op jit(solution)/shard_map/all_to_all | solution.py:322
  373.5 36.6 %collective-permute-start.4 = (f32[16,30,8,128]{3,2,1,0:T(8,128)}, f32[16,30,8,128]{3,2,1,0:T(8,128)S(1)}, u32[]{:S(2)}, u32[]{:S(2)}) collective-permute-start(f32[16,30,8,128]{3,2,1,0:T(8,128)} %get-tuple-element.27), channel_id=1, source_target_pairs={{0,1},{1,2},{2,3},{3,7},{7,6},{6,5},{5,4},{4,8},{8,9},{9,10},{10,1... | collective-permute-start | bytes 5898248 | tf_op jit(solution)/shard_map/ppermute | solution.py:359
  377.0 41.0 %collective-permute-start.5 = (f32[16,30,8,128]{3,2,1,0:T(8,128)}, f32[16,30,8,128]{3,2,1,0:T(8,128)}, u32[]{:S(2)}, u32[]{:S(2)}) collective-permute-start(f32[16,30,8,128]{3,2,1,0:T(8,128)} %get-tuple-element.29.rest_0_), channel_id=1, source_target_pairs={{1,0},{2,1},{3,2},{7,3},{6,7},{5,6},{4,5},{8,4},{9,8},{10,9},{11,1... | collective-permute-start | bytes 5898248 | tf_op jit(solution)/shard_map/ppermute | solution.py:360
  410.1 7.9 %copy-start.2 = (f32[16,30,8,128]{3,2,1,0:T(8,128)}, f32[16,30,8,128]{3,2,1,0:T(8,128)S(1)}, u32[]{:S(2)}) copy-start(f32[16,30,8,128]{3,2,1,0:T(8,128)S(1)} %collective-permute-done.4.above.refs_1_) | copy-start | bytes 5898244
  418.1 104.6 %all-to-all-start.4 = ((f32[16,36,8,128]{3,2,1,0:T(8,128)}), f32[16,36,8,128]{3,2,1,0:T(8,128)S(1)}, u32[]{:S(2)}, u32[]{:S(2)}) async-start(f32[16,36,8,128]{3,2,1,0:T(8,128)} %gate.6), calls=%async_computation.4 | async-start | bytes 4718592 | tf_op jit(solution)/shard_map/all_to_all | solution.py:322
  490.7 28.6 %collective-permute-start.6 = (f32[16,30,8,128]{3,2,1,0:T(8,128)}, f32[16,30,8,128]{3,2,1,0:T(8,128)}, u32[]{:S(2)}, u32[]{:S(2)}) collective-permute-start(f32[16,30,8,128]{3,2,1,0:T(8,128)} %get-tuple-element.31), channel_id=1, source_target_pairs={{0,1},{1,2},{2,3},{3,7},{7,6},{6,5},{5,4},{4,8},{8,9},{9,10},{10,1... | collective-permute-start | bytes 5898248 | tf_op jit(solution)/shard_map/ppermute | solution.py:359
  494.2 28.4 %collective-permute-start.7 = (f32[16,30,8,128]{3,2,1,0:T(8,128)}, f32[16,30,8,128]{3,2,1,0:T(8,128)}, u32[]{:S(2)}, u32[]{:S(2)}) collective-permute-start(f32[16,30,8,128]{3,2,1,0:T(8,128)} %get-tuple-element.33.rest_0_), channel_id=1, source_target_pairs={{1,0},{2,1},{3,2},{7,3},{6,7},{5,6},{4,5},{8,4},{9,8},{10,9},{11,1... | collective-permute-start | bytes 5898248 | tf_op jit(solution)/shard_map/ppermute | solution.py:360
  522.6 12.6 %copy-start = (f32[16,36,8,128]{3,2,1,0:T(8,128)}, f32[16,36,8,128]{3,2,1,0:T(8,128)S(1)}, u32[]{:S(2)}) copy-start(f32[16,36,8,128]{3,2,1,0:T(8,128)S(1)} %all-to-all-done.4.data) | copy-start | bytes 7077892
  522.6 48.6 %all-to-all-start.5 = ((f32[16,28,8,128]{3,2,1,0:T(8,128)}), f32[16,28,8,128]{3,2,1,0:T(8,128)}, u32[]{:S(2)}, u32[]{:S(2)}) async-start(f32[16,28,8,128]{3,2,1,0:T(8,128)} %gate.7), calls=%async_computation.5 | async-start | bytes 3670016 | tf_op jit(solution)/shard_map/all_to_all | solution.py:322
  535.2 35.3 %copy-start.16 = (s32[64,96]{1,0:T(8,128)S(1)}, s32[64,96]{1,0:T(8,128)}, u32[]{:S(2)}) copy-start(s32[64,96]{1,0:T(8,128)} %constant.30.clone) | copy-start | bytes 73732
  565.0 16.6 %collective-permute-start.8 = (f32[16,15,8,128]{3,2,1,0:T(8,128)}, f32[16,15,8,128]{3,2,1,0:T(8,128)S(1)}, u32[]{:S(2)}, u32[]{:S(2)}) collective-permute-start(f32[16,15,8,128]{3,2,1,0:T(8,128)} %get-tuple-element.35), channel_id=1, source_target_pairs={{0,1},{1,2},{2,3},{3,7},{7,6},{6,5},{5,4},{4,8},{8,9},{9,10},{10,1... | collective-permute-start | bytes 2949128 | tf_op jit(solution)/shard_map/ppermute | solution.py:359
  568.5 15.6 %collective-permute-start.9 = (f32[16,15,8,128]{3,2,1,0:T(8,128)}, f32[16,15,8,128]{3,2,1,0:T(8,128)S(1)}, u32[]{:S(2)}, u32[]{:S(2)}) collective-permute-start(f32[16,15,8,128]{3,2,1,0:T(8,128)} %get-tuple-element.36), channel_id=1, source_target_pairs={{1,0},{2,1},{3,2},{7,3},{6,7},{5,6},{4,5},{8,4},{9,8},{10,9},{11,1... | collective-permute-start | bytes 2949128 | tf_op jit(solution)/shard_map/ppermute | solution.py:360
  581.6 2.6 copy-start.6
  584.2 0.9 copy-start.7

commit v6 on v5

--- a/solution.py
+++ b/solution.py
@@ -91,8 +91,9 @@
     return -(-size // 16) * 16
 
 
-def along_x(groups, matrix, emit):
-    blocks, _, planes, width = groups[0][0].shape
+def along_x(groups, matrix, emit, first=0, blocks=None):
+    _, _, planes, width = groups[0][0].shape
+    blocks = groups[0][0].shape[0] if blocks is None else blocks
     left_high, left_low = halves(matrix)
     left = jnp.concatenate([left_high, left_low], axis=0)
     left = jnp.concatenate([left, left], axis=1)
@@ -107,7 +108,7 @@
         return jnp.concatenate(parts, axis=0)
 
     def pair(index, _):
-        block, plane = index // (planes // 2), (index % (planes // 2)) * 2
+        block, plane = first + index // (planes // 2), (index % (planes // 2)) * 2
         columns = jnp.concatenate([column(block, plane), column(block, plane + 1)], axis=1)
         product = jnp.dot(
             left, jnp.concatenate(halves(columns), axis=0), preferred_element_type=jnp.float32
@@ -221,33 +222,73 @@
     divide_yz(blurred, data, out, back_y[...], back_z[...])
 
 
-def finish_kernel(count, spread_x, above, below, current, *rest):
-    pieces, updated = rest[:count], rest[count]
+def finish_part(blocks, step, fixed, sources, targets):
+    (spread_x,), (above, below, current, *pieces), (updated,) = fixed, sources, targets
     rows = updated.shape[1]
 
     def emit(block, plane, value):
         set_x_plane(updated, block, plane, x_plane(current, block, plane) * value[:rows])
 
-    along_x([[above], pieces, [below]], spread_x[...], emit)
-
-
-def striped(kernel, name, microseconds, inputs, outs):
-    blocks = outs[0].shape[0]
-    step = 4 if blocks % 4 == 0 else 1
-
-    def spec(array):
-        return pl.BlockSpec((step,) + array.shape[1:], lambda g: (g, 0, 0, 0))
+    along_x([[above], pieces, [below]], spread_x[...], emit, step * blocks, blocks)
+
+
+def streamed(part, name, microseconds, steps, fixed, inputs, outs, cuts, after=(), spare=0):
+    counts = len(fixed), len(inputs), len(after), len(outs), len(inputs), len(outs)
+
+    def kernel(*refs):
+        groups, start = [], 0
+        for size in counts:
+            groups.append(refs[start : start + size])
+            start += size
+        held, sources, _, targets, ins, ready = groups
+        in_sem, out_sem = refs[start:]
+
+        def come(k, step):
+            cut = cuts[0](step)
+            return pltpu.make_async_copy(sources[k].at[cut], ins[k].at[cut], in_sem.at[k, step])
+
+        def go(k, step):
+            cut = cuts[1](step)
+            return pltpu.make_async_copy(ready[k].at[cut], targets[k].at[cut], out_sem.at[k, step])
+
+        def begin(step, _):
+            for k in range(len(inputs)):
+                come(k, step).start()
+            return 0
+
+        def work(step, _):
+            for k in range(len(inputs)):
+                come(k, step).wait()
+            part(step, held, ins, ready)
+            for k in range(len(outs)):
+                go(k, step).start()
+            return 0
+
+        def end(step, _):
+            for k in range(len(outs)):
+                go(k, step).wait()
+            return 0
+
+        lax.fori_loop(0, steps, begin, 0)
+        lax.fori_loop(0, steps, work, 0)
+        lax.fori_loop(0, steps, end, 0)
+
+    def scratch(array, more):
+        shape = array.shape if len(array.shape) == 4 else (array.shape[0], array.shape[1] + more, array.shape[2])
+        return pltpu.VMEM(shape, jnp.float32)
 
     return pl.pallas_call(
         kernel,
-        grid=(blocks // step,),
         out_shape=outs,
-        in_specs=[WHOLE] + [spec(array) for array in inputs[1:]],
-        out_specs=[spec(array) for array in outs],
+        in_specs=[WHOLE] * len(fixed) + [ANYWHERE] * (len(inputs) + len(after)),
+        out_specs=[ANYWHERE] * len(outs),
+        scratch_shapes=[scratch(array, spare) for array in inputs]
+        + [scratch(array, 0) for array in outs]
+        + [pltpu.SemaphoreType.DMA((len(inputs), steps)), pltpu.SemaphoreType.DMA((len(outs), steps))],
         compiler_params=pltpu.CompilerParams(vmem_limit_bytes=VMEM_LIMIT),
         cost_estimate=cost(microseconds),
         name=name,
-    )(*inputs)
+    )(*fixed, *inputs, *after)
 
 
 def call(kernel, name, microseconds, outs, in_specs, scratch=()):
@@ -263,30 +304,29 @@
     )
 
 
-def source_block(place, run):
-    return jnp.where(pl.program_id(0) % 2 == 0, place, run - 1 - place)
-
-
-def turn_kernel(run, chosen, source, *rest):
-    target = rest[-1]
+def x_rows(device, run, rows):
+    return pl.ds(pl.multiple_of(position(device, run) * rows, 8), rows)
+
+
+def turn_part(run, rows, chosen, device, _, sources, targets):
+    (source,), (target,) = sources, targets
     depth, extent, width = source.shape
     flat = source.reshape(depth * extent, width)
-    for place in range(run):
-        base = source_block(place, run) * (extent // run)
-        for place_row, row in enumerate(chosen):
-            target[place, place_row] = flat[pl.ds(base + row, depth, stride=extent), :]
-
-
-def turn_back_kernel(run, source, target):
-    _, rows, depth, width = source.shape
-    flat = source.reshape(run * rows * depth, width)
-    for place in range(run):
-        base = source_block(place, run) * rows
-        for plane in range(depth):
-            for row in range(0, rows, 8):
-                target[plane, pl.ds(pl.multiple_of(base + row, 8), 8), :] = flat[
-                    pl.ds((place * rows + row) * depth + plane, 8, stride=depth), :
-                ]
+    base = position(device, run) * rows
+    for place, row in enumerate(chosen):
+        target[device, place] = flat[pl.ds(base + row, depth, stride=extent), :]
+
+
+def turn_back_part(run, device, _, sources, targets):
+    (source,), (target,) = sources, targets
+    count, rows, depth, width = source.shape
+    flat = source.reshape(count * rows * depth, width)
+    base = position(device, run) * rows
+    for plane in range(depth):
+        for row in range(0, rows, 8):
+            target[plane, pl.ds(pl.multiple_of(base + row, 8), 8), :] = flat[
+                pl.ds((device * rows + row) * depth + plane, 8, stride=depth), :
+            ]
 
 
 def gate(blocks, arrays):
@@ -306,17 +346,18 @@
     rows = extent // count
     size = len(chosen)
     if depth % 8 == 0 and rows % 8 == 0:
-        blocks = pl.pallas_call(
-            functools.partial(turn_kernel, run, chosen),
-            grid=(count // run,),
-            out_shape=jax.ShapeDtypeStruct((count, size, depth, width), planes.dtype),
-            in_specs=[pl.BlockSpec((depth, run * rows, width), lambda g: (0, g, 0))]
-            + [ANYWHERE] * len(turn_after),
-            out_specs=pl.BlockSpec((run, size, depth, width), lambda g: (g, 0, 0, 0)),
-            compiler_params=pltpu.CompilerParams(vmem_limit_bytes=VMEM_LIMIT),
-            cost_estimate=cost(TURN_US),
-            name="turn",
-        )(planes, *turn_after)
+        (blocks,) = streamed(
+            functools.partial(turn_part, run, rows, chosen),
+            "turn",
+            TURN_US,
+            count,
+            [],
+            [planes],
+            [jax.ShapeDtypeStruct((count, size, depth, width), planes.dtype)],
+            (lambda step: (slice(None), x_rows(step, run, rows)), lambda step: (pl.ds(step, 1),)),
+            turn_after,
+            8,
+        )
         if send_after:
             blocks = gate(blocks, send_after)
         return lax.all_to_all(blocks, "slab", split_axis=0, concat_axis=0, tiled=True)
@@ -331,16 +372,16 @@
     rows, width = pencils.shape[1], pencils.shape[3]
     if depth % 8 == 0 and rows % 8 == 0:
         blocks = lax.all_to_all(pencils, "slab", split_axis=0, concat_axis=0, tiled=True)
-        return pl.pallas_call(
-            functools.partial(turn_back_kernel, run),
-            grid=(count // run,),
-            out_shape=jax.ShapeDtypeStruct((depth, rows * count, width), pencils.dtype),
-            in_specs=[pl.BlockSpec((run, rows, depth, width), lambda g: (g, 0, 0, 0))],
-            out_specs=pl.BlockSpec((depth, run * rows, width), lambda g: (0, g, 0)),
-            compiler_params=pltpu.CompilerParams(vmem_limit_bytes=VMEM_LIMIT),
-            cost_estimate=cost(TURN_US),
-            name="turn_back",
-        )(blocks)
+        return streamed(
+            functools.partial(turn_back_part, run),
+            "turn_back",
+            TURN_US,
+            count,
+            [],
+            [blocks],
+            [jax.ShapeDtypeStruct((depth, rows * count, width), pencils.dtype)],
+            (lambda step: (pl.ds(step, 1),), lambda step: (slice(None), x_rows(step, run, rows))),
+        )[0]
     order = device_order(count, run)
     blocks = pencils.swapaxes(1, 2).reshape(count, depth, rows, width)
     blocks = lax.all_to_all(blocks, "slab", split_axis=0, concat_axis=0, tiled=True)
@@ -437,12 +478,17 @@
         pieces = [first, inner, second]
     else:
         own, pieces = wide[:, margin : margin + rows], [center]
-    (current,) = striped(
-        functools.partial(finish_kernel, len(pieces)),
+    step = 2 if blocks % 2 == 0 else 1
+    cut = lambda place: (pl.ds(place * step, step),)
+    (current,) = streamed(
+        functools.partial(finish_part, step),
         "finish",
-        8,
-        [finish_x, above, below, own, *pieces],
+        7,
+        blocks // step,
+        [finish_x],
+        [above, below, own, *pieces],
         [volume(rows)],
+        (cut, cut),
     )
     return to_planes(current, count, run, depth)
 

time: 700 us -> 696 us (level)
  Pallas kernels: 175 us -> 163 us
  waiting for transfers between devices: 217 us -> 225 us
    pallas_call x8, Pallas kernels: 46.4 us -> 34.7 us  [streamed(): pl.pallas_call(kernel, out_shape=outs, in_specs=[WHOLE] * len(fixed) + [A...]
  transfers between devices with their start and end apart: 16 -> 16, of which waited for: 12 -> 12; matrix products, arithmetic and copies ran while one was open for 5% -> 5% of each run, Pallas kernels for 22% -> 21%
where the time goes in v6:
time: 696 us; the launch traced here: 695 us
  waiting for transfers between devices  225 us (32%)
  starting transfers between devices  167 us (24%)
  Pallas kernels  163 us (23%)
  blocking collectives  99.2 us (14%)
  local copies, waits for them, and re-layouts  21.9 us (3%)
  other arithmetic  18.2 us (3%)
    all_to_all x6, starting transfers between devices, to_pencils(): lax.all_to_all(blocks, 'slab', split_axis=0, concat_axis=0, tiled=True)  139 us
    ppermute x5, waiting for transfers between devices, halos(): above.insert(0, lax.ppermute(tail[:, rows - size:], 'slab', forth))  102 us
    all_to_all x1, blocking collectives, to_planes(): lax.all_to_all(pencils, 'slab', split_axis=0, concat_axis=0, tiled=True)  99.2 us
    all_to_all x6, waiting for transfers between devices, to_pencils(): lax.all_to_all(blocks, 'slab', split_axis=0, concat_axis=0, tiled=True)  95.7 us
    pallas_call x2, Pallas kernels, body(): call(view_kernel, 'view', 33, (volume(extent), volume(rows), end, end), [...  66.7 us
    pallas_call x8, Pallas kernels, streamed(): pl.pallas_call(kernel, out_shape=outs, in_specs=[WHOLE] * len(fixed) + [A...  34.7 us
    pallas_call x1, Pallas kernels, body(): call(functools.partial(last_kernel, margin), 'last', 30, tuple(outs), [WH...  29.8 us
    ppermute x5, waiting for transfers between devices, halos(): below.append(lax.ppermute(head[:, :size], 'slab', back))  27.5 us
  transfers between devices with their start and end apart: 16, of which 12 were waited for; matrix products, arithmetic and copies ran while one was open for 5% of the time, Pallas kernels for 21%

profile of v6, /device:TPU:1, one launch (start us, length us, event | category | flops | bytes accessed | tf_op | source)
XLA Modules:
  0.0 694.7 jit_solution(10414990703579473975)
XLA Ops:
  0.0 3.8 turn.6
  3.8 7.3 %all-to-all-start = ((f32[16,64,8,128]{3,2,1,0:T(8,128)}), f32[16,64,8,128]{3,2,1,0:T(8,128)}, u32[]{:S(2)}, u32[]{:S(2)}) async-start(f32[16,64,8,128]{3,2,1,0:T(8,128)} %turn.6), calls=%async_computation | async-start | bytes 8388608 | tf_op jit(solution)/shard_map/all_to_all | solution.py:363
  11.2 12.2 %slice_bitcast_fusion = (f32[8,1024,128]{2,1,0:T(8,128)}, f32[8,1024,128]{2,1,0:T(8,128)}, f32[8,1024,128]{2,1,0:T(8,128)}, f32[8,1024,128]{2,1,0:T(8,128)}) fusion(f32[4,8,1024,128]{3,2,1,0:T(8,128)} %param.13), kind=kLoop, calls=%fused_computation.5 | loop fusion | bytes 33554432 | tf_op jit(solution)/shard_map/squeeze | solution.py:450
  23.4 3.8 turn.7
  27.2 62.0 %all-to-all-done.own = f32[16,64,8,128]{3,2,1,0:T(8,128)} async-done(((f32[16,64,8,128]{3,2,1,0:T(8,128)}), f32[16,64,8,128]{3,2,1,0:T(8,128)}, u32[]{:S(2)}, u32[]{:S(2)}) %all-to-all-start) | async-done | bytes 4194336 | tf_op jit(solution)/shard_map/all_to_all | solution.py:363
  89.2 19.3 %all-to-all-start.1 = ((f32[16,64,8,128]{3,2,1,0:T(8,128)}), f32[16,64,8,128]{3,2,1,0:T(8,128)}, u32[]{:S(2)}, u32[]{:S(2)}) async-start(f32[16,64,8,128]{3,2,1,0:T(8,128)} %turn.7), calls=%async_computation.1 | async-start | bytes 8388608 | tf_op jit(solution)/shard_map/all_to_all | solution.py:363
  108.5 1.6 fusion.2
  110.2 3.5 collective-permute-start
  113.7 1.9 collective-permute-start.1
  115.6 3.8 turn.8.refs_0_
  119.5 28.4 %collective-permute-done.above.refs_1_ = f32[16,15,8,128]{3,2,1,0:T(8,128)S(1)} collective-permute-done((f32[16,15,8,128]{3,2,1,0:T(8,128)S(1)}, f32[16,15,8,128]{3,2,1,0:T(8,128)S(1)}, u32[]{:S(2)}, u32[]{:S(2)}) %collective-permute-start) | collective-permute-done | bytes 983072 | tf_op jit(solution)/shard_map/ppermute | solution.py:400
  147.9 4.2 collective-permute-done.1.below.refs_2_
  152.1 0.9 copy-done.4
  153.0 33.7 %all-to-all-done.1.data = f32[16,64,8,128]{3,2,1,0:T(8,128)} async-done(((f32[16,64,8,128]{3,2,1,0:T(8,128)}), f32[16,64,8,128]{3,2,1,0:T(8,128)}, u32[]{:S(2)}, u32[]{:S(2)}) %all-to-all-start.1) | async-done | bytes 4194336 | tf_op jit(solution)/shard_map/all_to_all | solution.py:363
  186.7 30.5 %all-to-all-start.2 = ((f32[16,64,8,128]{3,2,1,0:T(8,128)}), f32[16,64,8,128]{3,2,1,0:T(8,128)}, u32[]{:S(2)}, u32[]{:S(2)}) async-start(f32[16,64,8,128]{3,2,1,0:T(8,128)} %gate.4), calls=%async_computation.2 | async-start | bytes 8388608 | tf_op jit(solution)/shard_map/all_to_all | solution.py:363
  217.1 0.7 slice_reduce_fusion.1
  217.8 2.5 divide_bitcast_fusion.7
  220.8 1.0 select_reduce_fusion.4
  221.8 0.7 copy.32
  223.2 2.5 divide_bitcast_fusion.6
  225.7 3.7 select_reduce_fusion
  229.4 0.7 copy.31
  230.7 1.2 broadcast_divide_fusion
  231.9 2.4 broadcast_divide_fusion.5
  234.3 1.1 select_reduce_fusion.11
  235.4 25.9 %first.1 = (f32[16,96,8,128]{3,2,1,0:T(8,128)}, f32[16,64,8,128]{3,2,1,0:T(8,128)}, f32[16,30,8,128]{3,2,1,0:T(8,128)}, f32[16,30,8,128]{3,2,1,0:T(8,128)}) custom-call(f32[64,96]{1,0:T(8,128)} %get-tuple-element.52.blur_x, f32[128,128]{1,0:T(8,128)} %copy-done.13, f32[128,128]{1,0:T(8,128)} %bitcast.56, f32[128,128]{1,0:T(8,128)} %bitcast.55, ...), custom_call_target="tpu_custom_call" | custom-call | bytes 93600000 | tf_op jit(solution)/shard_map/first/pallas_call | solution.py:452
  261.3 3.5 collective-permute-start.2
  264.9 1.9 collective-permute-start.3
  266.8 3.9 turn.9.refs_0_
  270.7 22.2 %collective-permute-done.2.above.refs_1_ = f32[16,30,8,128]{3,2,1,0:T(8,128)S(1)} collective-permute-done((f32[16,30,8,128]{3,2,1,0:T(8,128)}, f32[16,30,8,128]{3,2,1,0:T(8,128)S(1)}, u32[]{:S(2)}, u32[]{:S(2)}) %collective-permute-start.2) | collective-permute-done | bytes 1966112 | tf_op jit(solution)/shard_map/ppermute | solution.py:400
  292.8 9.5 %collective-permute-done.3.below.refs_2_ = f32[16,30,8,128]{3,2,1,0:T(8,128)} collective-permute-done((f32[16,30,8,128]{3,2,1,0:T(8,128)}, f32[16,30,8,128]{3,2,1,0:T(8,128)}, u32[]{:S(2)}, u32[]{:S(2)}) %collective-permute-start.3) | collective-permute-done | bytes 1966112 | tf_op jit(solution)/shard_map/ppermute | solution.py:401
  302.4 33.2 %all-to-all-start.3 = ((f32[16,64,8,128]{3,2,1,0:T(8,128)}), f32[16,64,8,128]{3,2,1,0:T(8,128)}, u32[]{:S(2)}, u32[]{:S(2)}) async-start(f32[16,64,8,128]{3,2,1,0:T(8,128)} %gate.5), calls=%async_computation.3 | async-start | bytes 8388608 | tf_op jit(solution)/shard_map/all_to_all | solution.py:363
  335.6 0.7 copy.30
  336.3 0.7 copy.29
  337.0 1.1 select_reduce_fusion.8
  338.1 33.3 %view.2 = (f32[16,96,8,128]{3,2,1,0:T(8,128)}, f32[16,64,8,128]{3,2,1,0:T(8,128)}, f32[16,30,8,128]{3,2,1,0:T(8,128)}, f32[16,30,8,128]{3,2,1,0:T(8,128)}) custom-call(f32[96,128]{1,0:T(8,128)} %get-tuple-element.49.spread_x, f32[64,96]{1,0:T(8,128)} %get-tuple-element.53.blur_x, f32[128,128]{1,0:T(8,128)} %copy-done.11, f32[128,128]{1,0:T(8,128)} %bitcast.51, ...), custom_call_target="tpu_custom_call" | custom-call | bytes 118800000 | tf_op jit(solution)/shard_map/view/pallas_call | solution.py:464
  371.5 3.5 collective-permute-start.4
  375.0 1.9 collective-permute-start.5
  376.9 3.6 turn.10.refs_0_
  380.6 27.5 %collective-permute-done.4.above.refs_1_ = f32[16,30,8,128]{3,2,1,0:T(8,128)S(1)} collective-permute-done((f32[16,30,8,128]{3,2,1,0:T(8,128)}, f32[16,30,8,128]{3,2,1,0:T(8,128)S(1)}, u32[]{:S(2)}, u32[]{:S(2)}) %collective-permute-start.4) | collective-permute-done | bytes 1966112 | tf_op jit(solution)/shard_map/ppermute | solution.py:400
  408.1 7.9 %collective-permute-done.5.below.refs_2_ = f32[16,30,8,128]{3,2,1,0:T(8,128)} collective-permute-done((f32[16,30,8,128]{3,2,1,0:T(8,128)}, f32[16,30,8,128]{3,2,1,0:T(8,128)}, u32[]{:S(2)}, u32[]{:S(2)}) %collective-permute-start.5) | collective-permute-done | bytes 1966112 | tf_op jit(solution)/shard_map/ppermute | solution.py:401
  416.1 37.8 %all-to-all-start.4 = ((f32[16,36,8,128]{3,2,1,0:T(8,128)}), f32[16,36,8,128]{3,2,1,0:T(8,128)S(1)}, u32[]{:S(2)}, u32[]{:S(2)}) async-start(f32[16,36,8,128]{3,2,1,0:T(8,128)} %gate.6), calls=%async_computation.4 | async-start | bytes 4718592 | tf_op jit(solution)/shard_map/all_to_all | solution.py:363
  453.9 0.7 copy.28
  454.6 0.7 copy.27
  455.3 33.4 %view.3 = (f32[16,96,8,128]{3,2,1,0:T(8,128)}, f32[16,64,8,128]{3,2,1,0:T(8,128)}, f32[16,30,8,128]{3,2,1,0:T(8,128)}, f32[16,30,8,128]{3,2,1,0:T(8,128)}) custom-call(f32[96,128]{1,0:T(8,128)} %get-tuple-element.50.spread_x, f32[64,96]{1,0:T(8,128)} %get-tuple-element.54.blur_x, f32[128,128]{1,0:T(8,128)} %copy-done.9, f32[128,128]{1,0:T(8,128)} %bitcast.54, ...), custom_call_target="tpu_custom_call" | custom-call | bytes 118800000 | tf_op jit(solution)/shard_map/view/pallas_call | solution.py:464
  488.7 3.5 collective-permute-start.6
  492.3 2.0 collective-permute-start.7
  494.3 3.4 turn.11.refs_0_
  497.8 19.5 %collective-permute-done.6.above.refs_1_ = f32[16,30,8,128]{3,2,1,0:T(8,128)} collective-permute-done((f32[16,30,8,128]{3,2,1,0:T(8,128)}, f32[16,30,8,128]{3,2,1,0:T(8,128)}, u32[]{:S(2)}, u32[]{:S(2)}) %collective-permute-start.6) | collective-permute-done | bytes 1966112 | tf_op jit(solution)/shard_map/ppermute | solution.py:400
  517.3 3.4 collective-permute-done.7.below.refs_2_
  520.6 11.1 %all-to-all-start.5 = ((f32[16,28,8,128]{3,2,1,0:T(8,128)}), f32[16,28,8,128]{3,2,1,0:T(8,128)}, u32[]{:S(2)}, u32[]{:S(2)}) async-start(f32[16,28,8,128]{3,2,1,0:T(8,128)} %gate.7), calls=%async_computation.5 | async-start | bytes 3670016 | tf_op jit(solution)/shard_map/all_to_all | solution.py:363
  531.8 0.7 copy.26
  532.5 0.7 copy.25
  533.2 29.8 %last.1 = (f32[16,64,8,128]{3,2,1,0:T(8,128)}, f32[16,28,8,128]{3,2,1,0:T(8,128)}, f32[16,18,8,128]{3,2,1,0:T(8,128)}, f32[16,18,8,128]{3,2,1,0:T(8,128)}, f32[1...) custom-call(f32[96,128]{1,0:T(8,128)} %get-tuple-element.51.spread_x, f32[64,96]{1,0:T(8,128)} %get-tuple-element.55.blur_x, ...), custom_call_target="tpu_custom_call" | custom-call | bytes 108000000 | tf_op jit(solution)/shard_map/last/pallas_call | solution.py:459
  563.0 3.5 collective-permute-start.8
  566.6 1.9 collective-permute-start.9
  568.5 0.8 select_reduce_fusion.15.refs_0_
  569.3 6.1 middle.1.refs_5_
  575.4 4.3 collective-permute-done.8.refs_1_
  579.6 2.6 collective-permute-done.9.refs_2_
  582.2 0.9 copy-done.7
  583.1 8.5 %finish.1 = f32[16,64,8,128]{3,2,1,0:T(8,128)} custom-call(f32[64,96]{1,0:T(8,128)} %select_reduce_fusion.15.refs_0_, f32[16,15,8,128]{3,2,1,0:T(8,128)} %copy-done.6, f32[16,15,8,128]{3,2,1,0:T(8,128)} %copy-done.7, f32[16,64,8,128]{3,2,1,0:T(8,128)} %get-tuple-element.37.refs_3_, f32[16,18,8,128]{3,2,1,0:T(8,128)} %get-tuple-element.38.refs_4_, ...), custom_call_target="tpu_custom_call" | custom-call | bytes 25200000 | tf_op jit(solution)/shard_map/finish/pallas_call | solution.py:280
  591.6 99.2 %all_to_all.35.refs_0_ = f32[16,64,8,128]{3,2,1,0:T(8,128)} all-to-all(f32[16,64,8,128]{3,2,1,0:T(8,128)} %finish.1), channel_id=1, replica_groups=mesh['groups'=2,'slab'=16] {'slab'}, dimensions={0} | all-to-all | bytes 8388608 | tf_op jit(solution)/shard_map/all_to_all | solution.py:374
  690.8 3.8 turn_back.1
  (54 shorter events, 1.7 us)
Async XLA Ops:
  3.8 85.4 %all-to-all-start = ((f32[16,64,8,128]{3,2,1,0:T(8,128)}), f32[16,64,8,128]{3,2,1,0:T(8,128)}, u32[]{:S(2)}, u32[]{:S(2)}) async-start(f32[16,64,8,128]{3,2,1,0:T(8,128)} %turn.6), calls=%async_computation | async-start | bytes 8388608 | tf_op jit(solution)/shard_map/all_to_all | solution.py:363
  89.2 97.4 %all-to-all-start.1 = ((f32[16,64,8,128]{3,2,1,0:T(8,128)}), f32[16,64,8,128]{3,2,1,0:T(8,128)}, u32[]{:S(2)}, u32[]{:S(2)}) async-start(f32[16,64,8,128]{3,2,1,0:T(8,128)} %turn.7), calls=%async_computation.1 | async-start | bytes 8388608 | tf_op jit(solution)/shard_map/all_to_all | solution.py:363
  110.2 37.7 %collective-permute-start = (f32[16,15,8,128]{3,2,1,0:T(8,128)S(1)}, f32[16,15,8,128]{3,2,1,0:T(8,128)S(1)}, u32[]{:S(2)}, u32[]{:S(2)}) collective-permute-start(f32[16,15,8,128]{3,2,1,0:T(8,128)S(1)} %get-tuple-element.73), channel_id=1, source_target_pairs={{0,1},{1,2},{2,3},{3,7},{7,6},{6,5},{5,4},{4,8},{8,9},{9,10},{10,1... | collective-permute-start | bytes 2949128 | tf_op jit(solution)/shard_map/ppermute | solution.py:400
  113.7 38.3 %collective-permute-start.1 = (f32[16,15,8,128]{3,2,1,0:T(8,128)S(1)}, f32[16,15,8,128]{3,2,1,0:T(8,128)S(1)}, u32[]{:S(2)}, u32[]{:S(2)}) collective-permute-start(f32[16,15,8,128]{3,2,1,0:T(8,128)S(1)} %get-tuple-element.72), channel_id=1, source_target_pairs={{1,0},{2,1},{3,2},{7,3},{6,7},{5,6},{4,5},{8,4},{9,8},{10,9},{11,1... | collective-permute-start | bytes 2949128 | tf_op jit(solution)/shard_map/ppermute | solution.py:401
  147.9 4.2 copy-start.3
  152.1 0.9 copy-start.4
  153.0 64.1 %copy-start.18 = (f32[4,2,31]{2,1,0:T(2,128)S(1)}, f32[4,2,31]{2,1,0:T(2,128)}, u32[]{:S(2)}) copy-start(f32[4,2,31]{2,1,0:T(2,128)} %param.14) | copy-start | bytes 2980
  153.0 69.6 %copy-start.19 = (f32[4,101]{1,0:T(4,128)S(1)}, f32[4,101]{1,0:T(4,128)}, u32[]{:S(2)}) copy-start(f32[4,101]{1,0:T(4,128)} %param.15) | copy-start | bytes 4852
  153.0 81.3 %copy-start.17 = (s32[64,96]{1,0:T(8,128)S(1)}, s32[64,96]{1,0:T(8,128)}, u32[]{:S(2)}) copy-start(s32[64,96]{1,0:T(8,128)} %constant.28.clone) | copy-start | bytes 73732
  186.7 115.7 %all-to-all-start.2 = ((f32[16,64,8,128]{3,2,1,0:T(8,128)}), f32[16,64,8,128]{3,2,1,0:T(8,128)}, u32[]{:S(2)}, u32[]{:S(2)}) async-start(f32[16,64,8,128]{3,2,1,0:T(8,128)} %gate.4), calls=%async_computation.2 | async-start | bytes 8388608 | tf_op jit(solution)/shard_map/all_to_all | solution.py:363
  221.8 13.6 %copy-start.13 = (f32[128,128]{1,0:T(8,128)}, f32[128,128]{1,0:T(8,128)S(1)}, u32[]{:S(2)}) copy-start(f32[128,128]{1,0:T(8,128)S(1)} %get-tuple-element.45.blur_y) | copy-start | bytes 196612
  221.8 113.8 %copy-start.11 = (f32[128,128]{1,0:T(8,128)}, f32[128,128]{1,0:T(8,128)S(1)}, u32[]{:S(2)}) copy-start(f32[128,128]{1,0:T(8,128)S(1)} %get-tuple-element.46.blur_y) | copy-start | bytes 196612
  221.8 232.1 %copy-start.9 = (f32[128,128]{1,0:T(8,128)}, f32[128,128]{1,0:T(8,128)S(1)}, u32[]{:S(2)}) copy-start(f32[128,128]{1,0:T(8,128)S(1)} %get-tuple-element.47.blur_y) | copy-start | bytes 196612
  221.8 310.0 %copy-start.8 = (f32[128,128]{1,0:T(8,128)}, f32[128,128]{1,0:T(8,128)S(1)}, u32[]{:S(2)}) copy-start(f32[128,128]{1,0:T(8,128)S(1)} %get-tuple-element.48.blur_y) | copy-start | bytes 196612
  229.4 6.0 copy-start.14
  229.4 106.9 %copy-start.12 = (f32[128,128]{1,0:T(8,128)}, f32[128,128]{1,0:T(8,128)S(1)}, u32[]{:S(2)}) copy-start(f32[128,128]{1,0:T(8,128)S(1)} %get-tuple-element.42.back_z) | copy-start | bytes 196612
  229.4 225.2 %copy-start.10 = (f32[128,128]{1,0:T(8,128)}, f32[128,128]{1,0:T(8,128)S(1)}, u32[]{:S(2)}) copy-start(f32[128,128]{1,0:T(8,128)S(1)} %get-tuple-element.43.back_z) | copy-start | bytes 196612
  229.4 303.1 %copy-start.5 = (f32[128,128]{1,0:T(8,128)}, f32[128,128]{1,0:T(8,128)S(1)}, u32[]{:S(2)}) copy-start(f32[128,128]{1,0:T(8,128)S(1)} %get-tuple-element.44.back_z) | copy-start | bytes 196612
  261.3 31.5 %collective-permute-start.2 = (f32[16,30,8,128]{3,2,1,0:T(8,128)}, f32[16,30,8,128]{3,2,1,0:T(8,128)S(1)}, u32[]{:S(2)}, u32[]{:S(2)}) collective-permute-start(f32[16,30,8,128]{3,2,1,0:T(8,128)} %get-tuple-element.23), channel_id=1, source_target_pairs={{0,1},{1,2},{2,3},{3,7},{7,6},{6,5},{5,4},{4,8},{8,9},{9,10},{10,1... | collective-permute-start | bytes 5898248 | tf_op jit(solution)/shard_map/ppermute | solution.py:400
  264.9 37.5 %collective-permute-start.3 = (f32[16,30,8,128]{3,2,1,0:T(8,128)}, f32[16,30,8,128]{3,2,1,0:T(8,128)}, u32[]{:S(2)}, u32[]{:S(2)}) collective-permute-start(f32[16,30,8,128]{3,2,1,0:T(8,128)} %get-tuple-element.25.refs_1_), channel_id=1, source_target_pairs={{1,0},{2,1},{3,2},{7,3},{6,7},{5,6},{4,5},{8,4},{9,8},{10,9},{11,1... | collective-permute-start | bytes 5898248 | tf_op jit(solution)/shard_map/ppermute | solution.py:401
  292.8 9.5 %copy-start.1 = (f32[16,30,8,128]{3,2,1,0:T(8,128)}, f32[16,30,8,128]{3,2,1,0:T(8,128)S(1)}, u32[]{:S(2)}) copy-start(f32[16,30,8,128]{3,2,1,0:T(8,128)S(1)} %collective-permute-done.2.above.refs_1_) | copy-start | bytes 5898244
  302.4 34.7 %copy-start.15 = (s32[96,128]{1,0:T(8,128)S(1)}, s32[96,128]{1,0:T(8,128)}, u32[]{:S(2)}) copy-start(s32[96,128]{1,0:T(8,128)} %constant.29.clone) | copy-start | bytes 147460
  302.4 113.7 %all-to-all-start.3 = ((f32[16,64,8,128]{3,2,1,0:T(8,128)}), f32[16,64,8,128]{3,2,1,0:T(8,128)}, u32[]{:S(2)}, u32[]{:S(2)}) async-start(f32[16,64,8,128]{3,2,1,0:T(8,128)} %gate.5), calls=%async_computation.3 | async-start | bytes 8388608 | tf_op jit(solution)/shard_map/all_to_all | solution.py:363
  371.5 36.6 %collective-permute-start.4 = (f32[16,30,8,128]{3,2,1,0:T(8,128)}, f32[16,30,8,128]{3,2,1,0:T(8,128)S(1)}, u32[]{:S(2)}, u32[]{:S(2)}) collective-permute-start(f32[16,30,8,128]{3,2,1,0:T(8,128)} %get-tuple-element.27), channel_id=1, source_target_pairs={{0,1},{1,2},{2,3},{3,7},{7,6},{6,5},{5,4},{4,8},{8,9},{9,10},{10,1... | collective-permute-start | bytes 5898248 | tf_op jit(solution)/shard_map/ppermute | solution.py:400
  375.0 41.0 %collective-permute-start.5 = (f32[16,30,8,128]{3,2,1,0:T(8,128)}, f32[16,30,8,128]{3,2,1,0:T(8,128)}, u32[]{:S(2)}, u32[]{:S(2)}) collective-permute-start(f32[16,30,8,128]{3,2,1,0:T(8,128)} %get-tuple-element.29.refs_1_), channel_id=1, source_target_pairs={{1,0},{2,1},{3,2},{7,3},{6,7},{5,6},{4,5},{8,4},{9,8},{10,9},{11,1... | collective-permute-start | bytes 5898248 | tf_op jit(solution)/shard_map/ppermute | solution.py:401
  408.1 7.9 %copy-start.2 = (f32[16,30,8,128]{3,2,1,0:T(8,128)}, f32[16,30,8,128]{3,2,1,0:T(8,128)S(1)}, u32[]{:S(2)}) copy-start(f32[16,30,8,128]{3,2,1,0:T(8,128)S(1)} %collective-permute-done.4.above.refs_1_) | copy-start | bytes 5898244
  416.1 104.6 %all-to-all-start.4 = ((f32[16,36,8,128]{3,2,1,0:T(8,128)}), f32[16,36,8,128]{3,2,1,0:T(8,128)S(1)}, u32[]{:S(2)}, u32[]{:S(2)}) async-start(f32[16,36,8,128]{3,2,1,0:T(8,128)} %gate.6), calls=%async_computation.4 | async-start | bytes 4718592 | tf_op jit(solution)/shard_map/all_to_all | solution.py:363
  488.7 28.6 %collective-permute-start.6 = (f32[16,30,8,128]{3,2,1,0:T(8,128)}, f32[16,30,8,128]{3,2,1,0:T(8,128)}, u32[]{:S(2)}, u32[]{:S(2)}) collective-permute-start(f32[16,30,8,128]{3,2,1,0:T(8,128)} %get-tuple-element.31), channel_id=1, source_target_pairs={{0,1},{1,2},{2,3},{3,7},{7,6},{6,5},{5,4},{4,8},{8,9},{9,10},{10,1... | collective-permute-start | bytes 5898248 | tf_op jit(solution)/shard_map/ppermute | solution.py:400
  492.3 28.4 %collective-permute-start.7 = (f32[16,30,8,128]{3,2,1,0:T(8,128)}, f32[16,30,8,128]{3,2,1,0:T(8,128)}, u32[]{:S(2)}, u32[]{:S(2)}) collective-permute-start(f32[16,30,8,128]{3,2,1,0:T(8,128)} %get-tuple-element.33.refs_1_), channel_id=1, source_target_pairs={{1,0},{2,1},{3,2},{7,3},{6,7},{5,6},{4,5},{8,4},{9,8},{10,9},{11,1... | collective-permute-start | bytes 5898248 | tf_op jit(solution)/shard_map/ppermute | solution.py:401
  520.6 12.6 %copy-start = (f32[16,36,8,128]{3,2,1,0:T(8,128)}, f32[16,36,8,128]{3,2,1,0:T(8,128)S(1)}, u32[]{:S(2)}) copy-start(f32[16,36,8,128]{3,2,1,0:T(8,128)S(1)} %all-to-all-done.4.data) | copy-start | bytes 7077892
  520.6 48.7 %all-to-all-start.5 = ((f32[16,28,8,128]{3,2,1,0:T(8,128)}), f32[16,28,8,128]{3,2,1,0:T(8,128)}, u32[]{:S(2)}, u32[]{:S(2)}) async-start(f32[16,28,8,128]{3,2,1,0:T(8,128)} %gate.7), calls=%async_computation.5 | async-start | bytes 3670016 | tf_op jit(solution)/shard_map/all_to_all | solution.py:363
  533.2 35.3 %copy-start.16 = (s32[64,96]{1,0:T(8,128)S(1)}, s32[64,96]{1,0:T(8,128)}, u32[]{:S(2)}) copy-start(s32[64,96]{1,0:T(8,128)} %constant.30.clone) | copy-start | bytes 73732
  563.0 16.6 %collective-permute-start.8 = (f32[16,15,8,128]{3,2,1,0:T(8,128)}, f32[16,15,8,128]{3,2,1,0:T(8,128)S(1)}, u32[]{:S(2)}, u32[]{:S(2)}) collective-permute-start(f32[16,15,8,128]{3,2,1,0:T(8,128)} %get-tuple-element.35), channel_id=1, source_target_pairs={{0,1},{1,2},{2,3},{3,7},{7,6},{6,5},{5,4},{4,8},{8,9},{9,10},{10,1... | collective-permute-start | bytes 2949128 | tf_op jit(solution)/shard_map/ppermute | solution.py:400
  566.6 15.6 %collective-permute-start.9 = (f32[16,15,8,128]{3,2,1,0:T(8,128)}, f32[16,15,8,128]{3,2,1,0:T(8,128)S(1)}, u32[]{:S(2)}, u32[]{:S(2)}) collective-permute-start(f32[16,15,8,128]{3,2,1,0:T(8,128)} %get-tuple-element.36), channel_id=1, source_target_pairs={{1,0},{2,1},{3,2},{7,3},{6,7},{5,6},{4,5},{8,4},{9,8},{10,9},{11,1... | collective-permute-start | bytes 2949128 | tf_op jit(solution)/shard_map/ppermute | solution.py:401
  579.6 2.6 copy-start.6
  582.2 0.9 copy-start.7

commit v7 on v6

--- a/solution.py
+++ b/solution.py
@@ -118,7 +118,7 @@
         emit(block, plane + 1, mixed[:, width:])
         return 0
 
-    lax.fori_loop(0, blocks * planes // 2, pair, 0, unroll=4)
+    lax.fori_loop(0, blocks * planes // 2, pair, 0, unroll=8)
 
 
 def x_matrix(taps, groups, target):
@@ -478,7 +478,7 @@
         pieces = [first, inner, second]
     else:
         own, pieces = wide[:, margin : margin + rows], [center]
-    step = 2 if blocks % 2 == 0 else 1
+    step = 4 if blocks % 4 == 0 else 1
     cut = lambda place: (pl.ds(place * step, step),)
     (current,) = streamed(
         functools.partial(finish_part, step),

time: 696 us -> 694 us (level)
  Pallas kernels: 163 us -> 152 us
    all_to_all x6, waiting for transfers between devices: 95.7 us -> 106 us  [to_pencils(): lax.all_to_all(blocks, 'slab', split_axis=0, concat_axis=0, tiled=True)]
    ppermute x5, waiting for transfers between devices: 27.5 us -> 20.3 us  [halos(): below.append(lax.ppermute(head[:, :size], 'slab', back))]
  transfers between devices with their start and end apart: 16 -> 16, of which waited for: 12 -> 13; matrix products, arithmetic and copies ran while one was open for 5% -> 6% of each run, Pallas kernels for 21% -> 20%
where the time goes in v7:
time: 694 us; the launch traced here: 693 us
  waiting for transfers between devices  227 us (33%)
  starting transfers between devices  171 us (25%)
  Pallas kernels  152 us (22%)
  blocking collectives  102 us (15%)
  local copies, waits for them, and re-layouts  23.2 us (3%)
  other arithmetic  18.2 us (3%)
    all_to_all x6, starting transfers between devices, to_pencils(): lax.all_to_all(blocks, 'slab', split_axis=0, concat_axis=0, tiled=True)  143 us
    all_to_all x6, waiting for transfers between devices, to_pencils(): lax.all_to_all(blocks, 'slab', split_axis=0, concat_axis=0, tiled=True)  106 us
    all_to_all x1, blocking collectives, to_planes(): lax.all_to_all(pencils, 'slab', split_axis=0, concat_axis=0, tiled=True)  102 us
    ppermute x5, waiting for transfers between devices, halos(): above.insert(0, lax.ppermute(tail[:, rows - size:], 'slab', forth))  102 us
    pallas_call x2, Pallas kernels, body(): call(view_kernel, 'view', 33, (volume(extent), volume(rows), end, end), [...  60.8 us
    pallas_call x8, Pallas kernels, streamed(): pl.pallas_call(kernel, out_shape=outs, in_specs=[WHOLE] * len(fixed) + [A...  33.6 us
    pallas_call x1, Pallas kernels, body(): call(functools.partial(last_kernel, margin), 'last', 30, tuple(outs), [WH...  26.8 us
    pallas_call x1, Pallas kernels, body(): call(first_kernel, 'first', 26, (volume(extent), volume(rows), end, end),...  24.3 us
  transfers between devices with their start and end apart: 16, of which 13 were waited for; matrix products, arithmetic and copies ran while one was open for 6% of the time, Pallas kernels for 20%

profile of v7, /device:TPU:1, one launch (start us, length us, event | category | flops | bytes accessed | tf_op | source)
XLA Modules:
  0.0 693.0 jit_solution(6603219751330699783)
XLA Ops:
  0.0 3.8 turn.6
  3.8 7.3 %all-to-all-start = ((f32[16,64,8,128]{3,2,1,0:T(8,128)}), f32[16,64,8,128]{3,2,1,0:T(8,128)}, u32[]{:S(2)}, u32[]{:S(2)}) async-start(f32[16,64,8,128]{3,2,1,0:T(8,128)} %turn.6), calls=%async_computation | async-start | bytes 8388608 | tf_op jit(solution)/shard_map/all_to_all | solution.py:363
  11.2 12.2 %slice_bitcast_fusion = (f32[8,1024,128]{2,1,0:T(8,128)}, f32[8,1024,128]{2,1,0:T(8,128)}, f32[8,1024,128]{2,1,0:T(8,128)}, f32[8,1024,128]{2,1,0:T(8,128)}) fusion(f32[4,8,1024,128]{3,2,1,0:T(8,128)} %param.13), kind=kLoop, calls=%fused_computation.5 | loop fusion | bytes 33554432 | tf_op jit(solution)/shard_map/squeeze | solution.py:450
  23.4 3.8 turn.7
  27.2 62.0 %all-to-all-done.own = f32[16,64,8,128]{3,2,1,0:T(8,128)} async-done(((f32[16,64,8,128]{3,2,1,0:T(8,128)}), f32[16,64,8,128]{3,2,1,0:T(8,128)}, u32[]{:S(2)}, u32[]{:S(2)}) %all-to-all-start) | async-done | bytes 4194336 | tf_op jit(solution)/shard_map/all_to_all | solution.py:363
  89.2 19.3 %all-to-all-start.1 = ((f32[16,64,8,128]{3,2,1,0:T(8,128)}), f32[16,64,8,128]{3,2,1,0:T(8,128)}, u32[]{:S(2)}, u32[]{:S(2)}) async-start(f32[16,64,8,128]{3,2,1,0:T(8,128)} %turn.7), calls=%async_computation.1 | async-start | bytes 8388608 | tf_op jit(solution)/shard_map/all_to_all | solution.py:363
  108.5 1.6 fusion.2
  110.2 3.5 collective-permute-start
  113.7 1.9 collective-permute-start.1
  115.6 3.8 turn.8.refs_0_
  119.5 28.4 %collective-permute-done.above.refs_1_ = f32[16,15,8,128]{3,2,1,0:T(8,128)S(1)} collective-permute-done((f32[16,15,8,128]{3,2,1,0:T(8,128)S(1)}, f32[16,15,8,128]{3,2,1,0:T(8,128)S(1)}, u32[]{:S(2)}, u32[]{:S(2)}) %collective-permute-start) | collective-permute-done | bytes 983072 | tf_op jit(solution)/shard_map/ppermute | solution.py:400
  147.9 4.2 collective-permute-done.1.below.refs_2_
  152.1 0.9 copy-done.4
  153.0 33.7 %all-to-all-done.1.data = f32[16,64,8,128]{3,2,1,0:T(8,128)} async-done(((f32[16,64,8,128]{3,2,1,0:T(8,128)}), f32[16,64,8,128]{3,2,1,0:T(8,128)}, u32[]{:S(2)}, u32[]{:S(2)}) %all-to-all-start.1) | async-done | bytes 4194336 | tf_op jit(solution)/shard_map/all_to_all | solution.py:363
  186.7 30.5 %all-to-all-start.2 = ((f32[16,64,8,128]{3,2,1,0:T(8,128)}), f32[16,64,8,128]{3,2,1,0:T(8,128)}, u32[]{:S(2)}, u32[]{:S(2)}) async-start(f32[16,64,8,128]{3,2,1,0:T(8,128)} %gate.4), calls=%async_computation.2 | async-start | bytes 8388608 | tf_op jit(solution)/shard_map/all_to_all | solution.py:363
  217.8 2.5 divide_bitcast_fusion.7
  220.8 1.0 select_reduce_fusion.4
  221.8 0.7 copy.32
  223.2 2.5 divide_bitcast_fusion.6
  225.7 3.7 select_reduce_fusion
  230.7 1.2 broadcast_divide_fusion
  231.9 2.4 broadcast_divide_fusion.5
  234.3 1.1 select_reduce_fusion.11
  235.4 24.3 %first.1 = (f32[16,96,8,128]{3,2,1,0:T(8,128)}, f32[16,64,8,128]{3,2,1,0:T(8,128)}, f32[16,30,8,128]{3,2,1,0:T(8,128)}, f32[16,30,8,128]{3,2,1,0:T(8,128)}) custom-call(f32[64,96]{1,0:T(8,128)} %get-tuple-element.52.blur_x, f32[128,128]{1,0:T(8,128)} %copy-done.13, f32[128,128]{1,0:T(8,128)} %bitcast.56, f32[128,128]{1,0:T(8,128)} %bitcast.55, ...), custom_call_target="tpu_custom_call" | custom-call | bytes 93600000 | tf_op jit(solution)/shard_map/first/pallas_call | solution.py:452
  259.7 3.5 collective-permute-start.2
  263.3 1.9 collective-permute-start.3
  265.2 3.9 turn.9.refs_0_
  269.1 23.8 %collective-permute-done.2.above.refs_1_ = f32[16,30,8,128]{3,2,1,0:T(8,128)S(1)} collective-permute-done((f32[16,30,8,128]{3,2,1,0:T(8,128)}, f32[16,30,8,128]{3,2,1,0:T(8,128)S(1)}, u32[]{:S(2)}, u32[]{:S(2)}) %collective-permute-start.2) | collective-permute-done | bytes 1966112 | tf_op jit(solution)/shard_map/ppermute | solution.py:400
  292.8 7.9 %collective-permute-done.3.below.refs_2_ = f32[16,30,8,128]{3,2,1,0:T(8,128)} collective-permute-done((f32[16,30,8,128]{3,2,1,0:T(8,128)}, f32[16,30,8,128]{3,2,1,0:T(8,128)}, u32[]{:S(2)}, u32[]{:S(2)}) %collective-permute-start.3) | collective-permute-done | bytes 1966112 | tf_op jit(solution)/shard_map/ppermute | solution.py:401
  300.8 34.8 %all-to-all-start.3 = ((f32[16,64,8,128]{3,2,1,0:T(8,128)}), f32[16,64,8,128]{3,2,1,0:T(8,128)}, u32[]{:S(2)}, u32[]{:S(2)}) async-start(f32[16,64,8,128]{3,2,1,0:T(8,128)} %gate.5), calls=%async_computation.3 | async-start | bytes 8388608 | tf_op jit(solution)/shard_map/all_to_all | solution.py:363
  335.6 0.7 copy.30
  336.3 0.7 copy.29
  337.0 1.1 select_reduce_fusion.8
  338.1 30.4 %view.2 = (f32[16,96,8,128]{3,2,1,0:T(8,128)}, f32[16,64,8,128]{3,2,1,0:T(8,128)}, f32[16,30,8,128]{3,2,1,0:T(8,128)}, f32[16,30,8,128]{3,2,1,0:T(8,128)}) custom-call(f32[96,128]{1,0:T(8,128)} %get-tuple-element.49.spread_x, f32[64,96]{1,0:T(8,128)} %get-tuple-element.53.blur_x, f32[128,128]{1,0:T(8,128)} %copy-done.11, f32[128,128]{1,0:T(8,128)} %bitcast.51, ...), custom_call_target="tpu_custom_call" | custom-call | bytes 118800000 | tf_op jit(solution)/shard_map/view/pallas_call | solution.py:464
  368.5 3.5 collective-permute-start.4
  372.0 2.1 collective-permute-start.5
  374.1 3.6 turn.10.refs_0_
  377.8 27.4 %collective-permute-done.4.above.refs_1_ = f32[16,30,8,128]{3,2,1,0:T(8,128)S(1)} collective-permute-done((f32[16,30,8,128]{3,2,1,0:T(8,128)}, f32[16,30,8,128]{3,2,1,0:T(8,128)S(1)}, u32[]{:S(2)}, u32[]{:S(2)}) %collective-permute-start.4) | collective-permute-done | bytes 1966112 | tf_op jit(solution)/shard_map/ppermute | solution.py:400
  405.2 1.3 copy-done.2
  406.5 7.4 %all-to-all-done.3.data = f32[16,64,8,128]{3,2,1,0:T(8,128)} async-done(((f32[16,64,8,128]{3,2,1,0:T(8,128)}), f32[16,64,8,128]{3,2,1,0:T(8,128)}, u32[]{:S(2)}, u32[]{:S(2)}) %all-to-all-start.3) | async-done | bytes 4194336 | tf_op jit(solution)/shard_map/all_to_all | solution.py:363
  413.9 40.0 %all-to-all-start.4 = ((f32[16,36,8,128]{3,2,1,0:T(8,128)}), f32[16,36,8,128]{3,2,1,0:T(8,128)S(1)}, u32[]{:S(2)}, u32[]{:S(2)}) async-start(f32[16,36,8,128]{3,2,1,0:T(8,128)} %gate.6), calls=%async_computation.4 | async-start | bytes 4718592 | tf_op jit(solution)/shard_map/all_to_all | solution.py:363
  453.9 0.7 copy.28
  454.6 0.7 copy.27
  455.3 30.4 %view.3 = (f32[16,96,8,128]{3,2,1,0:T(8,128)}, f32[16,64,8,128]{3,2,1,0:T(8,128)}, f32[16,30,8,128]{3,2,1,0:T(8,128)}, f32[16,30,8,128]{3,2,1,0:T(8,128)}) custom-call(f32[96,128]{1,0:T(8,128)} %get-tuple-element.50.spread_x, f32[64,96]{1,0:T(8,128)} %get-tuple-element.54.blur_x, f32[128,128]{1,0:T(8,128)} %copy-done.9, f32[128,128]{1,0:T(8,128)} %bitcast.54, ...), custom_call_target="tpu_custom_call" | custom-call | bytes 118800000 | tf_op jit(solution)/shard_map/view/pallas_call | solution.py:464
  485.7 3.5 collective-permute-start.6
  489.3 2.0 collective-permute-start.7
  491.3 3.4 turn.11.refs_0_
  494.8 19.5 %collective-permute-done.6.above.refs_1_ = f32[16,30,8,128]{3,2,1,0:T(8,128)} collective-permute-done((f32[16,30,8,128]{3,2,1,0:T(8,128)}, f32[16,30,8,128]{3,2,1,0:T(8,128)}, u32[]{:S(2)}, u32[]{:S(2)}) %collective-permute-start.6) | collective-permute-done | bytes 1966112 | tf_op jit(solution)/shard_map/ppermute | solution.py:400
  514.3 6.3 collective-permute-done.7.below.refs_2_
  520.6 11.1 %all-to-all-start.5 = ((f32[16,28,8,128]{3,2,1,0:T(8,128)}), f32[16,28,8,128]{3,2,1,0:T(8,128)}, u32[]{:S(2)}, u32[]{:S(2)}) async-start(f32[16,28,8,128]{3,2,1,0:T(8,128)} %gate.7), calls=%async_computation.5 | async-start | bytes 3670016 | tf_op jit(solution)/shard_map/all_to_all | solution.py:363
  531.8 0.7 copy.26
  532.5 0.7 copy.25
  533.2 26.8 %last.1 = (f32[16,64,8,128]{3,2,1,0:T(8,128)}, f32[16,28,8,128]{3,2,1,0:T(8,128)}, f32[16,18,8,128]{3,2,1,0:T(8,128)}, f32[16,18,8,128]{3,2,1,0:T(8,128)}, f32[1...) custom-call(f32[96,128]{1,0:T(8,128)} %get-tuple-element.51.spread_x, f32[64,96]{1,0:T(8,128)} %get-tuple-element.55.blur_x, ...), custom_call_target="tpu_custom_call" | custom-call | bytes 108000000 | tf_op jit(solution)/shard_map/last/pallas_call | solution.py:459
  560.1 3.5 collective-permute-start.8
  563.6 1.9 collective-permute-start.9
  565.5 0.8 select_reduce_fusion.15.refs_0_
  566.3 2.5 all-to-all-done.5.data
  568.8 6.1 middle.1.refs_5_
  574.9 2.5 collective-permute-done.8.refs_1_
  577.4 1.8 collective-permute-done.9.refs_2_
  579.2 0.9 copy-done.7
  580.1 7.4 %finish.1 = f32[16,64,8,128]{3,2,1,0:T(8,128)} custom-call(f32[64,96]{1,0:T(8,128)} %select_reduce_fusion.15.refs_0_, f32[16,15,8,128]{3,2,1,0:T(8,128)} %copy-done.6, f32[16,15,8,128]{3,2,1,0:T(8,128)} %copy-done.7, f32[16,64,8,128]{3,2,1,0:T(8,128)} %get-tuple-element.37.refs_3_, f32[16,18,8,128]{3,2,1,0:T(8,128)} %get-tuple-element.38.refs_4_, ...), custom_call_target="tpu_custom_call" | custom-call | bytes 25200000 | tf_op jit(solution)/shard_map/finish/pallas_call | solution.py:280
  587.5 101.6 %all_to_all.35.refs_0_ = f32[16,64,8,128]{3,2,1,0:T(8,128)} all-to-all(f32[16,64,8,128]{3,2,1,0:T(8,128)} %finish.1), channel_id=1, replica_groups=mesh['groups'=2,'slab'=16] {'slab'}, dimensions={0} | all-to-all | bytes 8388608 | tf_op jit(solution)/shard_map/all_to_all | solution.py:374
  689.1 3.8 turn_back.1
  (54 shorter events, 3.1 us)
Async XLA Ops:
  3.8 85.4 %all-to-all-start = ((f32[16,64,8,128]{3,2,1,0:T(8,128)}), f32[16,64,8,128]{3,2,1,0:T(8,128)}, u32[]{:S(2)}, u32[]{:S(2)}) async-start(f32[16,64,8,128]{3,2,1,0:T(8,128)} %turn.6), calls=%async_computation | async-start | bytes 8388608 | tf_op jit(solution)/shard_map/all_to_all | solution.py:363
  89.2 97.4 %all-to-all-start.1 = ((f32[16,64,8,128]{3,2,1,0:T(8,128)}), f32[16,64,8,128]{3,2,1,0:T(8,128)}, u32[]{:S(2)}, u32[]{:S(2)}) async-start(f32[16,64,8,128]{3,2,1,0:T(8,128)} %turn.7), calls=%async_computation.1 | async-start | bytes 8388608 | tf_op jit(solution)/shard_map/all_to_all | solution.py:363
  110.2 37.7 %collective-permute-start = (f32[16,15,8,128]{3,2,1,0:T(8,128)S(1)}, f32[16,15,8,128]{3,2,1,0:T(8,128)S(1)}, u32[]{:S(2)}, u32[]{:S(2)}) collective-permute-start(f32[16,15,8,128]{3,2,1,0:T(8,128)S(1)} %get-tuple-element.73), channel_id=1, source_target_pairs={{0,1},{1,2},{2,3},{3,7},{7,6},{6,5},{5,4},{4,8},{8,9},{9,10},{10,1... | collective-permute-start | bytes 2949128 | tf_op jit(solution)/shard_map/ppermute | solution.py:400
  113.7 38.3 %collective-permute-start.1 = (f32[16,15,8,128]{3,2,1,0:T(8,128)S(1)}, f32[16,15,8,128]{3,2,1,0:T(8,128)S(1)}, u32[]{:S(2)}, u32[]{:S(2)}) collective-permute-start(f32[16,15,8,128]{3,2,1,0:T(8,128)S(1)} %get-tuple-element.72), channel_id=1, source_target_pairs={{1,0},{2,1},{3,2},{7,3},{6,7},{5,6},{4,5},{8,4},{9,8},{10,9},{11,1... | collective-permute-start | bytes 2949128 | tf_op jit(solution)/shard_map/ppermute | solution.py:401
  147.9 4.2 copy-start.3
  152.1 0.9 copy-start.4
  153.0 64.1 %copy-start.18 = (f32[4,2,31]{2,1,0:T(2,128)S(1)}, f32[4,2,31]{2,1,0:T(2,128)}, u32[]{:S(2)}) copy-start(f32[4,2,31]{2,1,0:T(2,128)} %param.14) | copy-start | bytes 2980
  153.0 69.6 %copy-start.19 = (f32[4,101]{1,0:T(4,128)S(1)}, f32[4,101]{1,0:T(4,128)}, u32[]{:S(2)}) copy-start(f32[4,101]{1,0:T(4,128)} %param.15) | copy-start | bytes 4852
  153.0 81.3 %copy-start.17 = (s32[64,96]{1,0:T(8,128)S(1)}, s32[64,96]{1,0:T(8,128)}, u32[]{:S(2)}) copy-start(s32[64,96]{1,0:T(8,128)} %constant.28.clone) | copy-start | bytes 73732
  186.7 114.1 %all-to-all-start.2 = ((f32[16,64,8,128]{3,2,1,0:T(8,128)}), f32[16,64,8,128]{3,2,1,0:T(8,128)}, u32[]{:S(2)}, u32[]{:S(2)}) async-start(f32[16,64,8,128]{3,2,1,0:T(8,128)} %gate.4), calls=%async_computation.2 | async-start | bytes 8388608 | tf_op jit(solution)/shard_map/all_to_all | solution.py:363
  221.8 13.6 %copy-start.13 = (f32[128,128]{1,0:T(8,128)}, f32[128,128]{1,0:T(8,128)S(1)}, u32[]{:S(2)}) copy-start(f32[128,128]{1,0:T(8,128)S(1)} %get-tuple-element.45.blur_y) | copy-start | bytes 196612
  221.8 113.8 %copy-start.11 = (f32[128,128]{1,0:T(8,128)}, f32[128,128]{1,0:T(8,128)S(1)}, u32[]{:S(2)}) copy-start(f32[128,128]{1,0:T(8,128)S(1)} %get-tuple-element.46.blur_y) | copy-start | bytes 196612
  221.8 232.1 %copy-start.9 = (f32[128,128]{1,0:T(8,128)}, f32[128,128]{1,0:T(8,128)S(1)}, u32[]{:S(2)}) copy-start(f32[128,128]{1,0:T(8,128)S(1)} %get-tuple-element.47.blur_y) | copy-start | bytes 196612
  221.8 310.0 %copy-start.8 = (f32[128,128]{1,0:T(8,128)}, f32[128,128]{1,0:T(8,128)S(1)}, u32[]{:S(2)}) copy-start(f32[128,128]{1,0:T(8,128)S(1)} %get-tuple-element.48.blur_y) | copy-start | bytes 196612
  229.4 6.0 copy-start.14
  229.4 106.9 %copy-start.12 = (f32[128,128]{1,0:T(8,128)}, f32[128,128]{1,0:T(8,128)S(1)}, u32[]{:S(2)}) copy-start(f32[128,128]{1,0:T(8,128)S(1)} %get-tuple-element.42.back_z) | copy-start | bytes 196612
  229.4 225.2 %copy-start.10 = (f32[128,128]{1,0:T(8,128)}, f32[128,128]{1,0:T(8,128)S(1)}, u32[]{:S(2)}) copy-start(f32[128,128]{1,0:T(8,128)S(1)} %get-tuple-element.43.back_z) | copy-start | bytes 196612
  229.4 303.1 %copy-start.5 = (f32[128,128]{1,0:T(8,128)}, f32[128,128]{1,0:T(8,128)S(1)}, u32[]{:S(2)}) copy-start(f32[128,128]{1,0:T(8,128)S(1)} %get-tuple-element.44.back_z) | copy-start | bytes 196612
  259.7 33.1 %collective-permute-start.2 = (f32[16,30,8,128]{3,2,1,0:T(8,128)}, f32[16,30,8,128]{3,2,1,0:T(8,128)S(1)}, u32[]{:S(2)}, u32[]{:S(2)}) collective-permute-start(f32[16,30,8,128]{3,2,1,0:T(8,128)} %get-tuple-element.23), channel_id=1, source_target_pairs={{0,1},{1,2},{2,3},{3,7},{7,6},{6,5},{5,4},{4,8},{8,9},{9,10},{10,1... | collective-permute-start | bytes 5898248 | tf_op jit(solution)/shard_map/ppermute | solution.py:400
  263.3 37.5 %collective-permute-start.3 = (f32[16,30,8,128]{3,2,1,0:T(8,128)}, f32[16,30,8,128]{3,2,1,0:T(8,128)}, u32[]{:S(2)}, u32[]{:S(2)}) collective-permute-start(f32[16,30,8,128]{3,2,1,0:T(8,128)} %get-tuple-element.25.refs_1_), channel_id=1, source_target_pairs={{1,0},{2,1},{3,2},{7,3},{6,7},{5,6},{4,5},{8,4},{9,8},{10,9},{11,1... | collective-permute-start | bytes 5898248 | tf_op jit(solution)/shard_map/ppermute | solution.py:401
  292.8 7.9 %copy-start.1 = (f32[16,30,8,128]{3,2,1,0:T(8,128)}, f32[16,30,8,128]{3,2,1,0:T(8,128)S(1)}, u32[]{:S(2)}) copy-start(f32[16,30,8,128]{3,2,1,0:T(8,128)S(1)} %collective-permute-done.2.above.refs_1_) | copy-start | bytes 5898244
  300.8 36.3 %copy-start.15 = (s32[96,128]{1,0:T(8,128)S(1)}, s32[96,128]{1,0:T(8,128)}, u32[]{:S(2)}) copy-start(s32[96,128]{1,0:T(8,128)} %constant.29.clone) | copy-start | bytes 147460
  300.8 113.1 %all-to-all-start.3 = ((f32[16,64,8,128]{3,2,1,0:T(8,128)}), f32[16,64,8,128]{3,2,1,0:T(8,128)}, u32[]{:S(2)}, u32[]{:S(2)}) async-start(f32[16,64,8,128]{3,2,1,0:T(8,128)} %gate.5), calls=%async_computation.3 | async-start | bytes 8388608 | tf_op jit(solution)/shard_map/all_to_all | solution.py:363
  368.5 36.7 %collective-permute-start.4 = (f32[16,30,8,128]{3,2,1,0:T(8,128)}, f32[16,30,8,128]{3,2,1,0:T(8,128)S(1)}, u32[]{:S(2)}, u32[]{:S(2)}) collective-permute-start(f32[16,30,8,128]{3,2,1,0:T(8,128)} %get-tuple-element.27), channel_id=1, source_target_pairs={{0,1},{1,2},{2,3},{3,7},{7,6},{6,5},{5,4},{4,8},{8,9},{9,10},{10,1... | collective-permute-start | bytes 5898248 | tf_op jit(solution)/shard_map/ppermute | solution.py:400
  372.0 33.1 %collective-permute-start.5 = (f32[16,30,8,128]{3,2,1,0:T(8,128)}, f32[16,30,8,128]{3,2,1,0:T(8,128)}, u32[]{:S(2)}, u32[]{:S(2)}) collective-permute-start(f32[16,30,8,128]{3,2,1,0:T(8,128)} %get-tuple-element.29.refs_1_), channel_id=1, source_target_pairs={{1,0},{2,1},{3,2},{7,3},{6,7},{5,6},{4,5},{8,4},{9,8},{10,9},{11,1... | collective-permute-start | bytes 5898248 | tf_op jit(solution)/shard_map/ppermute | solution.py:401
  405.2 1.3 copy-start.2
  413.9 106.8 %all-to-all-start.4 = ((f32[16,36,8,128]{3,2,1,0:T(8,128)}), f32[16,36,8,128]{3,2,1,0:T(8,128)S(1)}, u32[]{:S(2)}, u32[]{:S(2)}) async-start(f32[16,36,8,128]{3,2,1,0:T(8,128)} %gate.6), calls=%async_computation.4 | async-start | bytes 4718592 | tf_op jit(solution)/shard_map/all_to_all | solution.py:363
  485.7 28.6 %collective-permute-start.6 = (f32[16,30,8,128]{3,2,1,0:T(8,128)}, f32[16,30,8,128]{3,2,1,0:T(8,128)}, u32[]{:S(2)}, u32[]{:S(2)}) collective-permute-start(f32[16,30,8,128]{3,2,1,0:T(8,128)} %get-tuple-element.31), channel_id=1, source_target_pairs={{0,1},{1,2},{2,3},{3,7},{7,6},{6,5},{5,4},{4,8},{8,9},{9,10},{10,1... | collective-permute-start | bytes 5898248 | tf_op jit(solution)/shard_map/ppermute | solution.py:400
  489.3 31.4 %collective-permute-start.7 = (f32[16,30,8,128]{3,2,1,0:T(8,128)}, f32[16,30,8,128]{3,2,1,0:T(8,128)}, u32[]{:S(2)}, u32[]{:S(2)}) collective-permute-start(f32[16,30,8,128]{3,2,1,0:T(8,128)} %get-tuple-element.33.refs_1_), channel_id=1, source_target_pairs={{1,0},{2,1},{3,2},{7,3},{6,7},{5,6},{4,5},{8,4},{9,8},{10,9},{11,1... | collective-permute-start | bytes 5898248 | tf_op jit(solution)/shard_map/ppermute | solution.py:401
  520.6 12.6 %copy-start = (f32[16,36,8,128]{3,2,1,0:T(8,128)}, f32[16,36,8,128]{3,2,1,0:T(8,128)S(1)}, u32[]{:S(2)}) copy-start(f32[16,36,8,128]{3,2,1,0:T(8,128)S(1)} %all-to-all-done.4.data) | copy-start | bytes 7077892
  520.6 48.1 %all-to-all-start.5 = ((f32[16,28,8,128]{3,2,1,0:T(8,128)}), f32[16,28,8,128]{3,2,1,0:T(8,128)}, u32[]{:S(2)}, u32[]{:S(2)}) async-start(f32[16,28,8,128]{3,2,1,0:T(8,128)} %gate.7), calls=%async_computation.5 | async-start | bytes 3670016 | tf_op jit(solution)/shard_map/all_to_all | solution.py:363
  533.2 32.3 %copy-start.16 = (s32[64,96]{1,0:T(8,128)S(1)}, s32[64,96]{1,0:T(8,128)}, u32[]{:S(2)}) copy-start(s32[64,96]{1,0:T(8,128)} %constant.30.clone) | copy-start | bytes 73732
  560.1 17.3 %collective-permute-start.8 = (f32[16,15,8,128]{3,2,1,0:T(8,128)}, f32[16,15,8,128]{3,2,1,0:T(8,128)S(1)}, u32[]{:S(2)}, u32[]{:S(2)}) collective-permute-start(f32[16,15,8,128]{3,2,1,0:T(8,128)} %get-tuple-element.35), channel_id=1, source_target_pairs={{0,1},{1,2},{2,3},{3,7},{7,6},{6,5},{5,4},{4,8},{8,9},{9,10},{10,1... | collective-permute-start | bytes 2949128 | tf_op jit(solution)/shard_map/ppermute | solution.py:400
  563.6 15.6 %collective-permute-start.9 = (f32[16,15,8,128]{3,2,1,0:T(8,128)}, f32[16,15,8,128]{3,2,1,0:T(8,128)S(1)}, u32[]{:S(2)}, u32[]{:S(2)}) collective-permute-start(f32[16,15,8,128]{3,2,1,0:T(8,128)} %get-tuple-element.36), channel_id=1, source_target_pairs={{1,0},{2,1},{3,2},{7,3},{6,7},{5,6},{4,5},{8,4},{9,8},{10,9},{11,1... | collective-permute-start | bytes 2949128 | tf_op jit(solution)/shard_map/ppermute | solution.py:401
  577.4 1.8 copy-start.6
  579.2 0.9 copy-start.7

commit v8 on v7

--- a/solution.py
+++ b/solution.py
@@ -437,7 +437,7 @@
     def matrices(v):
         return blur_x[v], columns[v], depths[v].T, columns[v].T, depths[v]
 
-    outer = 9 * rows // 32
+    outer = rows // 4
     split = outer >= margin + 1 and outer % 2 == 0 and views > 1
     ends = tuple(r for r in every if r < outer or r >= rows - outer)
     inside = tuple(r for r in every if outer <= r < rows - outer)

time: 694 us -> 694 us (level)
  transfers between devices with their start and end apart: 16 -> 16, of which waited for: 13 -> 12; matrix products, arithmetic and copies ran while one was open for 6% -> 6% of each run, Pallas kernels for 20% -> 20%
where the time goes in v8:
time: 694 us; the launch traced here: 693 us
  waiting for transfers between devices  227 us (33%)
  starting transfers between devices  169 us (24%)
  Pallas kernels  151 us (22%)
  blocking collectives  103 us (15%)
  local copies, waits for them, and re-layouts  23.2 us (3%)
  other arithmetic  18.6 us (3%)
    all_to_all x6, starting transfers between devices, to_pencils(): lax.all_to_all(blocks, 'slab', split_axis=0, concat_axis=0, tiled=True)  142 us
    all_to_all x6, waiting for transfers between devices, to_pencils(): lax.all_to_all(blocks, 'slab', split_axis=0, concat_axis=0, tiled=True)  111 us
    all_to_all x1, blocking collectives, to_planes(): lax.all_to_all(pencils, 'slab', split_axis=0, concat_axis=0, tiled=True)  103 us
    ppermute x5, waiting for transfers between devices, halos(): above.insert(0, lax.ppermute(tail[:, rows - size:], 'slab', forth))  98.3 us
    pallas_call x2, Pallas kernels, body(): call(view_kernel, 'view', 33, (volume(extent), volume(rows), end, end), [...  60.7 us
    pallas_call x8, Pallas kernels, streamed(): pl.pallas_call(kernel, out_shape=outs, in_specs=[WHOLE] * len(fixed) + [A...  33.6 us
    pallas_call x1, Pallas kernels, body(): call(functools.partial(last_kernel, margin), 'last', 30, tuple(outs), [WH...  26.4 us
    pallas_call x1, Pallas kernels, body(): call(first_kernel, 'first', 26, (volume(extent), volume(rows), end, end),...  24.3 us
  transfers between devices with their start and end apart: 16, of which 12 were waited for; matrix products, arithmetic and copies ran while one was open for 6% of the time, Pallas kernels for 20%

profile of v8, /device:TPU:1, one launch (start us, length us, event | category | flops | bytes accessed | tf_op | source)
XLA Modules:
  0.0 693.0 jit_solution(5242329898988793619)
XLA Ops:
  0.0 3.8 turn.6
  3.8 7.3 %all-to-all-start = ((f32[16,64,8,128]{3,2,1,0:T(8,128)}), f32[16,64,8,128]{3,2,1,0:T(8,128)}, u32[]{:S(2)}, u32[]{:S(2)}) async-start(f32[16,64,8,128]{3,2,1,0:T(8,128)} %turn.6), calls=%async_computation | async-start | bytes 8388608 | tf_op jit(solution)/shard_map/all_to_all | solution.py:363
  11.2 12.2 %slice_bitcast_fusion = (f32[8,1024,128]{2,1,0:T(8,128)}, f32[8,1024,128]{2,1,0:T(8,128)}, f32[8,1024,128]{2,1,0:T(8,128)}, f32[8,1024,128]{2,1,0:T(8,128)}) fusion(f32[4,8,1024,128]{3,2,1,0:T(8,128)} %param.13), kind=kLoop, calls=%fused_computation.5 | loop fusion | bytes 33554432 | tf_op jit(solution)/shard_map/squeeze | solution.py:450
  23.4 3.8 turn.7
  27.2 62.0 %all-to-all-done.own = f32[16,64,8,128]{3,2,1,0:T(8,128)} async-done(((f32[16,64,8,128]{3,2,1,0:T(8,128)}), f32[16,64,8,128]{3,2,1,0:T(8,128)}, u32[]{:S(2)}, u32[]{:S(2)}) %all-to-all-start) | async-done | bytes 4194336 | tf_op jit(solution)/shard_map/all_to_all | solution.py:363
  89.2 19.3 %all-to-all-start.1 = ((f32[16,64,8,128]{3,2,1,0:T(8,128)}), f32[16,64,8,128]{3,2,1,0:T(8,128)}, u32[]{:S(2)}, u32[]{:S(2)}) async-start(f32[16,64,8,128]{3,2,1,0:T(8,128)} %turn.7), calls=%async_computation.1 | async-start | bytes 8388608 | tf_op jit(solution)/shard_map/all_to_all | solution.py:363
  108.5 1.6 fusion.2
  110.2 3.5 collective-permute-start
  113.7 1.9 collective-permute-start.1
  115.6 3.8 turn.8.refs_0_
  119.5 28.4 %collective-permute-done.above.refs_1_ = f32[16,15,8,128]{3,2,1,0:T(8,128)S(1)} collective-permute-done((f32[16,15,8,128]{3,2,1,0:T(8,128)S(1)}, f32[16,15,8,128]{3,2,1,0:T(8,128)S(1)}, u32[]{:S(2)}, u32[]{:S(2)}) %collective-permute-start) | collective-permute-done | bytes 983072 | tf_op jit(solution)/shard_map/ppermute | solution.py:400
  147.9 4.2 collective-permute-done.1.below.refs_2_
  152.1 0.9 copy-done.4
  153.0 33.7 %all-to-all-done.1.data = f32[16,64,8,128]{3,2,1,0:T(8,128)} async-done(((f32[16,64,8,128]{3,2,1,0:T(8,128)}), f32[16,64,8,128]{3,2,1,0:T(8,128)}, u32[]{:S(2)}, u32[]{:S(2)}) %all-to-all-start.1) | async-done | bytes 4194336 | tf_op jit(solution)/shard_map/all_to_all | solution.py:363
  186.7 30.5 %all-to-all-start.2 = ((f32[16,64,8,128]{3,2,1,0:T(8,128)}), f32[16,64,8,128]{3,2,1,0:T(8,128)}, u32[]{:S(2)}, u32[]{:S(2)}) async-start(f32[16,64,8,128]{3,2,1,0:T(8,128)} %gate.4), calls=%async_computation.2 | async-start | bytes 8388608 | tf_op jit(solution)/shard_map/all_to_all | solution.py:363
  217.8 2.5 divide_bitcast_fusion.7
  220.7 1.0 select_reduce_fusion.4
  221.7 0.7 copy.32
  223.2 2.6 divide_bitcast_fusion.6
  225.8 3.7 select_reduce_fusion
  229.5 0.7 copy.31
  230.9 1.3 broadcast_divide_fusion
  232.2 2.5 broadcast_divide_fusion.5
  234.7 1.1 select_reduce_fusion.11
  235.8 24.3 %first.1 = (f32[16,96,8,128]{3,2,1,0:T(8,128)}, f32[16,64,8,128]{3,2,1,0:T(8,128)}, f32[16,30,8,128]{3,2,1,0:T(8,128)}, f32[16,30,8,128]{3,2,1,0:T(8,128)}) custom-call(f32[64,96]{1,0:T(8,128)} %get-tuple-element.52.blur_x, f32[128,128]{1,0:T(8,128)} %copy-done.13, f32[128,128]{1,0:T(8,128)} %bitcast.56, f32[128,128]{1,0:T(8,128)} %bitcast.55, ...), custom_call_target="tpu_custom_call" | custom-call | bytes 93600000 | tf_op jit(solution)/shard_map/first/pallas_call | solution.py:452
  260.1 3.5 collective-permute-start.2
  263.7 1.9 collective-permute-start.3
  265.6 3.9 turn.9.refs_0_
  269.5 23.4 %collective-permute-done.2.above.refs_1_ = f32[16,30,8,128]{3,2,1,0:T(8,128)S(1)} collective-permute-done((f32[16,30,8,128]{3,2,1,0:T(8,128)}, f32[16,30,8,128]{3,2,1,0:T(8,128)S(1)}, u32[]{:S(2)}, u32[]{:S(2)}) %collective-permute-start.2) | collective-permute-done | bytes 1966112 | tf_op jit(solution)/shard_map/ppermute | solution.py:400
  292.8 8.3 %collective-permute-done.3.below.refs_2_ = f32[16,30,8,128]{3,2,1,0:T(8,128)} collective-permute-done((f32[16,30,8,128]{3,2,1,0:T(8,128)}, f32[16,30,8,128]{3,2,1,0:T(8,128)}, u32[]{:S(2)}, u32[]{:S(2)}) %collective-permute-start.3) | collective-permute-done | bytes 1966112 | tf_op jit(solution)/shard_map/ppermute | solution.py:401
  301.2 34.4 %all-to-all-start.3 = ((f32[16,64,8,128]{3,2,1,0:T(8,128)}), f32[16,64,8,128]{3,2,1,0:T(8,128)}, u32[]{:S(2)}, u32[]{:S(2)}) async-start(f32[16,64,8,128]{3,2,1,0:T(8,128)} %gate.5), calls=%async_computation.3 | async-start | bytes 8388608 | tf_op jit(solution)/shard_map/all_to_all | solution.py:363
  335.6 0.7 copy.30
  336.3 0.7 copy.29
  337.0 1.1 select_reduce_fusion.8
  338.1 30.3 %view.2 = (f32[16,96,8,128]{3,2,1,0:T(8,128)}, f32[16,64,8,128]{3,2,1,0:T(8,128)}, f32[16,30,8,128]{3,2,1,0:T(8,128)}, f32[16,30,8,128]{3,2,1,0:T(8,128)}) custom-call(f32[96,128]{1,0:T(8,128)} %get-tuple-element.49.spread_x, f32[64,96]{1,0:T(8,128)} %get-tuple-element.53.blur_x, f32[128,128]{1,0:T(8,128)} %copy-done.11, f32[128,128]{1,0:T(8,128)} %bitcast.51, ...), custom_call_target="tpu_custom_call" | custom-call | bytes 118800000 | tf_op jit(solution)/shard_map/view/pallas_call | solution.py:464
  368.4 3.5 collective-permute-start.4
  372.0 2.1 collective-permute-start.5
  374.1 3.5 turn.10.refs_0_
  377.6 27.5 %collective-permute-done.4.above.refs_1_ = f32[16,30,8,128]{3,2,1,0:T(8,128)S(1)} collective-permute-done((f32[16,30,8,128]{3,2,1,0:T(8,128)}, f32[16,30,8,128]{3,2,1,0:T(8,128)S(1)}, u32[]{:S(2)}, u32[]{:S(2)}) %collective-permute-start.4) | collective-permute-done | bytes 1966112 | tf_op jit(solution)/shard_map/ppermute | solution.py:400
  405.1 1.2 copy-done.2
  406.4 7.5 %all-to-all-done.3.data = f32[16,64,8,128]{3,2,1,0:T(8,128)} async-done(((f32[16,64,8,128]{3,2,1,0:T(8,128)}), f32[16,64,8,128]{3,2,1,0:T(8,128)}, u32[]{:S(2)}, u32[]{:S(2)}) %all-to-all-start.3) | async-done | bytes 4194336 | tf_op jit(solution)/shard_map/all_to_all | solution.py:363
  413.9 40.0 %all-to-all-start.4 = ((f32[16,32,8,128]{3,2,1,0:T(8,128)}), f32[16,32,8,128]{3,2,1,0:T(8,128)S(1)}, u32[]{:S(2)}, u32[]{:S(2)}) async-start(f32[16,32,8,128]{3,2,1,0:T(8,128)} %gate.6), calls=%async_computation.4 | async-start | bytes 4194304 | tf_op jit(solution)/shard_map/all_to_all | solution.py:363
  453.9 0.7 copy.28
  454.6 0.7 copy.27
  455.3 30.4 %view.3 = (f32[16,96,8,128]{3,2,1,0:T(8,128)}, f32[16,64,8,128]{3,2,1,0:T(8,128)}, f32[16,30,8,128]{3,2,1,0:T(8,128)}, f32[16,30,8,128]{3,2,1,0:T(8,128)}) custom-call(f32[96,128]{1,0:T(8,128)} %get-tuple-element.50.spread_x, f32[64,96]{1,0:T(8,128)} %get-tuple-element.54.blur_x, f32[128,128]{1,0:T(8,128)} %copy-done.9, f32[128,128]{1,0:T(8,128)} %bitcast.54, ...), custom_call_target="tpu_custom_call" | custom-call | bytes 118800000 | tf_op jit(solution)/shard_map/view/pallas_call | solution.py:464
  485.7 3.5 collective-permute-start.6
  489.2 2.1 collective-permute-start.7
  491.3 3.5 turn.11.refs_0_
  494.9 19.0 %collective-permute-done.6.above.refs_1_ = f32[16,30,8,128]{3,2,1,0:T(8,128)} collective-permute-done((f32[16,30,8,128]{3,2,1,0:T(8,128)}, f32[16,30,8,128]{3,2,1,0:T(8,128)}, u32[]{:S(2)}, u32[]{:S(2)}) %collective-permute-start.6) | collective-permute-done | bytes 1966112 | tf_op jit(solution)/shard_map/ppermute | solution.py:400
  513.9 2.1 collective-permute-done.7.below.refs_2_
  516.0 10.1 %all-to-all-start.5 = ((f32[16,32,8,128]{3,2,1,0:T(8,128)}), f32[16,32,8,128]{3,2,1,0:T(8,128)}, u32[]{:S(2)}, u32[]{:S(2)}) async-start(f32[16,32,8,128]{3,2,1,0:T(8,128)} %gate.7), calls=%async_computation.5 | async-start | bytes 4194304 | tf_op jit(solution)/shard_map/all_to_all | solution.py:363
  526.1 0.7 copy.26
  526.8 0.7 copy.25
  527.6 26.4 %last.1 = (f32[16,64,8,128]{3,2,1,0:T(8,128)}, f32[16,32,8,128]{3,2,1,0:T(8,128)}, f32[16,16,8,128]{3,2,1,0:T(8,128)}, f32[16,16,8,128]{3,2,1,0:T(8,128)}, f32[1...) custom-call(f32[96,128]{1,0:T(8,128)} %get-tuple-element.51.spread_x, f32[64,96]{1,0:T(8,128)} %get-tuple-element.55.blur_x, ...), custom_call_target="tpu_custom_call" | custom-call | bytes 108000000 | tf_op jit(solution)/shard_map/last/pallas_call | solution.py:459
  554.0 3.5 collective-permute-start.8
  557.5 1.9 collective-permute-start.9
  559.5 0.8 select_reduce_fusion.15.refs_0_
  560.3 7.5 %all-to-all-done.5.data = f32[16,32,8,128]{3,2,1,0:T(8,128)} async-done(((f32[16,32,8,128]{3,2,1,0:T(8,128)}), f32[16,32,8,128]{3,2,1,0:T(8,128)}, u32[]{:S(2)}, u32[]{:S(2)}) %all-to-all-start.5) | async-done | bytes 2097184 | tf_op jit(solution)/shard_map/all_to_all | solution.py:363
  567.8 6.2 middle.1.refs_5_
  574.0 3.7 collective-permute-done.9.refs_2_
  577.6 1.0 copy-done.7
  578.6 7.4 %finish.1 = f32[16,64,8,128]{3,2,1,0:T(8,128)} custom-call(f32[64,96]{1,0:T(8,128)} %select_reduce_fusion.15.refs_0_, f32[16,15,8,128]{3,2,1,0:T(8,128)} %copy-done.6, f32[16,15,8,128]{3,2,1,0:T(8,128)} %copy-done.7, f32[16,64,8,128]{3,2,1,0:T(8,128)} %get-tuple-element.37.refs_3_, f32[16,16,8,128]{3,2,1,0:T(8,128)} %get-tuple-element.38.refs_4_, ...), custom_call_target="tpu_custom_call" | custom-call | bytes 25200000 | tf_op jit(solution)/shard_map/finish/pallas_call | solution.py:280
  586.1 103.0 %all_to_all.35.refs_0_ = f32[16,64,8,128]{3,2,1,0:T(8,128)} all-to-all(f32[16,64,8,128]{3,2,1,0:T(8,128)} %finish.1), channel_id=1, replica_groups=mesh['groups'=2,'slab'=16] {'slab'}, dimensions={0} | all-to-all | bytes 8388608 | tf_op jit(solution)/shard_map/all_to_all | solution.py:374
  689.1 3.8 turn_back.1
  (54 shorter events, 2.5 us)
Async XLA Ops:
  3.8 85.4 %all-to-all-start = ((f32[16,64,8,128]{3,2,1,0:T(8,128)}), f32[16,64,8,128]{3,2,1,0:T(8,128)}, u32[]{:S(2)}, u32[]{:S(2)}) async-start(f32[16,64,8,128]{3,2,1,0:T(8,128)} %turn.6), calls=%async_computation | async-start | bytes 8388608 | tf_op jit(solution)/shard_map/all_to_all | solution.py:363
  89.2 97.4 %all-to-all-start.1 = ((f32[16,64,8,128]{3,2,1,0:T(8,128)}), f32[16,64,8,128]{3,2,1,0:T(8,128)}, u32[]{:S(2)}, u32[]{:S(2)}) async-start(f32[16,64,8,128]{3,2,1,0:T(8,128)} %turn.7), calls=%async_computation.1 | async-start | bytes 8388608 | tf_op jit(solution)/shard_map/all_to_all | solution.py:363
  110.2 37.7 %collective-permute-start = (f32[16,15,8,128]{3,2,1,0:T(8,128)S(1)}, f32[16,15,8,128]{3,2,1,0:T(8,128)S(1)}, u32[]{:S(2)}, u32[]{:S(2)}) collective-permute-start(f32[16,15,8,128]{3,2,1,0:T(8,128)S(1)} %get-tuple-element.73), channel_id=1, source_target_pairs={{0,1},{1,2},{2,3},{3,7},{7,6},{6,5},{5,4},{4,8},{8,9},{9,10},{10,1... | collective-permute-start | bytes 2949128 | tf_op jit(solution)/shard_map/ppermute | solution.py:400
  113.7 38.3 %collective-permute-start.1 = (f32[16,15,8,128]{3,2,1,0:T(8,128)S(1)}, f32[16,15,8,128]{3,2,1,0:T(8,128)S(1)}, u32[]{:S(2)}, u32[]{:S(2)}) collective-permute-start(f32[16,15,8,128]{3,2,1,0:T(8,128)S(1)} %get-tuple-element.72), channel_id=1, source_target_pairs={{1,0},{2,1},{3,2},{7,3},{6,7},{5,6},{4,5},{8,4},{9,8},{10,9},{11,1... | collective-permute-start | bytes 2949128 | tf_op jit(solution)/shard_map/ppermute | solution.py:401
  147.9 4.2 copy-start.3
  152.1 0.9 copy-start.4
  153.0 64.1 %copy-start.18 = (f32[4,2,31]{2,1,0:T(2,128)S(1)}, f32[4,2,31]{2,1,0:T(2,128)}, u32[]{:S(2)}) copy-start(f32[4,2,31]{2,1,0:T(2,128)} %param.14) | copy-start | bytes 2980
  153.0 69.5 %copy-start.19 = (f32[4,101]{1,0:T(4,128)S(1)}, f32[4,101]{1,0:T(4,128)}, u32[]{:S(2)}) copy-start(f32[4,101]{1,0:T(4,128)} %param.15) | copy-start | bytes 4852
  153.0 81.7 %copy-start.17 = (s32[64,96]{1,0:T(8,128)S(1)}, s32[64,96]{1,0:T(8,128)}, u32[]{:S(2)}) copy-start(s32[64,96]{1,0:T(8,128)} %constant.28.clone) | copy-start | bytes 73732
  186.7 114.5 %all-to-all-start.2 = ((f32[16,64,8,128]{3,2,1,0:T(8,128)}), f32[16,64,8,128]{3,2,1,0:T(8,128)}, u32[]{:S(2)}, u32[]{:S(2)}) async-start(f32[16,64,8,128]{3,2,1,0:T(8,128)} %gate.4), calls=%async_computation.2 | async-start | bytes 8388608 | tf_op jit(solution)/shard_map/all_to_all | solution.py:363
  221.7 14.1 %copy-start.13 = (f32[128,128]{1,0:T(8,128)}, f32[128,128]{1,0:T(8,128)S(1)}, u32[]{:S(2)}) copy-start(f32[128,128]{1,0:T(8,128)S(1)} %get-tuple-element.45.blur_y) | copy-start | bytes 196612
  221.7 113.9 %copy-start.11 = (f32[128,128]{1,0:T(8,128)}, f32[128,128]{1,0:T(8,128)S(1)}, u32[]{:S(2)}) copy-start(f32[128,128]{1,0:T(8,128)S(1)} %get-tuple-element.46.blur_y) | copy-start | bytes 196612
  221.7 232.2 %copy-start.9 = (f32[128,128]{1,0:T(8,128)}, f32[128,128]{1,0:T(8,128)S(1)}, u32[]{:S(2)}) copy-start(f32[128,128]{1,0:T(8,128)S(1)} %get-tuple-element.47.blur_y) | copy-start | bytes 196612
  221.7 304.4 %copy-start.8 = (f32[128,128]{1,0:T(8,128)}, f32[128,128]{1,0:T(8,128)S(1)}, u32[]{:S(2)}) copy-start(f32[128,128]{1,0:T(8,128)S(1)} %get-tuple-element.48.blur_y) | copy-start | bytes 196612
  229.4 6.4 copy-start.14
  229.5 106.9 %copy-start.12 = (f32[128,128]{1,0:T(8,128)}, f32[128,128]{1,0:T(8,128)S(1)}, u32[]{:S(2)}) copy-start(f32[128,128]{1,0:T(8,128)S(1)} %get-tuple-element.42.back_z) | copy-start | bytes 196612
  229.5 225.1 %copy-start.10 = (f32[128,128]{1,0:T(8,128)}, f32[128,128]{1,0:T(8,128)S(1)}, u32[]{:S(2)}) copy-start(f32[128,128]{1,0:T(8,128)S(1)} %get-tuple-element.43.back_z) | copy-start | bytes 196612
  229.5 297.4 %copy-start.5 = (f32[128,128]{1,0:T(8,128)}, f32[128,128]{1,0:T(8,128)S(1)}, u32[]{:S(2)}) copy-start(f32[128,128]{1,0:T(8,128)S(1)} %get-tuple-element.44.back_z) | copy-start | bytes 196612
  260.1 32.7 %collective-permute-start.2 = (f32[16,30,8,128]{3,2,1,0:T(8,128)}, f32[16,30,8,128]{3,2,1,0:T(8,128)S(1)}, u32[]{:S(2)}, u32[]{:S(2)}) collective-permute-start(f32[16,30,8,128]{3,2,1,0:T(8,128)} %get-tuple-element.23), channel_id=1, source_target_pairs={{0,1},{1,2},{2,3},{3,7},{7,6},{6,5},{5,4},{4,8},{8,9},{9,10},{10,1... | collective-permute-start | bytes 5898248 | tf_op jit(solution)/shard_map/ppermute | solution.py:400
  263.7 37.5 %collective-permute-start.3 = (f32[16,30,8,128]{3,2,1,0:T(8,128)}, f32[16,30,8,128]{3,2,1,0:T(8,128)}, u32[]{:S(2)}, u32[]{:S(2)}) collective-permute-start(f32[16,30,8,128]{3,2,1,0:T(8,128)} %get-tuple-element.25.refs_1_), channel_id=1, source_target_pairs={{1,0},{2,1},{3,2},{7,3},{6,7},{5,6},{4,5},{8,4},{9,8},{10,9},{11,1... | collective-permute-start | bytes 5898248 | tf_op jit(solution)/shard_map/ppermute | solution.py:401
  292.8 8.4 %copy-start.1 = (f32[16,30,8,128]{3,2,1,0:T(8,128)}, f32[16,30,8,128]{3,2,1,0:T(8,128)S(1)}, u32[]{:S(2)}) copy-start(f32[16,30,8,128]{3,2,1,0:T(8,128)S(1)} %collective-permute-done.2.above.refs_1_) | copy-start | bytes 5898244
  301.2 35.9 %copy-start.15 = (s32[96,128]{1,0:T(8,128)S(1)}, s32[96,128]{1,0:T(8,128)}, u32[]{:S(2)}) copy-start(s32[96,128]{1,0:T(8,128)} %constant.29.clone) | copy-start | bytes 147460
  301.2 112.7 %all-to-all-start.3 = ((f32[16,64,8,128]{3,2,1,0:T(8,128)}), f32[16,64,8,128]{3,2,1,0:T(8,128)}, u32[]{:S(2)}, u32[]{:S(2)}) async-start(f32[16,64,8,128]{3,2,1,0:T(8,128)} %gate.5), calls=%async_computation.3 | async-start | bytes 8388608 | tf_op jit(solution)/shard_map/all_to_all | solution.py:363
  368.4 36.7 %collective-permute-start.4 = (f32[16,30,8,128]{3,2,1,0:T(8,128)}, f32[16,30,8,128]{3,2,1,0:T(8,128)S(1)}, u32[]{:S(2)}, u32[]{:S(2)}) collective-permute-start(f32[16,30,8,128]{3,2,1,0:T(8,128)} %get-tuple-element.27), channel_id=1, source_target_pairs={{0,1},{1,2},{2,3},{3,7},{7,6},{6,5},{5,4},{4,8},{8,9},{9,10},{10,1... | collective-permute-start | bytes 5898248 | tf_op jit(solution)/shard_map/ppermute | solution.py:400
  372.0 33.2 %collective-permute-start.5 = (f32[16,30,8,128]{3,2,1,0:T(8,128)}, f32[16,30,8,128]{3,2,1,0:T(8,128)}, u32[]{:S(2)}, u32[]{:S(2)}) collective-permute-start(f32[16,30,8,128]{3,2,1,0:T(8,128)} %get-tuple-element.29.refs_1_), channel_id=1, source_target_pairs={{1,0},{2,1},{3,2},{7,3},{6,7},{5,6},{4,5},{8,4},{9,8},{10,9},{11,1... | collective-permute-start | bytes 5898248 | tf_op jit(solution)/shard_map/ppermute | solution.py:401
  405.1 1.3 copy-start.2
  413.9 102.2 %all-to-all-start.4 = ((f32[16,32,8,128]{3,2,1,0:T(8,128)}), f32[16,32,8,128]{3,2,1,0:T(8,128)S(1)}, u32[]{:S(2)}, u32[]{:S(2)}) async-start(f32[16,32,8,128]{3,2,1,0:T(8,128)} %gate.6), calls=%async_computation.4 | async-start | bytes 4194304 | tf_op jit(solution)/shard_map/all_to_all | solution.py:363
  485.7 28.2 %collective-permute-start.6 = (f32[16,30,8,128]{3,2,1,0:T(8,128)}, f32[16,30,8,128]{3,2,1,0:T(8,128)}, u32[]{:S(2)}, u32[]{:S(2)}) collective-permute-start(f32[16,30,8,128]{3,2,1,0:T(8,128)} %get-tuple-element.31), channel_id=1, source_target_pairs={{0,1},{1,2},{2,3},{3,7},{7,6},{6,5},{5,4},{4,8},{8,9},{9,10},{10,1... | collective-permute-start | bytes 5898248 | tf_op jit(solution)/shard_map/ppermute | solution.py:400
  489.2 26.8 %collective-permute-start.7 = (f32[16,30,8,128]{3,2,1,0:T(8,128)}, f32[16,30,8,128]{3,2,1,0:T(8,128)}, u32[]{:S(2)}, u32[]{:S(2)}) collective-permute-start(f32[16,30,8,128]{3,2,1,0:T(8,128)} %get-tuple-element.33.refs_1_), channel_id=1, source_target_pairs={{1,0},{2,1},{3,2},{7,3},{6,7},{5,6},{4,5},{8,4},{9,8},{10,9},{11,1... | collective-permute-start | bytes 5898248 | tf_op jit(solution)/shard_map/ppermute | solution.py:401
  516.0 11.5 %copy-start = (f32[16,32,8,128]{3,2,1,0:T(8,128)}, f32[16,32,8,128]{3,2,1,0:T(8,128)S(1)}, u32[]{:S(2)}) copy-start(f32[16,32,8,128]{3,2,1,0:T(8,128)S(1)} %all-to-all-done.4.data) | copy-start | bytes 6291460
  516.0 51.7 %all-to-all-start.5 = ((f32[16,32,8,128]{3,2,1,0:T(8,128)}), f32[16,32,8,128]{3,2,1,0:T(8,128)}, u32[]{:S(2)}, u32[]{:S(2)}) async-start(f32[16,32,8,128]{3,2,1,0:T(8,128)} %gate.7), calls=%async_computation.5 | async-start | bytes 4194304 | tf_op jit(solution)/shard_map/all_to_all | solution.py:363
  527.6 31.9 %copy-start.16 = (s32[64,96]{1,0:T(8,128)S(1)}, s32[64,96]{1,0:T(8,128)}, u32[]{:S(2)}) copy-start(s32[64,96]{1,0:T(8,128)} %constant.30.clone) | copy-start | bytes 73732
  554.0 20.0 %collective-permute-start.8 = (f32[16,15,8,128]{3,2,1,0:T(8,128)}, f32[16,15,8,128]{3,2,1,0:T(8,128)S(1)}, u32[]{:S(2)}, u32[]{:S(2)}) collective-permute-start(f32[16,15,8,128]{3,2,1,0:T(8,128)} %get-tuple-element.35), channel_id=1, source_target_pairs={{0,1},{1,2},{2,3},{3,7},{7,6},{6,5},{5,4},{4,8},{8,9},{9,10},{10,1... | collective-permute-start | bytes 2949128 | tf_op jit(solution)/shard_map/ppermute | solution.py:400
  557.5 20.1 %collective-permute-start.9 = (f32[16,15,8,128]{3,2,1,0:T(8,128)}, f32[16,15,8,128]{3,2,1,0:T(8,128)S(1)}, u32[]{:S(2)}, u32[]{:S(2)}) collective-permute-start(f32[16,15,8,128]{3,2,1,0:T(8,128)} %get-tuple-element.36), channel_id=1, source_target_pairs={{1,0},{2,1},{3,2},{7,3},{6,7},{5,6},{4,5},{8,4},{9,8},{10,9},{11,1... | collective-permute-start | bytes 2949128 | tf_op jit(solution)/shard_map/ppermute | solution.py:401
  574.0 3.7 copy-start.6
  577.6 1.0 copy-start.7
